TPU v7x, 128 devices: a whole 4x4x4 slice. The times are simulated.
128 devices in a mesh: sx: 16 (over z, x), sy: 8 (over y, core).
Axes of the slice: x: 4, y: 4, z: 4, core: 2. Of those that a mesh axis runs over, the one named last changes fastest.
Arguments:
- modes: bfloat16 [160, 80, 64, 3, 128], P('sx', 'sy'), may hold values from -0.44921875 to 0.44921875
- centre: float32 [128, 64, 128], P('sx', 'sy'), may hold values from -6 to 6
- coupling: float32 [128, 64, 128], P('sx', 'sy'), may hold values from 0.5 to 2
- volume: float32 [128, 64, 128], P('sx', 'sy'), may hold values from 0.25 to 1
Outputs:
- coarse_rows: float32 [8, 16, 64, 576], P('sy')
All inputs are finite; a program needn't handle non-finite values.
Results may differ from a plain program's by a relative error of at most 0.0003.
Values may be sent and summed in bfloat16 or wider, within the bound.
No kernel may reach another device: no remote copies, remote signals or barrier semaphores. Data moves between devices by JAX's collectives and lax.ppermute only.
A program may use at most 192 MiB of HBM per device.

v0:
```python
import jax
import jax.numpy as jnp
from jax import lax
from jax.sharding import PartitionSpec as P


def with_halo(block, sides, width):
    for axis, dim in sides:
        count = lax.axis_size(axis)
        forward = [(i, i + 1) for i in range(count - 1)]
        backward = [(target, source) for source, target in forward]
        low = lax.ppermute(
            lax.slice_in_dim(block, block.shape[dim] - width, None, axis=dim), axis, forward
        )
        high = lax.ppermute(lax.slice_in_dim(block, 0, width, axis=dim), axis, backward)
        block = jnp.concatenate([low, block, high], axis=dim)
    return block


def cover_weights(start_x, start_y, length, cell, count_x, count_y, margin):

    def counts(start, count):
        places = start + jnp.arange(length, dtype=jnp.int32)
        base = jnp.floor_divide(places, cell)
        total = jnp.zeros((length,), jnp.int32)
        for step_off in (-1, 0, 1):
            owner = base + step_off
            inside = (
                (owner >= 0)
                & (owner < count)
                & (places >= owner * cell - margin)
                & (places < owner * cell + cell + margin)
            )
            total = total + inside.astype(jnp.int32)
        in_grid = (places >= 0) & (places < cell * count)
        return jnp.where(in_grid, total, 0)

    both = counts(start_x, count_x)[:, None] * counts(start_y, count_y)[None, :]
    safe = jnp.maximum(both, 1).astype(jnp.float32)
    return jnp.where(both > 0, 1.0 / safe, 0.0)


def depth_shift(values, offset):
    if offset == 0:
        return values
    zero_slab = jnp.zeros(values.shape[:-1] + (1,), values.dtype)
    if offset > 0:
        return jnp.concatenate([values[..., 1:], zero_slab], axis=-1)
    return jnp.concatenate([zero_slab, values[..., :-1]], axis=-1)


def frame_image(basis_block, coef_frame):
    centre = coef_frame[:, :, 0][:, :, None, None, :]
    coupling = coef_frame[:, :, 1][:, :, None, None, :]
    volume = coef_frame[:, :, 2][:, :, None, None, :]
    values = basis_block.astype(jnp.float32)
    weighted = coupling[1:-1, 1:-1] * values
    padded = jnp.pad(weighted, ((2, 2), (2, 2), (0, 0), (0, 0), (0, 0)))
    framed = jnp.pad(values, ((1, 1), (1, 1), (0, 0), (0, 0), (0, 0)))
    size_x = framed.shape[0]
    size_y = framed.shape[1]
    spread = jnp.zeros(framed.shape, jnp.float32)
    for off_x in (-1, 0, 1):
        for off_y in (-1, 0, 1):
            slab = padded[1 + off_x : 1 + off_x + size_x, 1 + off_y : 1 + off_y + size_y]
            for off_z in (-1, 0, 1):
                if off_x == 0 and off_y == 0 and (off_z == 0):
                    continue
                factor = 0.5 ** (abs(off_x) + abs(off_y) + abs(off_z) + 1)
                spread = spread + factor * depth_shift(slab, off_z)
    total = jnp.sum(framed, axis=3, keepdims=True)
    return centre * framed - coupling * spread + volume * (total - framed)


def pair_block(image, piece):
    return jnp.einsum(
        "xykbz,xylbz->kl", image, piece.astype(jnp.float32), precision=lax.Precision.HIGHEST
    )


def gram_rows(basis, coef_frame, pieces):
    count_k = basis.shape[2]
    block = 16

    def rows_for(start):
        image = frame_image(lax.dynamic_slice_in_dim(basis, start, block, 2), coef_frame)
        parts = [
            pair_block(
                image[place_x : place_x + piece.shape[0], place_y : place_y + piece.shape[1]], piece
            )
            for place_x, place_y, piece in pieces
        ]
        return jnp.concatenate(parts, axis=1)

    stacked = lax.map(rows_for, jnp.arange(count_k // block, dtype=jnp.int32) * block)
    return stacked.reshape(count_k, stacked.shape[2])


def local(modes, centre, coupling, volume):
    ext = modes.shape[0]
    cell = centre.shape[0]
    margin = (ext - cell) // 2
    band = 2 * margin + 1
    frame = ext + 2
    index_x = lax.axis_index("sx")
    index_y = lax.axis_index("sy")
    coef = jnp.stack([centre, coupling, volume], axis=2)
    coef_frame = with_halo(coef, (("sx", 0), ("sy", 1)), margin + 1)
    weights = cover_weights(
        index_x * cell - margin - 1,
        index_y * cell - margin - 1,
        frame,
        cell,
        lax.axis_size("sx"),
        lax.axis_size("sy"),
        margin,
    )

    def weighted(piece, place_x, place_y):
        share = weights[place_x : place_x + piece.shape[0], place_y : place_y + piece.shape[1]]
        return (share[:, :, None, None, None] * piece.astype(jnp.float32)).astype(jnp.bfloat16)

    basis = weighted(modes, 1, 1)
    rimmed = with_halo(modes, (("sx", 0), ("sy", 1)), band)
    spans = ((0, 0, band), (1, band, ext), (cell + 1, band + ext, band))
    pieces = []
    for near_x in (0, 1, 2):
        for near_y in (0, 1, 2):
            place_x, from_x, long_x = spans[near_x]
            place_y, from_y, long_y = spans[near_y]
            piece = rimmed[from_x : from_x + long_x, from_y : from_y + long_y]
            pieces.append((place_x, place_y, weighted(piece, place_x, place_y)))
    rows = gram_rows(basis, coef_frame, pieces)
    return lax.all_gather(rows[None, None], "sx", axis=1, tiled=True)


def solution(mesh):
    in_specs = (
        P("sx", "sy", None, None, None),
        P("sx", "sy", None),
        P("sx", "sy", None),
        P("sx", "sy", None),
    )
    out_specs = P("sy", None, None, None)
    return jax.shard_map(local, mesh=mesh, in_specs=in_specs, out_specs=out_specs, check_vma=False)
```

profile of v0, /device:TPU:24, one launch (start us, length us, event | category | flops | bytes accessed | tf_op | source)
XLA Modules:
  0.0 449.5 jit_solution(683854360307442168)
XLA Ops:
  6.5 2.5 fusion.40
  10.3 3.5 collective-permute-start.4
  16.4 4.5 %collective-permute-start = (f32[2,8,3,128]{3,1,0,2:T(8,128)S(1)}, f32[2,8,3,128]{3,1,0,2:T(8,128)S(1)}, u32[]{:S(2)}, u32[]{:S(2)}) collective-permute-start(f32[2,8,3,128]{3,1,0,2:T(8,128)S(1)} %get-tuple-element.257), channel_id=1, source_target_pairs={{0,8},{8,16},{16,24},{24,32},{32,40},{40,48},{48,56},{56,64},{64,7... | collective-permute-start | bytes 73736 | tf_op jit(solution)/shard_map/ppermute | solution.py:12
  22.3 23.5 %collective-permute-done.4 = bf16[3,10,64,3,128]{4,2,1,0,3:T(8,128)(2,1)S(1)} collective-permute-done((bf16[3,10,64,3,128]{4,2,1,0,3:T(8,128)(2,1)}, bf16[3,10,64,3,128]{4,2,1,0,3:T(8,128)(2,1)S(1)}, u32[]{:S(2)}, u32[]{:S(2)}) %collective-permute-start.4) | collective-permute-done | bytes 1474592 | tf_op jit(solution)/shard_map/ppermute | solution.py:12
  46.0 4.4 constant_dynamic-update-slice_fusion.1
  51.5 3.7 fusion.39
  55.2 1.9 collective-permute-start.6
  57.3 3.6 collective-permute-start.7
  61.1 4.1 multiply_convert_fusion
  65.3 2.1 collective-permute-start.2
  67.4 3.5 collective-permute-start.3
  70.9 15.0 %collective-permute-done.2 = f32[12,2,3,128]{3,1,0,2:T(2,128)S(1)} collective-permute-done((f32[12,2,3,128]{3,1,0,2:T(2,128)S(1)}, f32[12,2,3,128]{3,1,0,2:T(2,128)S(1)}, u32[]{:S(2)}, u32[]{:S(2)}) %collective-permute-start.2) | collective-permute-done | bytes 36896 | tf_op jit(solution)/shard_map/ppermute | solution.py:12
  85.9 2.0 collective-permute-done.3
  88.7 1.7 multiply_convert_fusion.1
  90.4 1.6 multiply_convert_fusion.4
  92.0 2.4 multiply_convert_fusion.6
  94.4 3.0 multiply_convert_fusion.3
  97.4 3.0 multiply_convert_fusion.2
  100.5 2.4 multiply_convert_fusion.5
  102.8 284.1 %while.13 = (s32[]{:T(128)}, f32[4,16,576]{2,1,0:T(8,128)S(1)}, f32[12,12,3,128]{3,1,0,2:T(8,128)}, s32[4]{0:T(128)S(1)}, bf16[10,10,64,3,128]{4,2,1,0,3:T(8,128...) while((s32[]{:T(128)}, f32[4,16,576]{2,1,0:T(8,128)S(1)}, ...), condition=%wide.region_2.3_spmd, body=%wide.region_0.2_spmd.sunk | while | flops 1260822528 | bytes 227858864 | solution.py:95
  106.4 2.1 broadcast_multiply_fusion.2
  108.5 22.7 %pad_slice_fusion.27 = (f32[12,12,16,3,127]{4,2,1,0,3:T(8,128)}, f32[12,12,16,3,127]{4,2,1,0,3:T(8,128)}, f32[12,12,16,3,127]{4,2,1,0,3:T(8,128)}, f32[12,12,16,...) fusion(f32[10,10,16,3,128]{4,2,1,0,3:T(8,128)S(1)} %broadcast_m, ...), kind=kLoop, calls=%fused_computation.25.clone.1 | loop fusion | bytes 65660928 | tf_op jit(solution)/shard_map/while/body/eval_jaxpr/slice | solution.py:49
  131.2 2.0 dynamic-slice_convert_fusion.2
  135.1 23.3 %fusion.99 = f32[12,12,16,3,128]{4,2,1,0,3:T(8,128)S(1)} fusion(f32[10,10,16,3,128]{4,2,1,0,3:T(8,128)} %copy-done, f32[10,10,16,3,128]{4,2,1,0,3:T(8,128)S(1)} %broadcast_multiply_fusion.2, f32[12,12,16,3,127]{4,2,1,0,3:T(8,128)} %get-tuple-element.371, f32[12,12,16,3,127]{4,2,1,0,3:T(8,128)} %get-tuple-element.372, ...), kind=kLoop, calls=%fused_computation.30.clone.1 | loop fusion | flops 50429952 | bytes 73058304 | tf_op jit(solution)/shard_map/while/body/eval_jaxpr/add | solution.py:72
  158.4 1.6 convolution_bitcast_fusion.18
  160.0 2.6 convolution_bitcast_fusion.19
  164.5 5.9 %convolution_bitcast_fusion.22 = f32[16,64]{1,0:T(8,128)S(1)} fusion(f32[12,12,16,3,128]{4,2,1,0,3:T(8,128)S(1)} %fusion.99, bf16[10,10,64,3,128]{4,2,1,0,3:T(8,128)(2,1)} %get-tuple-element.428), kind=kOutput, calls=%fused_computation.73.clone.1 | convolution fusion | flops 471859200 | bytes 8458240 | tf_op jit(solution)/shard_map/while/body/eval_jaxpr/xykbz,xylbz->kl/dot_general | solution.py:76
  177.5 2.1 broadcast_multiply_fusion.2
  179.6 22.7 %pad_slice_fusion.27 = (f32[12,12,16,3,127]{4,2,1,0,3:T(8,128)}, f32[12,12,16,3,127]{4,2,1,0,3:T(8,128)}, f32[12,12,16,3,127]{4,2,1,0,3:T(8,128)}, f32[12,12,16,...) fusion(f32[10,10,16,3,128]{4,2,1,0,3:T(8,128)S(1)} %broadcast_m, ...), kind=kLoop, calls=%fused_computation.25.clone.1 | loop fusion | bytes 65660928 | tf_op jit(solution)/shard_map/while/body/eval_jaxpr/slice | solution.py:49
  202.4 2.0 dynamic-slice_convert_fusion.2
  206.2 23.3 %fusion.99 = f32[12,12,16,3,128]{4,2,1,0,3:T(8,128)S(1)} fusion(f32[10,10,16,3,128]{4,2,1,0,3:T(8,128)} %copy-done, f32[10,10,16,3,128]{4,2,1,0,3:T(8,128)S(1)} %broadcast_multiply_fusion.2, f32[12,12,16,3,127]{4,2,1,0,3:T(8,128)} %get-tuple-element.371, f32[12,12,16,3,127]{4,2,1,0,3:T(8,128)} %get-tuple-element.372, ...), kind=kLoop, calls=%fused_computation.30.clone.1 | loop fusion | flops 50429952 | bytes 73058304 | tf_op jit(solution)/shard_map/while/body/eval_jaxpr/add | solution.py:72
  229.6 1.6 convolution_bitcast_fusion.18
  231.2 2.6 convolution_bitcast_fusion.19
  235.6 5.9 %convolution_bitcast_fusion.22 = f32[16,64]{1,0:T(8,128)S(1)} fusion(f32[12,12,16,3,128]{4,2,1,0,3:T(8,128)S(1)} %fusion.99, bf16[10,10,64,3,128]{4,2,1,0,3:T(8,128)(2,1)} %get-tuple-element.428), kind=kOutput, calls=%fused_computation.73.clone.1 | convolution fusion | flops 471859200 | bytes 8458240 | tf_op jit(solution)/shard_map/while/body/eval_jaxpr/xykbz,xylbz->kl/dot_general | solution.py:76
  248.7 2.1 broadcast_multiply_fusion.2
  250.8 22.7 %pad_slice_fusion.27 = (f32[12,12,16,3,127]{4,2,1,0,3:T(8,128)}, f32[12,12,16,3,127]{4,2,1,0,3:T(8,128)}, f32[12,12,16,3,127]{4,2,1,0,3:T(8,128)}, f32[12,12,16,...) fusion(f32[10,10,16,3,128]{4,2,1,0,3:T(8,128)S(1)} %broadcast_m, ...), kind=kLoop, calls=%fused_computation.25.clone.1 | loop fusion | bytes 65660928 | tf_op jit(solution)/shard_map/while/body/eval_jaxpr/slice | solution.py:49
  273.5 2.0 dynamic-slice_convert_fusion.2
  277.4 23.3 %fusion.99 = f32[12,12,16,3,128]{4,2,1,0,3:T(8,128)S(1)} fusion(f32[10,10,16,3,128]{4,2,1,0,3:T(8,128)} %copy-done, f32[10,10,16,3,128]{4,2,1,0,3:T(8,128)S(1)} %broadcast_multiply_fusion.2, f32[12,12,16,3,127]{4,2,1,0,3:T(8,128)} %get-tuple-element.371, f32[12,12,16,3,127]{4,2,1,0,3:T(8,128)} %get-tuple-element.372, ...), kind=kLoop, calls=%fused_computation.30.clone.1 | loop fusion | flops 50429952 | bytes 73058304 | tf_op jit(solution)/shard_map/while/body/eval_jaxpr/add | solution.py:72
  302.3 2.6 convolution_bitcast_fusion.19
  306.8 5.9 %convolution_bitcast_fusion.22 = f32[16,64]{1,0:T(8,128)S(1)} fusion(f32[12,12,16,3,128]{4,2,1,0,3:T(8,128)S(1)} %fusion.99, bf16[10,10,64,3,128]{4,2,1,0,3:T(8,128)(2,1)} %get-tuple-element.428), kind=kOutput, calls=%fused_computation.73.clone.1 | convolution fusion | flops 471859200 | bytes 8458240 | tf_op jit(solution)/shard_map/while/body/eval_jaxpr/xykbz,xylbz->kl/dot_general | solution.py:76
  319.8 1.9 broadcast_multiply_fusion.2
  321.7 22.7 %pad_slice_fusion.27 = (f32[12,12,16,3,127]{4,2,1,0,3:T(8,128)}, f32[12,12,16,3,127]{4,2,1,0,3:T(8,128)}, f32[12,12,16,3,127]{4,2,1,0,3:T(8,128)}, f32[12,12,16,...) fusion(f32[10,10,16,3,128]{4,2,1,0,3:T(8,128)S(1)} %broadcast_m, ...), kind=kLoop, calls=%fused_computation.25.clone.1 | loop fusion | bytes 65660928 | tf_op jit(solution)/shard_map/while/body/eval_jaxpr/slice | solution.py:49
  344.5 1.8 dynamic-slice_convert_fusion.2
  348.1 23.3 %fusion.99 = f32[12,12,16,3,128]{4,2,1,0,3:T(8,128)S(1)} fusion(f32[10,10,16,3,128]{4,2,1,0,3:T(8,128)} %copy-done, f32[10,10,16,3,128]{4,2,1,0,3:T(8,128)S(1)} %broadcast_multiply_fusion.2, f32[12,12,16,3,127]{4,2,1,0,3:T(8,128)} %get-tuple-element.371, f32[12,12,16,3,127]{4,2,1,0,3:T(8,128)} %get-tuple-element.372, ...), kind=kLoop, calls=%fused_computation.30.clone.1 | loop fusion | flops 50429952 | bytes 73058304 | tf_op jit(solution)/shard_map/while/body/eval_jaxpr/add | solution.py:72
  373.1 2.6 convolution_bitcast_fusion.19
  377.5 5.9 %convolution_bitcast_fusion.22 = f32[16,64]{1,0:T(8,128)S(1)} fusion(f32[12,12,16,3,128]{4,2,1,0,3:T(8,128)S(1)} %fusion.99, bf16[10,10,64,3,128]{4,2,1,0,3:T(8,128)(2,1)} %get-tuple-element.428), kind=kOutput, calls=%fused_computation.73.clone.1 | convolution fusion | flops 471859200 | bytes 8458240 | tf_op jit(solution)/shard_map/while/body/eval_jaxpr/xykbz,xylbz->kl/dot_general | solution.py:76
  387.7 51.5 %all-gather.2.cloned.1.call-done = f32[1,16,64,576]{3,2,0,1:T(8,128)} async-done(((f32[1,1,64,576]{3,2,0,1:T(8,128)}), f32[1,16,64,576]{3,2,0,1:T(8,128)}) %all-gather.2.cloned.1.call-update) | async-done | bytes 2359312 | tf_op jit(solution)/shard_map/all_gather | solution.py:134
  439.2 3.5 copy.37
  (143 shorter events, 46.5 us)
Async XLA Ops:
  6.5 432.6 %all-gather.2.cloned.1.call-start = ((), (), s32[]{:S(2)}) async-start(), calls=%async_computation | async-start | bytes 2785280 | tf_op jit(solution)/shard_map/all_gather | solution.py:134
  9.0 7.4 %copy-start.7 = (f32[8,8,128]{2,1,0:T(8,128)S(1)}, f32[8,8,128]{2,1,0:T(8,128)}, u32[]{:S(2)}) copy-start(f32[8,8,128]{2,1,0:T(8,128)} %param.9) | copy-start | bytes 98308
  9.0 7.4 %copy-start.8 = (f32[8,8,128]{2,1,0:T(8,128)S(1)}, f32[8,8,128]{2,1,0:T(8,128)}, u32[]{:S(2)}) copy-start(f32[8,8,128]{2,1,0:T(8,128)} %param.8) | copy-start | bytes 98308
  9.0 7.4 %copy-start.9 = (f32[8,8,128]{2,1,0:T(8,128)S(1)}, f32[8,8,128]{2,1,0:T(8,128)}, u32[]{:S(2)}) copy-start(f32[8,8,128]{2,1,0:T(8,128)} %param.7) | copy-start | bytes 98308
  10.3 35.5 %collective-permute-start.4 = (bf16[3,10,64,3,128]{4,2,1,0,3:T(8,128)(2,1)}, bf16[3,10,64,3,128]{4,2,1,0,3:T(8,128)(2,1)S(1)}, u32[]{:S(2)}, u32[]{:S(2)}) collective-permute-start(bf16[3,10,64,3,128]{4,2,1,0,3:T(8,128)(2,1)} %copy.25), channel_id=1, source_target_pairs={{0,8},{8,16},{16,24},{24,32},{32,40},{40,48},{48,56},{56,64},{64,7... | collective-permute-start | bytes 4423688 | tf_op jit(solution)/shard_map/ppermute | solution.py:12
  15.1 36.1 %collective-permute-start.5 = (bf16[3,10,64,3,128]{4,2,1,0,3:T(8,128)(2,1)}, bf16[3,10,64,3,128]{4,2,1,0,3:T(8,128)(2,1)S(1)}, u32[]{:S(2)}, u32[]{:S(2)}) collective-permute-start(bf16[3,10,64,3,128]{4,2,1,0,3:T(8,128)(2,1)} %copy.26), channel_id=1, source_target_pairs={{8,0},{16,8},{24,16},{32,24},{40,32},{48,40},{56,48},{64,56},{72,6... | collective-permute-start | bytes 4423688 | tf_op jit(solution)/shard_map/ppermute | solution.py:15
  16.4 48.9 %collective-permute-start = (f32[2,8,3,128]{3,1,0,2:T(8,128)S(1)}, f32[2,8,3,128]{3,1,0,2:T(8,128)S(1)}, u32[]{:S(2)}, u32[]{:S(2)}) collective-permute-start(f32[2,8,3,128]{3,1,0,2:T(8,128)S(1)} %get-tuple-element.257), channel_id=1, source_target_pairs={{0,8},{8,16},{16,24},{24,32},{32,40},{40,48},{48,56},{56,64},{64,7... | collective-permute-start | bytes 73736 | tf_op jit(solution)/shard_map/ppermute | solution.py:12
  21.0 44.3 %collective-permute-start.1 = (f32[2,8,3,128]{3,1,0,2:T(8,128)S(1)}, f32[2,8,3,128]{3,1,0,2:T(8,128)S(1)}, u32[]{:S(2)}, u32[]{:S(2)}) collective-permute-start(f32[2,8,3,128]{3,1,0,2:T(8,128)S(1)} %get-tuple-element.258), channel_id=1, source_target_pairs={{8,0},{16,8},{24,16},{32,24},{40,32},{48,40},{56,48},{64,56},{72,6... | collective-permute-start | bytes 73736 | tf_op jit(solution)/shard_map/ppermute | solution.py:15
  51.2 9.9 %slice-start = ((s8[4915200]{0:T(1024)(128)(4,1)}), s8[4194304]{0:T(1024)(128)(4,1)S(1)}, s32[]{:S(2)}) async-start(s8[4915200]{0:T(1024)(128)(4,1)} %bitcast.134), calls=%async_computation.1 | async-start | bytes 8388608
  51.5 9.6 %slice-start.1 = ((s8[4915200]{0:T(1024)(128)(4,1)}), s8[720896]{0:T(1024)(128)(4,1)S(1)}, s32[]{:S(2)}) async-start(s8[4915200]{0:T(1024)(128)(4,1)} %bitcast.134), calls=%async_computation.2 | async-start | bytes 1441792
  55.2 36.8 %collective-permute-start.6 = (bf16[16,3,64,3,128]{4,2,1,0,3:T(8,128)(2,1)}, bf16[16,3,64,3,128]{4,2,1,0,3:T(8,128)(2,1)}, u32[]{:S(2)}, u32[]{:S(2)}) collective-permute-start(bf16[16,3,64,3,128]{4,2,1,0,3:T(8,128)(2,1)} %get-tuple-element.248), channel_id=1, source_target_pairs={{0,1},{1,2},{2,3},{3,4},{4,5},{5,6},{6,7},{8,9},{9,10},{10,11},{11... | collective-permute-start | bytes 7077896 | tf_op jit(solution)/shard_map/ppermute | solution.py:12
  57.3 40.1 %collective-permute-start.7 = (bf16[16,3,64,3,128]{4,2,1,0,3:T(8,128)(2,1)}, bf16[16,3,64,3,128]{4,2,1,0,3:T(8,128)(2,1)}, u32[]{:S(2)}, u32[]{:S(2)}) collective-permute-start(bf16[16,3,64,3,128]{4,2,1,0,3:T(8,128)(2,1)} %get-tuple-element.247), channel_id=1, source_target_pairs={{1,0},{2,1},{3,2},{4,3},{5,4},{6,5},{7,6},{9,8},{10,9},{11,10},{12... | collective-permute-start | bytes 7077896 | tf_op jit(solution)/shard_map/ppermute | solution.py:15
  65.3 20.6 %collective-permute-start.2 = (f32[12,2,3,128]{3,1,0,2:T(2,128)S(1)}, f32[12,2,3,128]{3,1,0,2:T(2,128)S(1)}, u32[]{:S(2)}, u32[]{:S(2)}) collective-permute-start(f32[12,2,3,128]{3,1,0,2:T(2,128)S(1)} %get-tuple-element.255), channel_id=1, source_target_pairs={{0,1},{1,2},{2,3},{3,4},{4,5},{5,6},{6,7},{8,9},{9,10},{10,11},{11... | collective-permute-start | bytes 110600 | tf_op jit(solution)/shard_map/ppermute | solution.py:12
  67.4 20.5 %collective-permute-start.3 = (f32[12,2,3,128]{3,1,0,2:T(2,128)S(1)}, f32[12,2,3,128]{3,1,0,2:T(2,128)S(1)}, u32[]{:S(2)}, u32[]{:S(2)}) collective-permute-start(f32[12,2,3,128]{3,1,0,2:T(2,128)S(1)} %get-tuple-element.256), channel_id=1, source_target_pairs={{1,0},{2,1},{3,2},{4,3},{5,4},{6,5},{7,6},{9,8},{10,9},{11,10},{12... | collective-permute-start | bytes 110600 | tf_op jit(solution)/shard_map/ppermute | solution.py:15
  133.3 1.8 copy-start
  158.4 4.3 copy-start.6
  158.4 4.8 %copy-start.2 = (bf16[10,3,64,3,128]{4,2,1,0,3:T(8,128)(2,1)S(1)}, bf16[10,3,64,3,128]{4,2,1,0,3:T(8,128)(2,1)}, u32[]{:S(2)}) copy-start(bf16[10,3,64,3,128]{4,2,1,0,3:T(8,128)(2,1)} %get-tuple-element.432) | copy-start | bytes 4423684 | tf_op jit(solution)/shard_map/while
  164.4 5.9 %copy-start.3 = (bf16[10,3,64,3,128]{4,2,1,0,3:T(8,128)(2,1)S(1)}, bf16[10,3,64,3,128]{4,2,1,0,3:T(8,128)(2,1)}, u32[]{:S(2)}) copy-start(bf16[10,3,64,3,128]{4,2,1,0,3:T(8,128)(2,1)} %get-tuple-element.433) | copy-start | bytes 4423684 | tf_op jit(solution)/shard_map/while
  164.4 7.2 %copy-start.4 = (bf16[3,3,64,3,128]{4,2,1,0,3:T(8,128)(2,1)S(1)}, bf16[3,3,64,3,128]{4,2,1,0,3:T(8,128)(2,1)}, u32[]{:S(2)}) copy-start(bf16[3,3,64,3,128]{4,2,1,0,3:T(8,128)(2,1)} %get-tuple-element.434) | copy-start | bytes 1327108 | tf_op jit(solution)/shard_map/while
  170.3 1.8 copy-start.1
  170.3 3.0 copy-start.5
  204.4 1.8 copy-start
  229.6 4.3 copy-start.6
  229.6 4.8 %copy-start.2 = (bf16[10,3,64,3,128]{4,2,1,0,3:T(8,128)(2,1)S(1)}, bf16[10,3,64,3,128]{4,2,1,0,3:T(8,128)(2,1)}, u32[]{:S(2)}) copy-start(bf16[10,3,64,3,128]{4,2,1,0,3:T(8,128)(2,1)} %get-tuple-element.432) | copy-start | bytes 4423684 | tf_op jit(solution)/shard_map/while
  235.6 5.9 %copy-start.3 = (bf16[10,3,64,3,128]{4,2,1,0,3:T(8,128)(2,1)S(1)}, bf16[10,3,64,3,128]{4,2,1,0,3:T(8,128)(2,1)}, u32[]{:S(2)}) copy-start(bf16[10,3,64,3,128]{4,2,1,0,3:T(8,128)(2,1)} %get-tuple-element.433) | copy-start | bytes 4423684 | tf_op jit(solution)/shard_map/while
  235.6 7.2 %copy-start.4 = (bf16[3,3,64,3,128]{4,2,1,0,3:T(8,128)(2,1)S(1)}, bf16[3,3,64,3,128]{4,2,1,0,3:T(8,128)(2,1)}, u32[]{:S(2)}) copy-start(bf16[3,3,64,3,128]{4,2,1,0,3:T(8,128)(2,1)} %get-tuple-element.434) | copy-start | bytes 1327108 | tf_op jit(solution)/shard_map/while
  241.5 1.8 copy-start.1
  241.5 3.0 copy-start.5
  275.6 1.8 copy-start
  300.7 4.3 copy-start.6
  300.7 4.8 %copy-start.2 = (bf16[10,3,64,3,128]{4,2,1,0,3:T(8,128)(2,1)S(1)}, bf16[10,3,64,3,128]{4,2,1,0,3:T(8,128)(2,1)}, u32[]{:S(2)}) copy-start(bf16[10,3,64,3,128]{4,2,1,0,3:T(8,128)(2,1)} %get-tuple-element.432) | copy-start | bytes 4423684 | tf_op jit(solution)/shard_map/while
  306.7 5.9 %copy-start.3 = (bf16[10,3,64,3,128]{4,2,1,0,3:T(8,128)(2,1)S(1)}, bf16[10,3,64,3,128]{4,2,1,0,3:T(8,128)(2,1)}, u32[]{:S(2)}) copy-start(bf16[10,3,64,3,128]{4,2,1,0,3:T(8,128)(2,1)} %get-tuple-element.433) | copy-start | bytes 4423684 | tf_op jit(solution)/shard_map/while
  306.7 7.2 %copy-start.4 = (bf16[3,3,64,3,128]{4,2,1,0,3:T(8,128)(2,1)S(1)}, bf16[3,3,64,3,128]{4,2,1,0,3:T(8,128)(2,1)}, u32[]{:S(2)}) copy-start(bf16[3,3,64,3,128]{4,2,1,0,3:T(8,128)(2,1)} %get-tuple-element.434) | copy-start | bytes 1327108 | tf_op jit(solution)/shard_map/while
  312.6 1.8 copy-start.1
  312.6 3.0 copy-start.5
  346.3 1.8 copy-start
  371.4 4.3 copy-start.6
  371.4 4.8 %copy-start.2 = (bf16[10,3,64,3,128]{4,2,1,0,3:T(8,128)(2,1)S(1)}, bf16[10,3,64,3,128]{4,2,1,0,3:T(8,128)(2,1)}, u32[]{:S(2)}) copy-start(bf16[10,3,64,3,128]{4,2,1,0,3:T(8,128)(2,1)} %get-tuple-element.432) | copy-start | bytes 4423684 | tf_op jit(solution)/shard_map/while
  377.4 5.9 %copy-start.3 = (bf16[10,3,64,3,128]{4,2,1,0,3:T(8,128)(2,1)S(1)}, bf16[10,3,64,3,128]{4,2,1,0,3:T(8,128)(2,1)}, u32[]{:S(2)}) copy-start(bf16[10,3,64,3,128]{4,2,1,0,3:T(8,128)(2,1)} %get-tuple-element.433) | copy-start | bytes 4423684 | tf_op jit(solution)/shard_map/while
  377.4 7.2 %copy-start.4 = (bf16[3,3,64,3,128]{4,2,1,0,3:T(8,128)(2,1)S(1)}, bf16[3,3,64,3,128]{4,2,1,0,3:T(8,128)(2,1)}, u32[]{:S(2)}) copy-start(bf16[3,3,64,3,128]{4,2,1,0,3:T(8,128)(2,1)} %get-tuple-element.434) | copy-start | bytes 1327108 | tf_op jit(solution)/shard_map/while
  383.3 1.8 copy-start.1
  383.4 3.0 copy-start.5
  387.0 0.7 copy-start.10
Sparse Core Ops, SparseCore 0:
  387.8 51.3 all-gather.1
where the time goes:
time: 452 us; the launch traced here: 450 us
  other arithmetic  134 us (30%)
  local copies, waits for them, and re-layouts  118 us (26%)
  waiting for transfers between devices  92.8 us (21%)
  matrix products  60.9 us (13%)
  starting transfers between devices  21.7 us (5%)
  between operations  13.6 us (3%)
  loops' own time  8.51 us (2%)
    add x4, other arithmetic, frame_image(): return centre * framed - coupling * spread + volume * (total - framed)  93.3 us
    slice x4, local copies, waits for them, and re-layouts, depth_shift(): return jnp.concatenate([zero_slab, values[..., :-1]], axis=-1)  90.9 us
    dot_general x36, matrix products, pair_block(): jnp.einsum('xykbz,xylbz->kl', image, piece.astype(jnp.float32), precision...  60.9 us
    all_gather x1, waiting for transfers between devices, local(): return lax.all_gather(rows[None, None], 'sx', axis=1, tiled=True)  51.5 us
    ppermute x4, waiting for transfers between devices, with_halo(): lax.ppermute(lax.slice_in_dim(block, block.shape[dim] - width, None, axis...  38.5 us
    convert_element_type x7, other arithmetic, weighted(): (share[:, :, None, None, None] * piece.astype(jnp.float32)).astype(jnp.bf...  18.2 us
    ppermute x4, starting transfers between devices, with_halo(): lax.ppermute(lax.slice_in_dim(block, block.shape[dim] - width, None, axis...  12 us
    unnamed x17, local copies, waits for them, and re-layouts  11.4 us
  transfers between devices with their start and end apart: 9, of which 5 were waited for; matrix products, arithmetic and copies ran while one was open for 5% of the time, Pallas kernels for 0%

commit v1 on v0

v1 whole, which is shorter than its diff:
```python
import functools

import jax
import jax.numpy as jnp
from jax import lax
from jax.experimental import pallas as pl
from jax.experimental.pallas import tpu as pltpu
from jax.sharding import PartitionSpec as P

F32 = jnp.float32
BF16 = jnp.bfloat16
KAP, DIA, VOL, MID, LOW, UPP = range(6)
NT = (((1,), (1,)), ((), ()))
VMEM_LIMIT = 56 * 1024 * 1024


def cover(start, length, cell, count, margin):
    places = start + jnp.arange(length, dtype=jnp.int32)
    base = jnp.floor_divide(places, cell)
    total = jnp.zeros((length,), jnp.int32)
    for step_off in (-1, 0, 1):
        owner = base + step_off
        inside = (
            (owner >= 0)
            & (owner < count)
            & (places >= owner * cell - margin)
            & (places < owner * cell + cell + margin)
        )
        total = total + inside.astype(jnp.int32)
    in_grid = (places >= 0) & (places < cell * count)
    safe = jnp.maximum(total, 1).astype(F32)
    return jnp.where(in_grid & (total > 0), 1.0 / safe, 0.0)


def neighbours(count):
    up = [(i, i + 1) for i in range(count - 1)]
    return up, [(b, a) for a, b in up]


def with_halo(block, sides, width):
    for axis, dim in sides:
        up, down = neighbours(lax.axis_size(axis))
        low = lax.ppermute(
            lax.slice_in_dim(block, block.shape[dim] - width, None, axis=dim), axis, up
        )
        high = lax.ppermute(lax.slice_in_dim(block, 0, width, axis=dim), axis, down)
        block = jnp.concatenate([low, block, high], axis=dim)
    return block


def cell_rows(centre, coupling, volume, share_x, share_y):
    frame = with_halo(jnp.stack([centre, coupling, volume]), (("sx", 1), ("sy", 2)), 2)
    share = (share_x[:, None] * share_y[None, :])[:, :, None]
    kap = frame[1] * share
    vol = frame[2] * share * share
    dia = frame[0] * share * share - vol + 0.5 * kap * kap
    base = kap * (1.0 / 16.0)
    lane = lax.broadcasted_iota(jnp.int32, base.shape, 2)
    low = jnp.where(lane == 0, 0.0, base)
    upp = jnp.where(lane == base.shape[2] - 1, 0.0, base)
    none = jnp.zeros_like(base)
    return jnp.stack([kap, dia, vol, base + base, low, upp, none, none], axis=2)


def spread3(w):
    return [w[0], w[0] + w[0] + w[1], w[0] + w[1] + w[1] + w[2]]


def image_terms(lines, values, rows):
    out = []
    total = None
    if values is not None:
        total = rows[VOL] * (values[0] + values[1] + values[2])
    for a in range(3):
        r = lines[a]
        depth = rows[MID] * r + rows[LOW] * pltpu.roll(r, 1, 1) + rows[UPP] * pltpu.roll(r, 127, 1)
        out.append(-depth if values is None else rows[DIA] * values[a] + total - depth)
    return out


def put_image(img_ref, slot, pos, chunk, image):
    for a in range(3):
        high = image[a].astype(BF16)
        low = (image[a] - high.astype(F32)).astype(BF16)
        lanes = pl.ds((pos * 3 + a) * 128, 128)
        img_ref[slot, pl.ds(chunk * 16, 16), lanes] = high
        img_ref[slot, pl.ds(64 + chunk * 16, 16), lanes] = low


def cell_coefs(coef_ref, x, y, names):
    return {n: coef_ref[x, y, pl.ds(n, 1), :] for n in names}


def side(blocks):
    return jnp.concatenate(blocks, axis=1)


def fold(total):
    return total[:, :64] + total[:, 64:]


def fold_rows(total):
    return total[:64] + total[64:]


def own_kernel(m_hbm, coef_ref, out_ref, m_ref, q_ref, img_ref, acc_ref, sems):
    ext = m_ref.shape[0]
    copies = [pltpu.make_async_copy(m_hbm.at[x], m_ref.at[x], sems.at[x]) for x in range(ext)]
    for copy in copies:
        copy.start()
    zero = jnp.zeros(q_ref.shape[1:], F32)
    q_ref[0] = zero
    q_ref[ext + 1] = zero
    acc_ref[...] = jnp.zeros_like(acc_ref)

    def first(x, _):
        pltpu.make_async_copy(m_hbm.at[x], m_ref.at[x], sems.at[x]).wait()
        kaps = [coef_ref[x + 1, j + 1, pl.ds(KAP, 1), :] for j in range(ext)]
        for a in range(3):
            for chunk in range(4):
                rows = pl.ds(chunk * 16, 16)
                pair = None
                last = None
                for j in range(ext):
                    w = m_ref[x, j, a, rows, :].astype(F32) * kaps[j]
                    if j > 0:
                        now = last + w
                        q_ref[x + 1, j - 1, a, rows, :] = now + (last if pair is None else pair)
                        pair = now
                    last = w
                q_ref[x + 1, ext - 1, a, rows, :] = pair + last
        return 0

    lax.fori_loop(0, ext, first, 0)

    def second(x, _):
        total = acc_ref[...]
        for j in range(ext):
            rows_of = cell_coefs(coef_ref, x + 1, j + 1, (DIA, VOL, MID, LOW, UPP))
            for chunk in range(4):
                rows = pl.ds(chunk * 16, 16)
                values = [m_ref[x, j, a, rows, :].astype(F32) for a in range(3)]
                lines = []
                for a in range(3):
                    mid = q_ref[x + 1, j, a, rows, :]
                    lines.append(
                        (q_ref[x, j, a, rows, :] + mid) + (mid + q_ref[x + 2, j, a, rows, :])
                    )
                put_image(img_ref, j // 2, j % 2, chunk, image_terms(lines, values, rows_of))
            if j % 2 == 1:
                left = side([m_ref[x, i, a] for i in (j - 1, j) for a in range(3)])
                total = total + lax.dot_general(
                    left, img_ref[j // 2], NT, preferred_element_type=F32
                )
        acc_ref[...] = total
        return 0

    lax.fori_loop(0, ext, second, 0)
    out_ref[...] = fold(acc_ref[...])


def rows_kernel(m_hbm, south_hbm, north_hbm, coef_ref, out_ref, d_ref, r_ref, q_ref, img_ref, acc_ref, sems):
    ext = m_hbm.shape[0]
    copies = [
        pltpu.make_async_copy(south_hbm, r_ref.at[0], sems.at[0]),
        pltpu.make_async_copy(north_hbm, r_ref.at[1], sems.at[1]),
        pltpu.make_async_copy(m_hbm.at[:, pl.ds(0, 3)], d_ref.at[0], sems.at[2]),
        pltpu.make_async_copy(m_hbm.at[:, pl.ds(ext - 3, 3)], d_ref.at[1], sems.at[3]),
    ]
    for copy in copies:
        copy.start()
    q_ref[...] = jnp.zeros_like(q_ref)
    acc_ref[...] = jnp.zeros_like(acc_ref)
    for copy in copies:
        copy.wait()
    raw_at = ((2, 1, 0), (0, 1, 2))
    raw_coef = ((2, 1, 0), (9, 10, 11))
    img_coef = ((3, 2, 1), (8, 9, 10))
    own_at = ((2, 1, 0), (0, 1, 2))
    for s in range(2):

        def first(x, _, s=s):
            kaps = [coef_ref[x + 1, raw_coef[s][d], pl.ds(KAP, 1), :] for d in range(3)]
            for a in range(3):
                for chunk in range(4):
                    rows = pl.ds(chunk * 16, 16)
                    w = [r_ref[s, x, raw_at[s][d], a, rows, :].astype(F32) * kaps[d] for d in range(3)]
                    for e, value in enumerate(spread3(w)):
                        q_ref[x + 1, e, a, rows, :] = value
            return 0

        lax.fori_loop(0, ext, first, 0)

        def second(x, _, s=s):
            for e in range(3):
                rows_of = cell_coefs(coef_ref, x + 1, img_coef[s][e], (DIA, VOL, MID, LOW, UPP))
                for chunk in range(4):
                    rows = pl.ds(chunk * 16, 16)
                    values = None
                    if e > 0:
                        values = [r_ref[s, x, raw_at[s][e - 1], a, rows, :].astype(F32) for a in range(3)]
                    lines = []
                    for a in range(3):
                        mid = q_ref[x + 1, e, a, rows, :]
                        lines.append(
                            (q_ref[x, e, a, rows, :] + mid) + (mid + q_ref[x + 2, e, a, rows, :])
                        )
                    put_image(img_ref, 0, e, chunk, image_terms(lines, values, rows_of))
            left = side([d_ref[s, x, own_at[s][e], a] for e in range(3) for a in range(3)])
            acc_ref[s] += lax.dot_general(left, img_ref[0], NT, preferred_element_type=F32)
            return 0

        lax.fori_loop(0, ext, second, 0)
    out_ref[...] = side([fold(acc_ref[0]), fold(acc_ref[1])])


def columns_kernel(
    odd_ref, m_hbm, south_hbm, north_hbm, main_hbm, corner_hbm, coef_ref, own_ref, rows_ref, out_ref,
    d_ref, s_ref, n_ref, x_ref, y_ref, q_ref, img_ref, acc_ref, cor_ref, sems,
):
    ext = m_hbm.shape[0]
    odd = odd_ref[0]
    start = jnp.where(odd == 1, 0, ext - 3)
    copies = [
        pltpu.make_async_copy(m_hbm.at[pl.ds(start, 3)], d_ref.at[:, pl.ds(1, ext)], sems.at[0]),
        pltpu.make_async_copy(south_hbm, s_ref, sems.at[1]),
        pltpu.make_async_copy(north_hbm, n_ref, sems.at[2]),
        pltpu.make_async_copy(main_hbm, x_ref.at[:, pl.ds(1, ext)], sems.at[3]),
        pltpu.make_async_copy(corner_hbm, y_ref, sems.at[4]),
    ]
    for copy in copies:
        copy.start()
    none = jnp.zeros((3, 3, 64, 128), BF16)
    for edge in (0, ext + 1):
        d_ref[:, edge] = none
        x_ref[:, edge] = none
    q_ref[...] = jnp.zeros_like(q_ref)
    acc_ref[...] = jnp.zeros_like(acc_ref)
    cor_ref[...] = jnp.zeros_like(cor_ref)
    for copy in copies:
        copy.wait()

    def pick(high, low):
        return jnp.where(odd == 1, low, high)

    names = (DIA, VOL, MID, LOW, UPP)
    xi = [pick(d, 2 - d) for d in range(3)]
    xc = [pick(9 + d, 2 - d) for d in range(3)]
    xe = [pick(8 + e, 3 - e) for e in range(3)]
    xn = [pick(7 + e, 2 - e) for e in range(3)]
    yn = [pick(2 - e, 7 + e) for e in range(3)]
    yi = [pick(2 - d, d) for d in range(3)]
    yc = [pick(2 - d, 9 + d) for d in range(3)]
    ye = [pick(3 - e, 8 + e) for e in range(3)]

    def main_first(y, _):
        kaps = [coef_ref[xc[d], y + 1, pl.ds(KAP, 1), :] for d in range(3)]
        for a in range(3):
            for chunk in range(4):
                rows = pl.ds(chunk * 16, 16)
                w = [x_ref[xi[d], y + 1, a, rows, :].astype(F32) * kaps[d] for d in range(3)]
                for e, value in enumerate(spread3(w)):
                    q_ref[y + 2, e, a, rows, :] = value
        return 0

    lax.fori_loop(0, ext, main_first, 0)

    def main_second(f, corner, other):
        for e in range(3):
            rows_of = cell_coefs(coef_ref, xe[e], f, names)
            for chunk in range(4):
                rows = pl.ds(chunk * 16, 16)
                values = None
                if e > 0:
                    values = [x_ref[xi[e - 1], f, a, rows, :].astype(F32) for a in range(3)]
                lines = []
                for a in range(3):
                    mid = q_ref[f + 1, e, a, rows, :]
                    lines.append((q_ref[f, e, a, rows, :] + mid) + (mid + q_ref[f + 2, e, a, rows, :]))
                put_image(img_ref, 0, e, chunk, image_terms(lines, values, rows_of))
        left = side([d_ref[xi[e], f, a] for e in range(3) for a in range(3)])
        acc_ref[...] += lax.dot_general(left, img_ref[0], NT, preferred_element_type=F32)
        if corner is not None:
            right = side([other(e)[a] for e in range(3) for a in range(3)])
            cor_ref[corner] += lax.dot_general(img_ref[0], right, NT, preferred_element_type=F32)

    def loop(lo, hi, corner, other):
        def body(f, _):
            main_second(f, corner, None if other is None else lambda e: other(e, f))
            return 0

        lax.fori_loop(lo, hi, body, 0)

    loop(0, 3, 0, lambda e, f: [s_ref[xn[e], f, a] for a in range(3)])
    loop(3, 9, None, None)
    loop(9, 12, 1, lambda e, f: [n_ref[xn[e], f - 9, a] for a in range(3)])

    for s, ref in ((0, s_ref), (1, n_ref)):
        raw_y = (0, 1, 2) if s == 0 else (5, 4, 3)
        raw_f = (1, 2, 3) if s == 0 else (10, 9, 8)
        img_f = (0, 1, 2) if s == 0 else (11, 10, 9)
        img_y = (0, 1, 2) if s == 0 else (2, 1, 0)
        for t in range(3):
            kaps = [coef_ref[yc[d], raw_f[t], pl.ds(KAP, 1), :] for d in range(3)]
            for a in range(3):
                for chunk in range(4):
                    rows = pl.ds(chunk * 16, 16)
                    w = [y_ref[yi[d], raw_y[t], a, rows, :].astype(F32) * kaps[d] for d in range(3)]
                    for e, value in enumerate(spread3(w)):
                        q_ref[t, e, a, rows, :] = value
        for u in range(3):
            for e in range(3):
                rows_of = cell_coefs(coef_ref, ye[e], img_f[u], names)
                for chunk in range(4):
                    rows = pl.ds(chunk * 16, 16)
                    values = None
                    if e > 0 and u > 0:
                        values = [
                            y_ref[yi[e - 1], raw_y[u - 1], a, rows, :].astype(F32) for a in range(3)
                        ]
                    lines = []
                    for a in range(3):
                        q = [q_ref[t, e, a, rows, :] for t in range(u + 1)]
                        if u == 0:
                            lines.append(q[0])
                        elif u == 1:
                            lines.append(q[0] + q[0] + q[1])
                        else:
                            lines.append(q[0] + q[1] + q[1] + q[2])
                    put_image(img_ref, 0, e, chunk, image_terms(lines, values, rows_of))
            right = side([ref[yn[e], img_y[u], a] for e in range(3) for a in range(3)])
            cor_ref[2 + s] += lax.dot_general(img_ref[0], right, NT, preferred_element_type=F32)

    corner = [fold_rows(cor_ref[i]) for i in range(4)]
    east = [jnp.where(odd == 1, corner[2 + s], corner[s]) for s in range(2)]
    west = [jnp.where(odd == 1, corner[s], corner[2 + s]) for s in range(2)]
    around = rows_ref[...]
    out_ref[...] = side(
        [
            east[0], fold(acc_ref[...]), east[1], around[:, :64],
            own_ref[...], around[:, 64:], west[0], west[1],
        ]
    )


def final_kernel(odd_ref, slot_ref, *refs):
    *pieces, out_hbm, g_ref, o_ref, sems, out_sem = refs
    count = len(pieces) // 2
    copies = []
    for h in range(2):
        for i in range(count):
            ref = pieces[h * count + i]
            for j in range(4):
                at = h * 16 + i * 4 + j
                copies.append(
                    pltpu.make_async_copy(
                        ref.at[j], g_ref.at[slot_ref[at] + 1, pl.ds(h * 32, 32)], sems.at[at]
                    )
                )
    for copy in copies:
        copy.start()
    odd = odd_ref[0]
    none = jnp.zeros(g_ref.shape[1:], F32)
    g_ref[0] = none
    g_ref[17] = none
    for copy in copies:
        copy.wait()

    def body(p, _):
        before = g_ref.at[p]
        here = g_ref.at[p + 1]
        after = g_ref.at[p + 2]
        turned_from = jnp.where(odd == 1, p + 2, p)
        turned = jnp.transpose(g_ref[turned_from, :, pl.ds(0, 128)])[64:]
        own = here[:, pl.ds(64, 64)]
        left = jnp.where(odd == 1, own, turned)
        right = jnp.where(odd == 1, turned, own)
        o_ref[p] = jnp.concatenate(
            [
                before[:, pl.ds(0, 64)], left, before[:, pl.ds(128, 64)], here[:, pl.ds(192, 192)],
                after[:, pl.ds(384, 64)], right, after[:, pl.ds(448, 64)],
            ],
            axis=1,
        )
        return 0

    lax.fori_loop(0, 16, body, 0)
    done = pltpu.make_async_copy(o_ref, out_hbm, out_sem)
    done.start()
    done.wait()


def any_spec():
    return pl.BlockSpec(memory_space=pl.ANY)


def vmem_spec():
    return pl.BlockSpec(memory_space=pltpu.VMEM)


def smem_spec():
    return pl.BlockSpec(memory_space=pltpu.SMEM)


def call(kernel, out_shape, in_specs, out_spec, scratch, flops, name):
    return pl.pallas_call(
        kernel,
        out_shape=out_shape,
        in_specs=in_specs,
        out_specs=out_spec,
        scratch_shapes=scratch,
        compiler_params=pltpu.CompilerParams(vmem_limit_bytes=VMEM_LIMIT),
        cost_estimate=pl.CostEstimate(flops=flops, bytes_accessed=5_000_000, transcendentals=0),
        name=name,
    )


def ring(value, pairs):
    return [value] + [lax.ppermute(value, "sx", pairs(k)) for k in (1, 2, 3)]


def gathered(rows, nz, nx):
    def along_z(k):
        return [(z * nx + x, (z + k) % nz * nx + x) for z in range(nz) for x in range(nx)]

    def along_x(k):
        return [(z * nx + x, z * nx + (x + k) % nx) for z in range(nz) for x in range(nx)]

    half = rows.shape[0] // 2
    part = [rows[:half], rows[half:]]
    first = [jnp.stack(ring(part[0], along_z)), jnp.stack(ring(part[1], along_x))]
    return ring(first[0], along_x), ring(first[1], along_z)


def local(modes, centre, coupling, volume):
    ext = modes.shape[0]
    cell = centre.shape[0]
    margin = (ext - cell) // 2
    nx = lax.axis_size("sx")
    ny = lax.axis_size("sy")
    ix = lax.axis_index("sx")
    iy = lax.axis_index("sy")
    odd = lax.rem(iy, 2)
    share_x = cover(ix * cell - margin - 1, ext + 2, cell, nx, margin)
    share_y = cover(iy * cell - margin - 1, ext + 2, cell, ny, margin)
    coef = cell_rows(centre, coupling, volume, share_x, share_y)

    m = jnp.transpose(modes, (0, 1, 3, 2, 4))

    def flat(x, y):
        return x * ny + y

    main_pairs, other_pairs = [], []
    for y in range(ny):
        for x in range(nx - 1):
            lo, hi = flat(x, y), flat(x + 1, y)
            main_pairs.append((hi, lo) if y % 2 == 0 else (lo, hi))
            other_pairs.append((lo, hi) if y % 2 == 0 else (hi, lo))
    main_start = jnp.where(odd == 1, ext - 3, 0)
    corner_start = jnp.where(odd == 1, 0, ext - 3)
    main = lax.ppermute(lax.dynamic_slice_in_dim(m, main_start, 3, 0), ("sx", "sy"), main_pairs)
    edge = lax.dynamic_slice_in_dim(m, corner_start, 3, 0)
    edge = jnp.concatenate([edge[:, :3], edge[:, ext - 3 :]], axis=1)
    corner = lax.ppermute(edge, ("sx", "sy"), other_pairs)
    up, down = neighbours(ny)
    south = lax.ppermute(m[:, ext - 3 :], "sy", up)
    north = lax.ppermute(m[:, :3], "sy", down)

    odd1 = odd.astype(jnp.int32).reshape(1)
    own = call(
        own_kernel,
        jax.ShapeDtypeStruct((64, 64), F32),
        [any_spec(), vmem_spec()],
        vmem_spec(),
        [
            pltpu.VMEM((ext, ext, 3, 64, 128), BF16),
            pltpu.VMEM((ext + 2, ext, 3, 64, 128), F32),
            pltpu.VMEM((ext // 2, 128, 768), BF16),
            pltpu.VMEM((64, 128), F32),
            pltpu.SemaphoreType.DMA((ext,)),
        ],
        4_000_000_000,
        "own_gram",
    )(m, coef)
    around = call(
        rows_kernel,
        jax.ShapeDtypeStruct((64, 128), F32),
        [any_spec(), any_spec(), any_spec(), vmem_spec()],
        vmem_spec(),
        [
            pltpu.VMEM((2, ext, 3, 3, 64, 128), BF16),
            pltpu.VMEM((2, ext, 3, 3, 64, 128), BF16),
            pltpu.VMEM((ext + 2, 3, 3, 64, 128), F32),
            pltpu.VMEM((1, 128, 1152), BF16),
            pltpu.VMEM((2, 64, 128), F32),
            pltpu.SemaphoreType.DMA((4,)),
        ],
        2_000_000_000,
        "row_gram",
    )(m, south, north, coef)
    rows = call(
        columns_kernel,
        jax.ShapeDtypeStruct((64, 512), F32),
        [smem_spec()] + [any_spec()] * 5 + [vmem_spec()] * 3,
        vmem_spec(),
        [
            pltpu.VMEM((3, ext + 2, 3, 64, 128), BF16),
            pltpu.VMEM((ext, 3, 3, 64, 128), BF16),
            pltpu.VMEM((ext, 3, 3, 64, 128), BF16),
            pltpu.VMEM((3, ext + 2, 3, 64, 128), BF16),
            pltpu.VMEM((3, 6, 3, 64, 128), BF16),
            pltpu.VMEM((ext + 4, 3, 3, 64, 128), F32),
            pltpu.VMEM((1, 128, 1152), BF16),
            pltpu.VMEM((64, 128), F32),
            pltpu.VMEM((4, 128, 64), F32),
            pltpu.SemaphoreType.DMA((5,)),
        ],
        2_000_000_000,
        "column_gram",
    )(odd1, m, south, north, main, corner, coef, own, around)

    nz, nw = 4, nx // 4
    first, second = gathered(rows, nz, nw)
    iz, iw = ix // nw, lax.rem(ix, nw)
    slots = []
    for i in range(4):
        for j in range(4):
            slots.append(lax.rem(iz - j + nz, nz) * nw + lax.rem(iw - i + nw, nw))
    for i in range(4):
        for j in range(4):
            slots.append(lax.rem(iz - i + nz, nz) * nw + lax.rem(iw - j + nw, nw))
    slot = jnp.stack(slots).astype(jnp.int32)
    pieces = first + second
    out = call(
        final_kernel,
        jax.ShapeDtypeStruct((nx, 64, 576), F32),
        [smem_spec(), smem_spec()] + [any_spec()] * len(pieces),
        any_spec(),
        [
            pltpu.VMEM((nx + 2, 64, 512), F32),
            pltpu.VMEM((nx, 64, 576), F32),
            pltpu.SemaphoreType.DMA((32,)),
            pltpu.SemaphoreType.DMA,
        ],
        1_000_000,
        "assemble",
    )(odd1, slot, *pieces)
    return out[None]


def solution(mesh):
    in_specs = (
        P("sx", "sy", None, None, None),
        P("sx", "sy", None),
        P("sx", "sy", None),
        P("sx", "sy", None),
    )
    out_specs = P("sy", None, None, None)
    return jax.shard_map(local, mesh=mesh, in_specs=in_specs, out_specs=out_specs, check_vma=False)
```

time: 452 us -> 145 us (0.32)
  other arithmetic: 134 us -> 4.25 us
  local copies, waits for them, and re-layouts: 118 us -> 18.2 us
  matrix products: 60.9 us -> 0 us
  waiting for transfers between devices: 92.8 us -> 34.8 us
  Pallas kernels: 0 us -> 46.7 us
  starting transfers between devices: 21.7 us -> 40 us
  between operations: 13.6 us -> 0.31 us
  loops' own time: 8.51 us -> 0 us
    add x4 -> x0, other arithmetic: 93.3 us -> none  [frame_image(): return centre * framed - coupling * spread + volume * (total - framed)]
    slice x10 -> x2, local copies, waits for them, and re-layouts: 97.4 us -> 6.19 us  [the longest x1 4.2 us: local(): north = lax.ppermute(m[:, :3], 'sy', down)]
    dot_general x36 -> x0, matrix products: 60.9 us -> none  [pair_block(): jnp.einsum('xykbz,xylbz->kl', image, piece.astype(jnp.float32), precision...]
    all_gather x1 -> x0, waiting for transfers between devices: 51.5 us -> none  [local(): return lax.all_gather(rows[None, None], 'sx', axis=1, tiled=True)]
    pallas_call x0 -> x4, Pallas kernels: none -> 46.7 us  [the longest x1 14.2 us: local(): call(rows_kernel, jax.ShapeDtypeStruct((64, 128), F32), [any_spec(), any_...]
    ppermute x4 -> x2, waiting for transfers between devices: 38.5 us -> 0.01 us  [with_halo(): lax.ppermute(lax.slice_in_dim(block, block.shape[dim] - width, None, axis...]
    ppermute x4 -> x18, waiting for transfers between devices: 2.81 us -> 34.8 us  [the longest x12 25.3 us: ring(): return [value] + [lax.ppermute(value, 'sx', pairs(k)) for k in (1, 2, 3)]]
    convert_element_type x11 -> x0, other arithmetic: 26.1 us -> none  [the longest x7 18.2 us: weighted(): (share[:, :, None, None, None] * piece.astype(jnp.float32)).astype(jnp.bf...]
  transfers between devices with their start and end apart: 9 -> 20, of which waited for: 5 -> 8; matrix products, arithmetic and copies ran while one was open for 5% -> 10% of each run, Pallas kernels for 0% -> 19%
where the time goes in v1:
time: 145 us; the launch traced here: 144 us
  Pallas kernels  46.7 us (32%)
  starting transfers between devices  40 us (28%)
  waiting for transfers between devices  34.8 us (24%)
  local copies, waits for them, and re-layouts  18.2 us (13%)
  other arithmetic  4.25 us (3%)
    ppermute x12, waiting for transfers between devices, ring(): return [value] + [lax.ppermute(value, 'sx', pairs(k)) for k in (1, 2, 3)]  25.3 us
    ppermute x12, starting transfers between devices, ring(): return [value] + [lax.ppermute(value, 'sx', pairs(k)) for k in (1, 2, 3)]  18 us
    pallas_call x1, Pallas kernels, local(): call(rows_kernel, jax.ShapeDtypeStruct((64, 128), F32), [any_spec(), any_...  14.2 us
    pallas_call x1, Pallas kernels, local(): call(own_kernel, jax.ShapeDtypeStruct((64, 64), F32), [any_spec(), vmem_s...  13.4 us
    pallas_call x1, Pallas kernels, local(): call(columns_kernel, jax.ShapeDtypeStruct((64, 512), F32), [smem_spec()]...  11.9 us
    ppermute x2, waiting for transfers between devices, with_halo(): high = lax.ppermute(lax.slice_in_dim(block, 0, width, axis=dim), axis, down)  9.55 us
    ppermute x2, starting transfers between devices, with_halo(): lax.ppermute(lax.slice_in_dim(block, block.shape[dim] - width, None, axis...  7.58 us
    pallas_call x1, Pallas kernels, local(): call(final_kernel, jax.ShapeDtypeStruct((nx, 64, 576), F32), [smem_spec()...  7.22 us
  transfers between devices with their start and end apart: 20, of which 8 were waited for; matrix products, arithmetic and copies ran while one was open for 10% of the time, Pallas kernels for 19%

profile of v1, /device:TPU:24, one launch (start us, length us, event | category | flops | bytes accessed | tf_op | source)
XLA Modules:
  0.0 144.3 jit_solution(10469259984116200192)
XLA Ops:
  0.0 4.2 %fusion.10 = (bf16[10,3,3,64,128]{4,3,2,1,0:T(8,128)(2,1)}, bf16[10,3,3,64,128]{4,3,2,1,0:T(8,128)(2,1)}) fusion(bf16[10,10,3,64,128]{4,3,2,1,0:T(8,128)(2,1)} %bitcast.58), kind=kLoop, calls=%fused_computation.54 | loop fusion | bytes 5898240 | tf_op jit(solution)/shard_map/slice | solution.py:467
  4.2 1.9 %collective-permute-start = (bf16[10,3,3,64,128]{4,3,2,1,0:T(8,128)(2,1)}, bf16[10,3,3,64,128]{4,3,2,1,0:T(8,128)(2,1)S(1)}, u32[]{:S(2)}, u32[]{:S(2)}) collective-permute-start(bf16[10,3,3,64,128]{4,3,2,1,0:T(8,128)(2,1)} %get-tuple-element.12), channel_id=1, source_target_pairs={{0,1},{1,2},{2,3},{3,4},{4,5},{5,6},{6,7},{8,9},{9,10},{10,11},{11... | collective-permute-start | bytes 4423688 | tf_op jit(solution)/shard_map/ppermute | solution.py:466
  6.1 3.6 %collective-permute-start.1 = (bf16[10,3,3,64,128]{4,3,2,1,0:T(8,128)(2,1)}, bf16[10,3,3,64,128]{4,3,2,1,0:T(8,128)(2,1)S(1)}, u32[]{:S(2)}, u32[]{:S(2)}) collective-permute-start(bf16[10,3,3,64,128]{4,3,2,1,0:T(8,128)(2,1)} %get-tuple-element.11), channel_id=1, source_target_pairs={{1,0},{2,1},{3,2},{4,3},{5,4},{6,5},{7,6},{9,8},{10,9},{11,10},{12... | collective-permute-start | bytes 4423688 | tf_op jit(solution)/shard_map/ppermute | solution.py:467
  9.8 4.5 %dynamic-slice_bitcast_fusion = (bf16[3,10,3,64,128]{4,3,2,1,0:T(8,128)(2,1)}, bf16[3,10,3,64,128]{4,3,2,1,0:T(8,128)(2,1)}) fusion(bf16[10,10,64,3,128]{4,2,3,1,0:T(8,128)(2,1)} %param.4, s32[]{:T(128)S(6)} %select_n.68, s32[]{:T(128)S(6)} %select_n.67), kind=kLoop, calls=%fused_computation | loop fusion | bytes 5898248 | tf_op jit(solution)/shard_map/dynamic_slice | solution.py:462
  14.3 1.3 collective-permute-start.2
  15.7 0.7 pad_maximum_fusion.16
  16.3 1.3 collective-permute-start.5
  17.6 5.2 %collective-permute-start.4 = (f32[3,2,8,128]{3,0,2,1:T(4,128)}, f32[3,2,8,128]{3,0,2,1:T(4,128)S(1)}, u32[]{:S(2)}, u32[]{:S(2)}) collective-permute-start(f32[3,2,8,128]{3,0,2,1:T(4,128)} %get-tuple-element.21), channel_id=1, source_target_pairs={{0,8},{8,16},{16,24},{24,32},{32,40},{40,48},{48,56},{56,64},{64,7... | collective-permute-start | bytes 73736 | tf_op jit(solution)/shard_map/ppermute | solution.py:43
  22.8 2.0 %fusion.11 = (bf16[3,3,3,64,128]{4,3,2,1,0:T(8,128)(2,1)S(1)}, bf16[3,3,3,64,128]{4,3,2,1,0:T(8,128)(2,1)}) fusion(bf16[3,10,3,64,128]{4,3,2,1,0:T(8,128)(2,1)} %get-tuple-element.9), kind=kLoop, calls=%fused_computation.55 | loop fusion | bytes 1769472 | tf_op jit(solution)/shard_map/slice | solution.py:463
  24.8 0.1 broadcast_multiply_fusion
  24.9 2.0 %pad_maximum_fusion = bf16[3,6,3,64,128]{4,3,2,1,0:T(8,128)(2,1)} fusion(bf16[3,3,3,64,128]{4,3,2,1,0:T(8,128)(2,1)} %get-tuple-element.14, bf16[3,3,3,64,128]{4,3,2,1,0:T(8,128)(2,1)S(1)} %get-tuple-element.13), kind=kLoop, calls=%fused_computation.2 | loop fusion | flops 442368 | bytes 1769472 | tf_op jit(solution)/shard_map/concatenate | solution.py:463
  27.0 9.5 %collective-permute-done.5 = f32[3,2,8,128]{3,0,2,1:T(4,128)S(1)} collective-permute-done((f32[3,2,8,128]{3,0,2,1:T(4,128)}, f32[3,2,8,128]{3,0,2,1:T(4,128)S(1)}, u32[]{:S(2)}, u32[]{:S(2)}) %collective-permute-start.5) | collective-permute-done | bytes 24608 | tf_op jit(solution)/shard_map/ppermute | solution.py:46
  36.5 0.1 pad_maximum_fusion.13
  36.6 1.9 %collective-permute-start.7 = (f32[3,12,2,128]{3,0,2,1:T(4,128)S(1)}, f32[3,12,2,128]{3,0,2,1:T(4,128)S(1)}, u32[]{:S(2)}, u32[]{:S(2)}) collective-permute-start(f32[3,12,2,128]{3,0,2,1:T(4,128)S(1)} %get-tuple-element.16), channel_id=1, source_target_pairs={{1,0},{2,1},{3,2},{4,3},{5,4},{6,5},{7,6},{9,8},{10,9},{11,10},{12... | collective-permute-start | bytes 110600 | tf_op jit(solution)/shard_map/ppermute | solution.py:46
  38.5 2.4 %collective-permute-start.6 = (f32[3,12,2,128]{3,0,2,1:T(4,128)S(1)}, f32[3,12,2,128]{3,0,2,1:T(4,128)S(1)}, u32[]{:S(2)}, u32[]{:S(2)}) collective-permute-start(f32[3,12,2,128]{3,0,2,1:T(4,128)S(1)} %get-tuple-element.15), channel_id=1, source_target_pairs={{0,1},{1,2},{2,3},{3,4},{4,5},{5,6},{6,7},{8,9},{9,10},{10,11},{11... | collective-permute-start | bytes 110600 | tf_op jit(solution)/shard_map/ppermute | solution.py:43
  40.9 4.3 %collective-permute-start.3 = (bf16[3,6,3,64,128]{4,3,2,1,0:T(8,128)(2,1)}, bf16[3,6,3,64,128]{4,3,2,1,0:T(8,128)(2,1)}, u32[]{:S(2)}, u32[]{:S(2)}) collective-permute-start(bf16[3,6,3,64,128]{4,3,2,1,0:T(8,128)(2,1)} %pad_maximum_fusion), channel_id=1, source_target_pairs={{0,8},{8,16},{16,24},{24,32},{32,40},{40,48},{48,56},{56,64},{64,7... | collective-permute-start | bytes 2654216 | tf_op jit(solution)/shard_map/ppermute | solution.py:464
  45.3 0.2 broadcast_select_fusion
  45.5 1.1 broadcast_select_fusion.1
  46.6 2.7 %stack.143.coef_ref = f32[12,12,8,128]{3,2,1,0:T(8,128)} concatenate(f32[12,12,1,128]{3,2,1,0:T(1,128)S(1)} %get-tuple-element.6, f32[12,12,1,128]{3,2,1,0:T(1,128)} %get-tuple-element.25, f32[12,12,1,128]{3,2,1,0:T(1,128)} %get-tuple-element.26, f32[12,12,1,128]{3,2,1,0:T(1,128)S(1)} %get-tuple-element.24, f32[12,12,1,128]{3,2,1,0:T(1,128)S(1)} %get-tuple-element.23, ...), dimensions={2} | concatenate | bytes 1179648 | tf_op jit(solution)/shard_map/stack | solution.py:62
  49.4 13.4 %own_gram.1.own_ref = f32[64,64]{1,0:T(8,128)} custom-call(bf16[10,10,3,64,128]{4,3,2,1,0:T(8,128)(2,1)} %bitcast.59, f32[12,12,8,128]{3,2,1,0:T(8,128)} %stack.143.coef_ref), custom_call_target="tpu_custom_call" | custom-call | flops 4000000000 | bytes 5000000 | tf_op jit(solution)/shard_map/own_gram/pallas_call | solution.py:470
  62.8 1.1 copy-done
  63.9 1.1 copy-done.1
  65.1 14.2 %row_gram.1.rows_ref = f32[64,128]{1,0:T(8,128)} custom-call(bf16[10,10,3,64,128]{4,3,2,1,0:T(8,128)(2,1)} %bitcast.60, bf16[10,3,3,64,128]{4,3,2,1,0:T(8,128)(2,1)} %copy-done, bf16[10,3,3,64,128]{4,3,2,1,0:T(8,128)(2,1)} %copy-done.1, f32[12,12,8,128]{3,2,1,0:T(8,128)} %stack.143.coef_ref), custom_call_target="tpu_custom_call" | custom-call | flops 2000000000 | bytes 5000000 | tf_op jit(solution)/shard_map/row_gram/pallas_call | solution.py:485
  79.3 11.9 %column_gram.1 = f32[64,512]{1,0:T(8,128)} custom-call(s32[1]{0:T(128)} %bitcast.odd_ref, bf16[10,10,3,64,128]{4,3,2,1,0:T(8,128)(2,1)} %bitcast.61, bf16[10,3,3,64,128]{4,3,2,1,0:T(8,128)(2,1)} %copy-done, bf16[10,3,3,64,128]{4,3,2,1,0:T(8,128)(2,1)} %copy-done.1, bf16[3,10,3,64,128]{4,3,2,1,0:T(8,128)(2,1)} %collective-permute-done.2.main_hbm, ...), custom_call_target="tpu_custom_call" | custom-call | flops 2000000000 | bytes 5000000 | tf_op jit(solution)/shard_map/column_gram/pallas_call | solution.py:501
  91.2 0.9 slice_bitcast_fusion
  92.1 3.7 %collective-permute-start.10 = (f32[32,512]{1,0:T(8,128)S(1)}, f32[32,512]{1,0:T(8,128)S(1)}, u32[]{:S(2)}, u32[]{:S(2)}) collective-permute-start(f32[32,512]{1,0:T(8,128)S(1)} %get-tuple-element.20), channel_id=1, source_target_pairs={{0,96},{8,104},{16,112},{24,120},{32,0},{40,8},{48,16},{56,24},{64... | collective-permute-start | bytes 196616 | tf_op jit(solution)/shard_map/ppermute | solution.py:419
  95.8 1.3 collective-permute-start.8
  97.1 0.6 collective-permute-done.10
  97.7 4.2 %collective-permute-done.9 = f32[32,512]{1,0:T(8,128)S(1)} collective-permute-done((f32[32,512]{1,0:T(8,128)S(1)}, f32[32,512]{1,0:T(8,128)S(1)}, u32[]{:S(2)}, u32[]{:S(2)}) %collective-permute-start.9) | collective-permute-done | bytes 65568 | tf_op jit(solution)/shard_map/ppermute | solution.py:419
  101.9 1.2 collective-permute-done.8
  103.1 0.1 collective-permute-start.11
  103.2 3.2 %collective-permute-start.16 = (f32[32,512]{1,0:T(8,128)S(1)}, f32[32,512]{1,0:T(8,128)S(1)}, u32[]{:S(2)}, u32[]{:S(2)}) collective-permute-start(f32[32,512]{1,0:T(8,128)S(1)} %get-tuple-element.19), channel_id=1, source_target_pairs={{0,24},{8,0},{16,8},{24,16},{32,56},{40,32},{48,40},{56,48},{64,88... | collective-permute-start | bytes 196616 | tf_op jit(solution)/shard_map/ppermute | solution.py:419
  106.4 1.3 collective-permute-start.15
  107.7 0.4 collective-permute-start.14
  108.1 1.8 %collective-permute-start.12 = (f32[4,32,512]{2,1,0:T(8,128)S(1)}, f32[4,32,512]{2,1,0:T(8,128)S(1)}, u32[]{:S(2)}, u32[]{:S(2)}) collective-permute-start(f32[4,32,512]{2,1,0:T(8,128)S(1)} %pad_maximum_fusion.1.refs_0_), channel_id=1, source_target_pairs={{0,16},{8,24},{16,0},{24,8},{32,48},{40,56},{48,32},{56,40},{64,80... | collective-permute-start | bytes 786440 | tf_op jit(solution)/shard_map/ppermute | solution.py:419
  109.9 2.6 %collective-permute-start.13 = (f32[4,32,512]{2,1,0:T(8,128)S(1)}, f32[4,32,512]{2,1,0:T(8,128)S(1)}, u32[]{:S(2)}, u32[]{:S(2)}) collective-permute-start(f32[4,32,512]{2,1,0:T(8,128)S(1)} %pad_maximum_fusion.1.refs_0_), channel_id=1, source_target_pairs={{0,24},{8,0},{16,8},{24,16},{32,56},{40,32},{48,40},{56,48},{64,88... | collective-permute-start | bytes 786440 | tf_op jit(solution)/shard_map/ppermute | solution.py:419
  112.6 0.9 collective-permute-done.15
  113.4 7.7 %collective-permute-done.14 = f32[32,512]{1,0:T(8,128)S(1)} collective-permute-done((f32[32,512]{1,0:T(8,128)S(1)}, f32[32,512]{1,0:T(8,128)S(1)}, u32[]{:S(2)}, u32[]{:S(2)}) %collective-permute-start.14) | collective-permute-done | bytes 65568 | tf_op jit(solution)/shard_map/ppermute | solution.py:419
  121.2 0.1 collective-permute-start.17
  121.3 2.3 %collective-permute-start.18 = (f32[4,32,512]{2,1,0:T(8,128)S(1)}, f32[4,32,512]{2,1,0:T(8,128)S(1)}, u32[]{:S(2)}, u32[]{:S(2)}) collective-permute-start(f32[4,32,512]{2,1,0:T(8,128)S(1)} %pad_maximum_fusion.2.refs_4_), channel_id=1, source_target_pairs={{0,64},{8,72},{16,80},{24,88},{32,96},{40,104},{48,112},{56,120},{... | collective-permute-start | bytes 786440 | tf_op jit(solution)/shard_map/ppermute | solution.py:419
  123.6 1.2 collective-permute-start.19
  124.8 0.7 stack.137.slot_ref
  125.6 10.0 %collective-permute-done.17.refs_5_ = f32[4,32,512]{2,1,0:T(8,128)S(1)} collective-permute-done((f32[4,32,512]{2,1,0:T(8,128)S(1)}, f32[4,32,512]{2,1,0:T(8,128)S(1)}, u32[]{:S(2)}, u32[]{:S(2)}) %collective-permute-start.17) | collective-permute-done | bytes 262176 | tf_op jit(solution)/shard_map/ppermute | solution.py:419
  135.6 0.6 collective-permute-done.19.refs_7_
  136.3 0.1 copy-done.10
  136.3 0.1 copy-done.11
  136.4 0.7 copy-done.12
  137.1 7.2 %assemble.1 = f32[16,64,576]{2,1,0:T(8,128)} custom-call(s32[1]{0:T(128)} %bitcast.odd_ref, s32[32]{0:T(128)} %stack.137.slot_ref, f32[4,32,512]{2,1,0:T(8,128)} %copy-done.2, f32[4,32,512]{2,1,0:T(8,128)} %copy-done.7, f32[4,32,512]{2,1,0:T(8,128)} %copy-done.8, f32[4,32,512]{2,1,0:T(8,128)} %copy-done.9, f32[4,32,512]{2,1,0:T(8,128)} %copy-done.3, ...), custom_call_target="tpu_custom_call" | custom-call | flops 1000000 | bytes 5000000 | tf_op jit(solution)/shard_map/assemble/pallas_call | solution.py:534
  (40 shorter events, 0.2 us)
Async XLA Ops:
  4.2 58.6 %collective-permute-start = (bf16[10,3,3,64,128]{4,3,2,1,0:T(8,128)(2,1)}, bf16[10,3,3,64,128]{4,3,2,1,0:T(8,128)(2,1)S(1)}, u32[]{:S(2)}, u32[]{:S(2)}) collective-permute-start(bf16[10,3,3,64,128]{4,3,2,1,0:T(8,128)(2,1)} %get-tuple-element.12), channel_id=1, source_target_pairs={{0,1},{1,2},{2,3},{3,4},{4,5},{5,6},{6,7},{8,9},{9,10},{10,11},{11... | collective-permute-start | bytes 4423688 | tf_op jit(solution)/shard_map/ppermute | solution.py:466
  6.1 56.7 %collective-permute-start.1 = (bf16[10,3,3,64,128]{4,3,2,1,0:T(8,128)(2,1)}, bf16[10,3,3,64,128]{4,3,2,1,0:T(8,128)(2,1)S(1)}, u32[]{:S(2)}, u32[]{:S(2)}) collective-permute-start(bf16[10,3,3,64,128]{4,3,2,1,0:T(8,128)(2,1)} %get-tuple-element.11), channel_id=1, source_target_pairs={{1,0},{2,1},{3,2},{4,3},{5,4},{6,5},{7,6},{9,8},{10,9},{11,10},{12... | collective-permute-start | bytes 4423688 | tf_op jit(solution)/shard_map/ppermute | solution.py:467
  9.8 5.9 %copy-start.4 = (f32[8,8,128]{2,1,0:T(8,128)S(1)}, f32[8,8,128]{2,1,0:T(8,128)}, u32[]{:S(2)}) copy-start(f32[8,8,128]{2,1,0:T(8,128)} %param.7) | copy-start | bytes 98308
  9.8 5.8 %copy-start.5 = (f32[8,8,128]{2,1,0:T(8,128)S(1)}, f32[8,8,128]{2,1,0:T(8,128)}, u32[]{:S(2)}) copy-start(f32[8,8,128]{2,1,0:T(8,128)} %param.6) | copy-start | bytes 98308
  9.8 5.8 %copy-start.6 = (f32[8,8,128]{2,1,0:T(8,128)S(1)}, f32[8,8,128]{2,1,0:T(8,128)}, u32[]{:S(2)}) copy-start(f32[8,8,128]{2,1,0:T(8,128)} %param.5) | copy-start | bytes 98308
  14.3 64.9 %collective-permute-start.2 = (bf16[3,10,3,64,128]{4,3,2,1,0:T(8,128)(2,1)}, bf16[3,10,3,64,128]{4,3,2,1,0:T(8,128)(2,1)}, u32[]{:S(2)}, u32[]{:S(2)}) collective-permute-start(bf16[3,10,3,64,128]{4,3,2,1,0:T(8,128)(2,1)} %get-tuple-element.10), channel_id=1, source_target_pairs={{8,0},{16,8},{24,16},{32,24},{40,32},{48,40},{56,48},{64,56},{72,6... | collective-permute-start | bytes 4423688 | tf_op jit(solution)/shard_map/ppermute | solution.py:461
  16.3 20.2 %collective-permute-start.5 = (f32[3,2,8,128]{3,0,2,1:T(4,128)}, f32[3,2,8,128]{3,0,2,1:T(4,128)S(1)}, u32[]{:S(2)}, u32[]{:S(2)}) collective-permute-start(f32[3,2,8,128]{3,0,2,1:T(4,128)} %get-tuple-element.22), channel_id=1, source_target_pairs={{8,0},{16,8},{24,16},{32,24},{40,32},{48,40},{56,48},{64,56},{72,6... | collective-permute-start | bytes 73736 | tf_op jit(solution)/shard_map/ppermute | solution.py:46
  17.6 18.9 %collective-permute-start.4 = (f32[3,2,8,128]{3,0,2,1:T(4,128)}, f32[3,2,8,128]{3,0,2,1:T(4,128)S(1)}, u32[]{:S(2)}, u32[]{:S(2)}) collective-permute-start(f32[3,2,8,128]{3,0,2,1:T(4,128)} %get-tuple-element.21), channel_id=1, source_target_pairs={{0,8},{8,16},{16,24},{24,32},{32,40},{40,48},{48,56},{56,64},{64,7... | collective-permute-start | bytes 73736 | tf_op jit(solution)/shard_map/ppermute | solution.py:43
  36.6 4.4 %collective-permute-start.7 = (f32[3,12,2,128]{3,0,2,1:T(4,128)S(1)}, f32[3,12,2,128]{3,0,2,1:T(4,128)S(1)}, u32[]{:S(2)}, u32[]{:S(2)}) collective-permute-start(f32[3,12,2,128]{3,0,2,1:T(4,128)S(1)} %get-tuple-element.16), channel_id=1, source_target_pairs={{1,0},{2,1},{3,2},{4,3},{5,4},{6,5},{7,6},{9,8},{10,9},{11,10},{12... | collective-permute-start | bytes 110600 | tf_op jit(solution)/shard_map/ppermute | solution.py:46
  38.5 6.8 %collective-permute-start.6 = (f32[3,12,2,128]{3,0,2,1:T(4,128)S(1)}, f32[3,12,2,128]{3,0,2,1:T(4,128)S(1)}, u32[]{:S(2)}, u32[]{:S(2)}) collective-permute-start(f32[3,12,2,128]{3,0,2,1:T(4,128)S(1)} %get-tuple-element.15), channel_id=1, source_target_pairs={{0,1},{1,2},{2,3},{3,4},{4,5},{5,6},{6,7},{8,9},{9,10},{10,11},{11... | collective-permute-start | bytes 110600 | tf_op jit(solution)/shard_map/ppermute | solution.py:43
  40.9 38.3 %collective-permute-start.3 = (bf16[3,6,3,64,128]{4,3,2,1,0:T(8,128)(2,1)}, bf16[3,6,3,64,128]{4,3,2,1,0:T(8,128)(2,1)}, u32[]{:S(2)}, u32[]{:S(2)}) collective-permute-start(bf16[3,6,3,64,128]{4,3,2,1,0:T(8,128)(2,1)} %pad_maximum_fusion), channel_id=1, source_target_pairs={{0,8},{8,16},{16,24},{24,32},{32,40},{40,48},{48,56},{56,64},{64,7... | collective-permute-start | bytes 2654216 | tf_op jit(solution)/shard_map/ppermute | solution.py:464
  62.8 1.1 copy-start
  63.9 1.1 copy-start.1
  92.1 5.6 %collective-permute-start.10 = (f32[32,512]{1,0:T(8,128)S(1)}, f32[32,512]{1,0:T(8,128)S(1)}, u32[]{:S(2)}, u32[]{:S(2)}) collective-permute-start(f32[32,512]{1,0:T(8,128)S(1)} %get-tuple-element.20), channel_id=1, source_target_pairs={{0,96},{8,104},{16,112},{24,120},{32,0},{40,8},{48,16},{56,24},{64... | collective-permute-start | bytes 196616 | tf_op jit(solution)/shard_map/ppermute | solution.py:419
  95.8 6.1 %collective-permute-start.9 = (f32[32,512]{1,0:T(8,128)S(1)}, f32[32,512]{1,0:T(8,128)S(1)}, u32[]{:S(2)}, u32[]{:S(2)}) collective-permute-start(f32[32,512]{1,0:T(8,128)S(1)} %get-tuple-element.20), channel_id=1, source_target_pairs={{0,64},{8,72},{16,80},{24,88},{32,96},{40,104},{48,112},{56,120},{... | collective-permute-start | bytes 196616 | tf_op jit(solution)/shard_map/ppermute | solution.py:419
  95.8 7.3 %collective-permute-start.8 = (f32[32,512]{1,0:T(8,128)S(1)}, f32[32,512]{1,0:T(8,128)S(1)}, u32[]{:S(2)}, u32[]{:S(2)}) collective-permute-start(f32[32,512]{1,0:T(8,128)S(1)} %get-tuple-element.20), channel_id=1, source_target_pairs={{0,32},{8,40},{16,48},{24,56},{32,64},{40,72},{48,80},{56,88},{64,... | collective-permute-start | bytes 196616 | tf_op jit(solution)/shard_map/ppermute | solution.py:419
  103.1 33.2 %copy-start.2 = (f32[4,32,512]{2,1,0:T(8,128)}, f32[4,32,512]{2,1,0:T(8,128)S(1)}, u32[]{:S(2)}) copy-start(f32[4,32,512]{2,1,0:T(8,128)S(1)} %pad_maximum_fusion.1.refs_0_) | copy-start | bytes 786436
  103.1 20.5 %collective-permute-start.11 = (f32[4,32,512]{2,1,0:T(8,128)S(1)}, f32[4,32,512]{2,1,0:T(8,128)S(1)}, u32[]{:S(2)}, u32[]{:S(2)}) collective-permute-start(f32[4,32,512]{2,1,0:T(8,128)S(1)} %pad_maximum_fusion.1.refs_0_), channel_id=1, source_target_pairs={{0,8},{8,16},{16,24},{24,0},{32,40},{40,48},{48,56},{56,32},{64,72... | collective-permute-start | bytes 786440 | tf_op jit(solution)/shard_map/ppermute | solution.py:419
  103.2 6.8 %collective-permute-start.16 = (f32[32,512]{1,0:T(8,128)S(1)}, f32[32,512]{1,0:T(8,128)S(1)}, u32[]{:S(2)}, u32[]{:S(2)}) collective-permute-start(f32[32,512]{1,0:T(8,128)S(1)} %get-tuple-element.19), channel_id=1, source_target_pairs={{0,24},{8,0},{16,8},{24,16},{32,56},{40,32},{48,40},{56,48},{64,88... | collective-permute-start | bytes 196616 | tf_op jit(solution)/shard_map/ppermute | solution.py:419
  106.4 7.0 %collective-permute-start.15 = (f32[32,512]{1,0:T(8,128)S(1)}, f32[32,512]{1,0:T(8,128)S(1)}, u32[]{:S(2)}, u32[]{:S(2)}) collective-permute-start(f32[32,512]{1,0:T(8,128)S(1)} %get-tuple-element.19), channel_id=1, source_target_pairs={{0,16},{8,24},{16,0},{24,8},{32,48},{40,56},{48,32},{56,40},{64,80... | collective-permute-start | bytes 196616 | tf_op jit(solution)/shard_map/ppermute | solution.py:419
  107.7 13.5 %collective-permute-start.14 = (f32[32,512]{1,0:T(8,128)S(1)}, f32[32,512]{1,0:T(8,128)S(1)}, u32[]{:S(2)}, u32[]{:S(2)}) collective-permute-start(f32[32,512]{1,0:T(8,128)S(1)} %get-tuple-element.19), channel_id=1, source_target_pairs={{0,8},{8,16},{16,24},{24,0},{32,40},{40,48},{48,56},{56,32},{64,72... | collective-permute-start | bytes 196616 | tf_op jit(solution)/shard_map/ppermute | solution.py:419
  108.1 17.4 %collective-permute-start.12 = (f32[4,32,512]{2,1,0:T(8,128)S(1)}, f32[4,32,512]{2,1,0:T(8,128)S(1)}, u32[]{:S(2)}, u32[]{:S(2)}) collective-permute-start(f32[4,32,512]{2,1,0:T(8,128)S(1)} %pad_maximum_fusion.1.refs_0_), channel_id=1, source_target_pairs={{0,16},{8,24},{16,0},{24,8},{32,48},{40,56},{48,32},{56,40},{64,80... | collective-permute-start | bytes 786440 | tf_op jit(solution)/shard_map/ppermute | solution.py:419
  109.9 15.6 %collective-permute-start.13 = (f32[4,32,512]{2,1,0:T(8,128)S(1)}, f32[4,32,512]{2,1,0:T(8,128)S(1)}, u32[]{:S(2)}, u32[]{:S(2)}) collective-permute-start(f32[4,32,512]{2,1,0:T(8,128)S(1)} %pad_maximum_fusion.1.refs_0_), channel_id=1, source_target_pairs={{0,24},{8,0},{16,8},{24,16},{32,56},{40,32},{48,40},{56,48},{64,88... | collective-permute-start | bytes 786440 | tf_op jit(solution)/shard_map/ppermute | solution.py:419
  121.2 15.1 %copy-start.3 = (f32[4,32,512]{2,1,0:T(8,128)}, f32[4,32,512]{2,1,0:T(8,128)S(1)}, u32[]{:S(2)}) copy-start(f32[4,32,512]{2,1,0:T(8,128)S(1)} %pad_maximum_fusion.2.refs_4_) | copy-start | bytes 786436
  121.2 14.4 %collective-permute-start.17 = (f32[4,32,512]{2,1,0:T(8,128)S(1)}, f32[4,32,512]{2,1,0:T(8,128)S(1)}, u32[]{:S(2)}, u32[]{:S(2)}) collective-permute-start(f32[4,32,512]{2,1,0:T(8,128)S(1)} %pad_maximum_fusion.2.refs_4_), channel_id=1, source_target_pairs={{0,32},{8,40},{16,48},{24,56},{32,64},{40,72},{48,80},{56,88},{64,... | collective-permute-start | bytes 786440 | tf_op jit(solution)/shard_map/ppermute | solution.py:419
  121.3 14.3 %collective-permute-start.18 = (f32[4,32,512]{2,1,0:T(8,128)S(1)}, f32[4,32,512]{2,1,0:T(8,128)S(1)}, u32[]{:S(2)}, u32[]{:S(2)}) collective-permute-start(f32[4,32,512]{2,1,0:T(8,128)S(1)} %pad_maximum_fusion.2.refs_4_), channel_id=1, source_target_pairs={{0,64},{8,72},{16,80},{24,88},{32,96},{40,104},{48,112},{56,120},{... | collective-permute-start | bytes 786440 | tf_op jit(solution)/shard_map/ppermute | solution.py:419
  123.6 12.7 %copy-start.7 = (f32[4,32,512]{2,1,0:T(8,128)}, f32[4,32,512]{2,1,0:T(8,128)S(1)}, u32[]{:S(2)}) copy-start(f32[4,32,512]{2,1,0:T(8,128)S(1)} %collective-permute-done.11.refs_1_) | copy-start | bytes 786436
  123.6 12.7 %collective-permute-start.19 = (f32[4,32,512]{2,1,0:T(8,128)S(1)}, f32[4,32,512]{2,1,0:T(8,128)S(1)}, u32[]{:S(2)}, u32[]{:S(2)}) collective-permute-start(f32[4,32,512]{2,1,0:T(8,128)S(1)} %pad_maximum_fusion.2.refs_4_), channel_id=1, source_target_pairs={{0,96},{8,104},{16,112},{24,120},{32,0},{40,8},{48,16},{56,24},{64... | collective-permute-start | bytes 786440 | tf_op jit(solution)/shard_map/ppermute | solution.py:419
  125.5 10.7 %copy-start.8 = (f32[4,32,512]{2,1,0:T(8,128)}, f32[4,32,512]{2,1,0:T(8,128)S(1)}, u32[]{:S(2)}) copy-start(f32[4,32,512]{2,1,0:T(8,128)S(1)} %collective-permute-done.12.refs_2_) | copy-start | bytes 786436
  125.5 10.7 %copy-start.9 = (f32[4,32,512]{2,1,0:T(8,128)}, f32[4,32,512]{2,1,0:T(8,128)S(1)}, u32[]{:S(2)}) copy-start(f32[4,32,512]{2,1,0:T(8,128)S(1)} %collective-permute-done.13.refs_3_) | copy-start | bytes 786436
  135.6 0.7 copy-start.10
  135.6 0.8 copy-start.11
  136.4 0.7 copy-start.12

commit v2 on v0

v2 whole, which is shorter than its diff:
```python
import functools

import jax
import jax.numpy as jnp
from jax import lax
from jax.experimental import pallas as pl
from jax.experimental.pallas import tpu as pltpu
from jax.sharding import PartitionSpec as P

F32 = jnp.float32
BF16 = jnp.bfloat16
MID, LOW, UPP, DIA, VOL, OUT = range(6)
NT = (((1,), (1,)), ((), ()))
MIB = 1024 * 1024


def cover(start, length, cell, count, margin):
    places = start + jnp.arange(length, dtype=jnp.int32)
    base = jnp.floor_divide(places, cell)
    total = jnp.zeros((length,), jnp.int32)
    for step_off in (-1, 0, 1):
        owner = base + step_off
        inside = (
            (owner >= 0)
            & (owner < count)
            & (places >= owner * cell - margin)
            & (places < owner * cell + cell + margin)
        )
        total = total + inside.astype(jnp.int32)
    in_grid = (places >= 0) & (places < cell * count)
    safe = jnp.maximum(total, 1).astype(F32)
    return jnp.where(in_grid & (total > 0), 1.0 / safe, 0.0)


def neighbours(count):
    up = [(i, i + 1) for i in range(count - 1)]
    return up, [(b, a) for a, b in up]


def spread3(w):
    return [w[0], w[0] + w[0] + w[1], w[0] + w[1] + w[1] + w[2]]


def put_image(img_ref, slot, pos, chunk, image):
    for a in range(3):
        high = image[a].astype(BF16)
        low = (image[a] - high.astype(F32)).astype(BF16)
        lanes = pl.ds((pos * 3 + a) * 128, 128)
        img_ref[slot, pl.ds(chunk * 16, 16), lanes] = high
        img_ref[slot, pl.ds(64 + chunk * 16, 16), lanes] = low


def cell_image(lines, values, rows):
    if values is None:
        return [-(rows[2] * lines[a]) for a in range(3)]
    total = rows[1] * (values[0] + values[1] + values[2])
    return [rows[0] * values[a] + total - rows[2] * lines[a] for a in range(3)]


def coef_rows(coef_ref, x, y, names):
    return [coef_ref[x, n, pl.ds(y, 1), :] for n in names]


def depth_sum(raw, rows):
    return (
        raw.astype(F32) * rows[0]
        + pltpu.roll(raw, 1, 1).astype(F32) * rows[1]
        + pltpu.roll(raw, 127, 1).astype(F32) * rows[2]
    )


def side(blocks):
    return jnp.concatenate(blocks, axis=1)


def fold(total):
    return total[:, :64] + total[:, 64:]


def fold_rows(total):
    return total[:64] + total[64:]


def pack_kernel(odd_ref, m_hbm, main_ref, corner_ref, south_ref, north_ref, sems):
    ext = m_hbm.shape[0]
    odd = odd_ref[0]
    here = jnp.where(odd == 1, ext - 3, 0)
    there = jnp.where(odd == 1, 0, ext - 3)
    copies = [
        pltpu.make_async_copy(m_hbm.at[pl.ds(here, 3)], main_ref, sems.at[0]),
        pltpu.make_async_copy(
            m_hbm.at[pl.ds(there, 3), pl.ds(0, 3)], corner_ref.at[:, pl.ds(0, 3)], sems.at[1]
        ),
        pltpu.make_async_copy(
            m_hbm.at[pl.ds(there, 3), pl.ds(ext - 3, 3)], corner_ref.at[:, pl.ds(3, 3)], sems.at[2]
        ),
        pltpu.make_async_copy(m_hbm.at[:, pl.ds(ext - 3, 3)], south_ref, sems.at[3]),
        pltpu.make_async_copy(m_hbm.at[:, pl.ds(0, 3)], north_ref, sems.at[4]),
    ]
    for copy in copies:
        copy.start()
    for copy in copies:
        copy.wait()


def gate_kernel(*refs):
    pass


def own_kernel(
    odd_ref, sx_ref, sy_ref, m_hbm, mid_ref, lo_ref, hi_ref,
    out_ref, coef_ref, simg_hbm, nimg_hbm, ximg_hbm,
    m_ref, q_ref, img_ref, acc_ref, sems, strip_sems,
):
    ext = m_hbm.shape[0]
    frame = ext + 2
    odd = odd_ref[0]

    def load(x):
        return pltpu.make_async_copy(m_hbm.at[x], m_ref.at[x + 1], sems.at[x])

    for x in range(ext):
        load(x).start()
    none = jnp.zeros(m_ref.shape[1:], BF16)
    for edge in (0, ext + 1, ext + 2):
        m_ref[edge] = none
    zero = jnp.zeros(q_ref.shape[1:], F32)
    q_ref[0] = zero
    q_ref[1] = zero
    acc_ref[...] = jnp.zeros_like(acc_ref)

    lane = lax.broadcasted_iota(jnp.int32, (frame, 128), 1)
    place = lax.broadcasted_iota(jnp.int32, (frame, 128), 0)
    share_y = jnp.zeros((frame, 128), F32)
    for g in range(frame):
        share_y = jnp.where(place == g, sy_ref[g], share_y)

    def coefs(f, _):
        share = share_y * sx_ref[f]
        cen, cpl, vol = [
            jnp.concatenate([lo_ref[f, n], mid_ref[f, n], hi_ref[f, n]], axis=0) for n in range(3)
        ]
        kap = cpl * share
        vol = vol * share * share
        coef_ref[f, MID] = kap + kap
        coef_ref[f, LOW] = jnp.where(lane == 0, 0.0, pltpu.roll(kap, 1, 1))
        coef_ref[f, UPP] = jnp.where(lane == 127, 0.0, pltpu.roll(kap, 127, 1))
        coef_ref[f, DIA] = cen * share * share - vol + 0.5 * kap * kap
        coef_ref[f, VOL] = vol
        coef_ref[f, OUT] = kap * (1.0 / 16.0)
        return 0

    lax.fori_loop(0, frame, coefs, 0)

    def strips(f):
        return [
            pltpu.make_async_copy(
                img_ref.at[f, :, pl.ds(0, 1152)], simg_hbm.at[f - 1], strip_sems.at[0, f - 1]
            ),
            pltpu.make_async_copy(
                img_ref.at[f, :, pl.ds((frame - 3) * 384, 1152)], nimg_hbm.at[f - 1], strip_sems.at[1, f - 1]
            ),
        ]

    first_x = jnp.where(odd == 1, 0, frame - 3)

    def strip_x(f):
        return pltpu.make_async_copy(
            img_ref.at[f, :, pl.ds(384, ext * 384)], ximg_hbm.at[f - first_x], strip_sems.at[2, f - first_x]
        )

    def line(f, last, edge):
        if not last:
            kaps = [coef_rows(coef_ref, f + 1, g, (MID, LOW, UPP)) for g in range(1, ext + 1)]
            for a in range(3):
                for chunk in range(4):
                    rows = pl.ds(chunk * 16, 16)
                    pair = None
                    before = None
                    for j in range(ext):
                        w = depth_sum(m_ref[f + 1, j, a, rows, :], kaps[j])
                        if j == 0:
                            q_ref[f + 2, 0, a, rows, :] = w
                            pair = w
                        else:
                            now = before + w
                            q_ref[f + 2, j, a, rows, :] = now + pair
                            pair = now
                        before = w
                    q_ref[f + 2, ext, a, rows, :] = pair + before
                    q_ref[f + 2, ext + 1, a, rows, :] = before
        total = acc_ref[...]
        for g in range(frame):
            rows_of = coef_rows(coef_ref, f, g, (DIA, VOL, OUT))
            for chunk in range(4):
                rows = pl.ds(chunk * 16, 16)
                values = None
                if 1 <= g <= ext and not edge:
                    values = [m_ref[f, g - 1, a, rows, :].astype(F32) for a in range(3)]
                lines = []
                for a in range(3):
                    mid = q_ref[f + 1, g, a, rows, :]
                    if last:
                        lines.append(q_ref[f, g, a, rows, :])
                    else:
                        lines.append(
                            (q_ref[f, g, a, rows, :] + mid) + (mid + q_ref[f + 2, g, a, rows, :])
                        )
                put_image(img_ref, f, g, chunk, cell_image(lines, values, rows_of))
            if g % 2 == 0 and 1 < g <= ext and not edge:
                left = side([m_ref[f, i, a] for i in (g - 2, g - 1) for a in range(3)])
                total = total + lax.dot_general(
                    left, img_ref[f, :, pl.ds((g - 1) * 384, 768)], NT, preferred_element_type=F32
                )
        acc_ref[...] = total

        @pl.when((f >= first_x) & (f < first_x + 3))
        def _():
            strip_x(f).start()

        if not edge:
            for copy in strips(f):
                copy.start()

    load(0).wait()
    line(0, False, True)

    def body(f, _):
        @pl.when(f < ext)
        def _():
            load(f).wait()

        line(f, False, False)
        return 0

    lax.fori_loop(1, ext + 1, body, 0)
    line(ext + 1, True, True)
    out_ref[...] = fold(acc_ref[...])
    for f in range(1, ext + 1):
        for copy in strips(f):
            copy.wait()
    for i in range(3):
        strip_x(first_x + i).wait()


def rows_kernel(
    south_ref, north_ref, simg_hbm, nimg_hbm, coef_ref, out_ref, cimg_ref,
    img_ref, z_ref, acc_ref, sems,
):
    ext = south_ref.shape[0]
    raw_refs = (south_ref, north_ref)
    images = [
        pltpu.make_async_copy(ref, img_ref.at[s], sems.at[s])
        for s, ref in enumerate((simg_hbm, nimg_hbm))
    ]
    for copy in images:
        copy.start()
    acc_ref[...] = jnp.zeros_like(acc_ref)
    for s in range(2):
        r_ref = raw_refs[s]
        raw_y = (2, 1, 0) if s == 0 else (0, 1, 2)
        raw_g = (2, 1, 0) if s == 0 else (9, 10, 11)
        img_g = (3, 2, 1) if s == 0 else (8, 9, 10)
        img_y = (2, 1, 0) if s == 0 else (0, 1, 2)
        for t in range(2):
            raw_x = (0, 1, 2) if t == 0 else (9, 8, 7)
            raw_f = (1, 2, 3) if t == 0 else (10, 9, 8)
            img_f = (0, 1, 2) if t == 0 else (11, 10, 9)
            img_x = (0, 1, 2) if t == 0 else (2, 1, 0)

            def chunked(chunk, _, s=s, t=t, r_ref=r_ref, raw_x=raw_x, raw_f=raw_f, img_f=img_f, img_x=img_x):
                rows = pl.ds(pl.multiple_of(chunk * 16, 16), 16)
                low_rows = pl.ds(pl.multiple_of(64 + chunk * 16, 16), 16)
                for a in range(3):
                    across = []
                    for c in range(3):
                        w = [
                            depth_sum(
                                r_ref[raw_x[c], raw_y[d], a, rows, :],
                                coef_rows(coef_ref, raw_f[c], raw_g[d], (MID, LOW, UPP)),
                            )
                            for d in range(3)
                        ]
                        across.append(spread3(w))
                    for e in range(3):
                        for c, value in enumerate(spread3([across[i][e] for i in range(3)])):
                            z_ref[c, e, a] = value
                for c in range(3):
                    for e in range(3):
                        values = None
                        if c > 0 and e > 0:
                            values = [
                                r_ref[raw_x[c - 1], raw_y[e - 1], a, rows, :].astype(F32)
                                for a in range(3)
                            ]
                        image = cell_image(
                            [z_ref[c, e, a] for a in range(3)], values,
                            coef_rows(coef_ref, img_f[c], img_g[e], (DIA, VOL, OUT)),
                        )
                        for a in range(3):
                            high = image[a].astype(BF16)
                            low = (image[a] - high.astype(F32)).astype(BF16)
                            lanes = pl.ds(((img_x[c] * 3 + img_y[e]) * 3 + a) * 128, 128)
                            cimg_ref[t, s, rows, lanes] = high
                            cimg_ref[t, s, low_rows, lanes] = low
                return 0

            lax.fori_loop(0, 4, chunked, 0)
    for s in range(2):
        images[s].wait()

        def dots(x, _, s=s):
            right = side([raw_refs[s][x, j, a] for j in range(3) for a in range(3)])
            acc_ref[s] += lax.dot_general(img_ref[s, x], right, NT, preferred_element_type=F32)
            return 0

        lax.fori_loop(0, ext, dots, 0)
    out_ref[...] = side([fold_rows(acc_ref[0]), fold_rows(acc_ref[1])])


def corner_dot(raw, img):
    left = side([raw(i, j, a) for i in range(3) for j in range(3) for a in range(3)])
    return fold(lax.dot_general(left, img, NT, preferred_element_type=F32))


def other_kernel(odd_ref, corner_ref, cimg_ref, own_ref, rows_ref, out_ref, keep_ref):
    t = odd_ref[0]
    south = corner_dot(lambda i, j, a: corner_ref[i, j, a], cimg_ref[t, 0])
    north = corner_dot(lambda i, j, a: corner_ref[i, j + 3, a], cimg_ref[t, 1])
    around = rows_ref[...]
    out_ref[...] = side([own_ref[...], around[:, 64:], south, around[:, :64]])
    keep_ref[...] = north


def main_kernel(odd_ref, main_ref, ximg_ref, cimg_ref, keep_ref, out_ref):
    t = 1 - odd_ref[0]
    ext = main_ref.shape[1]
    total = None
    for i in range(3):
        right = side([main_ref[i, j, a] for j in range(ext) for a in range(3)])
        part = lax.dot_general(ximg_ref[i], right, NT, preferred_element_type=F32)
        total = part if total is None else total + part
    south = corner_dot(lambda i, j, a: main_ref[i, j, a], cimg_ref[t, 0])
    north = corner_dot(lambda i, j, a: main_ref[i, ext - 3 + j, a], cimg_ref[t, 1])
    out_ref[...] = side([south, fold_rows(total), north, keep_ref[...]])


def final_kernel(odd_ref, slot_ref, *refs):
    *pieces, out_hbm, e_ref, l_ref, o_ref, sems, out_sems = refs
    copies = []
    for h, ref in enumerate((e_ref, l_ref)):
        for i in range(4):
            for j in range(4):
                at = h * 16 + i * 4 + j
                copies.append(
                    pltpu.make_async_copy(
                        pieces[h * 4 + i].at[j], ref.at[slot_ref[at] + 1], sems.at[at]
                    )
                )
    for copy in copies:
        copy.start()
    odd = odd_ref[0]
    none = jnp.zeros(e_ref.shape[1:], F32)
    for ref in (e_ref, l_ref):
        ref[0] = none
        ref[17] = none
    for copy in copies:
        copy.wait()

    def put(p):
        return pltpu.make_async_copy(o_ref.at[p], out_hbm.at[p], out_sems.at[p])

    low = lax.broadcasted_iota(jnp.int32, (64, 128), 1) < 64

    def turned(tile):
        return jnp.transpose(jnp.concatenate([tile, tile], axis=0))[64:]

    def join(lower, upper):
        return jnp.where(low, lower, upper)

    def tiles(ref, p):
        return ref[p, :, pl.ds(0, 128)], ref[p, :, pl.ds(128, 128)]

    def even(p, _):
        (e_one, e_two), (_, e_after) = tiles(e_ref, p + 1), tiles(e_ref, p + 2)
        (b_one, b_two), (l_one, _), (_, l_after) = [tiles(l_ref, p + i) for i in range(3)]
        o_ref[p, :, pl.ds(0, 512)] = side(
            [join(b_one, turned(b_one)), join(b_two, e_two), e_one, join(e_after, l_one)]
        )
        o_ref[p, :, pl.ds(512, 64)] = l_after[:, 64:]
        put(p).start()
        return 0

    def uneven(p, _):
        (_, e_before), (e_one, e_two) = tiles(e_ref, p), tiles(e_ref, p + 1)
        (_, b_two), (l_one, _), (a_one, a_two) = [tiles(l_ref, p + i) for i in range(3)]
        o_ref[p, :, pl.ds(0, 512)] = side(
            [
                join(e_before, l_one), join(pltpu.roll(b_two, 64, 1), e_two), e_one,
                join(a_one, turned(a_one)),
            ]
        )
        o_ref[p, :, pl.ds(512, 64)] = a_two[:, :64]
        put(p).start()
        return 0

    @pl.when(odd == 0)
    def _():
        lax.fori_loop(0, 16, even, 0)

    @pl.when(odd == 1)
    def _():
        lax.fori_loop(0, 16, uneven, 0)

    for p in range(16):
        put(p).wait()


def any_spec():
    return pl.BlockSpec(memory_space=pl.ANY)


def vmem_spec():
    return pl.BlockSpec(memory_space=pltpu.VMEM)


def smem_spec():
    return pl.BlockSpec(memory_space=pltpu.SMEM)


def shape(*dims, dtype=F32):
    return jax.ShapeDtypeStruct(dims, dtype)


def call(kernel, out_shape, in_specs, out_specs, scratch, mib, name):
    return pl.pallas_call(
        kernel,
        out_shape=out_shape,
        in_specs=in_specs,
        out_specs=out_specs,
        scratch_shapes=scratch,
        compiler_params=pltpu.CompilerParams(vmem_limit_bytes=mib * MIB),
        cost_estimate=pl.CostEstimate(flops=1000, bytes_accessed=1000, transcendentals=0),
        name=name,
    )


def along(nz, nx, dz, dx):
    return [
        (z * nx + x, (z + dz) % nz * nx + (x + dx) % nx) for z in range(nz) for x in range(nx)
    ]


def ring(value, steps):
    return [value] + [lax.ppermute(value, "sx", pairs) for pairs in steps]


def neighbours(count):
    up = [(i, i + 1) for i in range(count - 1)]
    return up, [(b, a) for a, b in up]


def coef_frame(centre, coupling, volume):
    own = jnp.stack([centre, coupling, volume], axis=1)
    up, down = neighbours(lax.axis_size("sx"))
    low = lax.ppermute(own[-2:], "sx", up)
    high = lax.ppermute(own[:2], "sx", down)
    mid = jnp.concatenate([low, own, high], axis=0)
    up, down = neighbours(lax.axis_size("sy"))
    lo = lax.ppermute(mid[:, :, -2:], "sy", up)
    hi = lax.ppermute(mid[:, :, :2], "sy", down)
    return mid, lo, hi


def local(modes, centre, coupling, volume):
    ext = modes.shape[0]
    cell = centre.shape[0]
    margin = (ext - cell) // 2
    nx = lax.axis_size("sx")
    ny = lax.axis_size("sy")
    ix = lax.axis_index("sx")
    iy = lax.axis_index("sy")
    odd = lax.rem(iy, 2).astype(jnp.int32).reshape(1)
    share_x = cover(ix * cell - margin - 1, ext + 2, cell, nx, margin)
    share_y = cover(iy * cell - margin - 1, ext + 2, cell, ny, margin)
    mid, lo, hi = coef_frame(centre, coupling, volume)
    m = jnp.transpose(modes, (0, 1, 3, 2, 4))
    frame = ext + 2

    main, corner, south, north = call(
        pack_kernel,
        [
            shape(3, ext, 3, 64, 128, dtype=BF16),
            shape(3, 6, 3, 64, 128, dtype=BF16),
            shape(ext, 3, 3, 64, 128, dtype=BF16),
            shape(ext, 3, 3, 64, 128, dtype=BF16),
        ],
        [smem_spec(), any_spec()],
        [vmem_spec()] * 4,
        [pltpu.SemaphoreType.DMA((5,))],
        8,
        "pack",
    )(odd, m)
    packed = (main, corner, south, north)
    main, corner, south, north = pl.pallas_call(
        gate_kernel,
        out_shape=[shape(*x.shape, dtype=x.dtype) for x in packed],
        in_specs=[any_spec()] * 6,
        out_specs=[any_spec()] * 4,
        input_output_aliases={i: i for i in range(4)},
        compiler_params=pltpu.CompilerParams(vmem_limit_bytes=MIB),
        name="gate",
    )(*packed, lo, hi)
    main_pairs, other_pairs = [], []
    for y in range(ny):
        for x in range(nx - 1):
            lower, higher = x * ny + y, (x + 1) * ny + y
            main_pairs.append((higher, lower) if y % 2 == 0 else (lower, higher))
            other_pairs.append((lower, higher) if y % 2 == 0 else (higher, lower))
    main = lax.ppermute(main, ("sx", "sy"), main_pairs)
    corner = lax.ppermute(corner, ("sx", "sy"), other_pairs)
    up, down = neighbours(ny)
    south = lax.ppermute(south, "sy", up)
    north = lax.ppermute(north, "sy", down)

    own, coef, simg, nimg, ximg = call(
        own_kernel,
        [
            shape(64, 64),
            shape(frame, 6, frame, 128),
            shape(ext, 128, 1152, dtype=BF16),
            shape(ext, 128, 1152, dtype=BF16),
            shape(3, 128, ext * 384, dtype=BF16),
        ],
        [smem_spec()] * 3 + [any_spec()] + [vmem_spec()] * 3,
        [vmem_spec(), vmem_spec(), any_spec(), any_spec(), any_spec()],
        [
            pltpu.VMEM((ext + 3, ext, 3, 64, 128), BF16),
            pltpu.VMEM((ext + 3, frame, 3, 64, 128), F32),
            pltpu.VMEM((frame, 128, frame * 384), BF16),
            pltpu.VMEM((64, 128), F32),
            pltpu.SemaphoreType.DMA((ext,)),
            pltpu.SemaphoreType.DMA((3, ext)),
        ],
        44,
        "own_gram",
    )(odd, share_x, share_y, m, mid, lo, hi)
    around, cimg = call(
        rows_kernel,
        [shape(64, 128), shape(2, 2, 128, 3456, dtype=BF16)],
        [vmem_spec()] * 2 + [any_spec()] * 2 + [vmem_spec()],
        [vmem_spec(), vmem_spec()],
        [
            pltpu.VMEM((2, ext, 128, 1152), BF16),
            pltpu.VMEM((3, 3, 3, 16, 128), F32),
            pltpu.VMEM((2, 128, 64), F32),
            pltpu.SemaphoreType.DMA((2,)),
        ],
        18,
        "row_gram",
    )(south, north, simg, nimg, coef)
    early, keep = call(
        other_kernel,
        [shape(64, 256), shape(64, 64)],
        [smem_spec()] + [vmem_spec()] * 4,
        [vmem_spec()] * 2,
        [],
        10,
        "corner_gram",
    )(odd, corner, cimg, own, around)
    late = call(
        main_kernel,
        shape(64, 256),
        [smem_spec()] + [vmem_spec()] * 4,
        vmem_spec(),
        [],
        12,
        "column_gram",
    )(odd, main, ximg, cimg, keep)

    nz, nw = 4, nx // 4
    z_steps = [along(nz, nw, k, 0) for k in (1, 2, 3)]
    x_steps = [along(nz, nw, 0, k) for k in (1, 2, 3)]
    early = ring(jnp.stack(ring(early, z_steps)), x_steps)
    late = ring(jnp.stack(ring(late, x_steps)), z_steps)
    iz, iw = ix // nw, lax.rem(ix, nw)
    slots = []
    for i in range(4):
        for j in range(4):
            slots.append(lax.rem(iz - j + nz, nz) * nw + lax.rem(iw - i + nw, nw))
    for i in range(4):
        for j in range(4):
            slots.append(lax.rem(iz - i + nz, nz) * nw + lax.rem(iw - j + nw, nw))
    slot = jnp.stack(slots).astype(jnp.int32)
    pieces = early + late
    out = call(
        final_kernel,
        shape(nx, 64, 576),
        [smem_spec(), smem_spec()] + [any_spec()] * len(pieces),
        any_spec(),
        [
            pltpu.VMEM((nx + 2, 64, 256), F32),
            pltpu.VMEM((nx + 2, 64, 256), F32),
            pltpu.VMEM((nx, 64, 576), F32),
            pltpu.SemaphoreType.DMA((32,)),
            pltpu.SemaphoreType.DMA((nx,)),
        ],
        8,
        "assemble",
    )(odd, slot, *pieces)
    return out[None]


def solution(mesh):
    in_specs = (
        P("sx", "sy", None, None, None),
        P("sx", "sy", None),
        P("sx", "sy", None),
        P("sx", "sy", None),
    )
    out_specs = P("sy", None, None, None)
    return jax.shard_map(local, mesh=mesh, in_specs=in_specs, out_specs=out_specs, check_vma=False)
```

time: 452 us -> 111 us (0.25)
  the two profiles are of different devices: /device:TPU:24 before, /device:TPU:1 now
where the time goes in v2:
time: 111 us; the launch traced here: 110 us
  Pallas kernels  39.6 us (36%)
  starting transfers between devices  37.4 us (34%)
  waiting for transfers between devices  28.8 us (26%)
  local copies, waits for them, and re-layouts  2.52 us (2%)
  other arithmetic  1.65 us (1%)
    ppermute x12, waiting for transfers between devices, ring(): return [value] + [lax.ppermute(value, 'sx', pairs) for pairs in steps]  25.5 us
    pallas_call x1, Pallas kernels, local(): call(own_kernel, [shape(64, 64), shape(frame, 6, frame, 128), shape(ext,...  16.4 us
    ppermute x12, starting transfers between devices, ring(): return [value] + [lax.ppermute(value, 'sx', pairs) for pairs in steps]  15.1 us
    pallas_call x1, Pallas kernels, local(): call(rows_kernel, [shape(64, 128), shape(2, 2, 128, 3456, dtype=BF16)], [...  8.43 us
    pallas_call x1, Pallas kernels, local(): call(final_kernel, shape(nx, 64, 576), [smem_spec(), smem_spec()] + [any_...  6.74 us
    ppermute x1, starting transfers between devices, local(): main = lax.ppermute(main, ('sx', 'sy'), main_pairs)  4.25 us
    ppermute x1, starting transfers between devices, coef_frame(): hi = lax.ppermute(mid[:, :, :2], 'sy', down)  4.01 us
    ppermute x1, starting transfers between devices, coef_frame(): low = lax.ppermute(own[-2:], 'sx', up)  3.93 us
  transfers between devices with their start and end apart: 20, of which 9 were waited for; matrix products, arithmetic and copies ran while one was open for 0% of the time, Pallas kernels for 30%

profile of v2, /device:TPU:1, one launch (start us, length us, event | category | flops | bytes accessed | tf_op | source)
XLA Modules:
  0.0 110.1 jit_solution(6409321598420838356)
XLA Ops:
  0.0 0.8 pad_maximum_fusion.5
  0.8 3.9 %collective-permute-start = (f32[2,3,8,128]{3,2,1,0:T(8,128)S(1)}, f32[2,3,8,128]{3,2,1,0:T(8,128)S(1)}, u32[]{:S(2)}, u32[]{:S(2)}) collective-permute-start(f32[2,3,8,128]{3,2,1,0:T(8,128)S(1)} %get-tuple-element.41), channel_id=1, source_target_pairs={{0,8},{8,16},{16,24},{24,32},{32,40},{40,48},{48,56},{56,64},{64,7... | collective-permute-start | bytes 73736 | tf_op jit(solution)/shard_map/ppermute | solution.py:466
  4.7 1.3 %collective-permute-start.1 = (f32[2,3,8,128]{3,2,1,0:T(8,128)S(1)}, f32[2,3,8,128]{3,2,1,0:T(8,128)S(1)}, u32[]{:S(2)}, u32[]{:S(2)}) collective-permute-start(f32[2,3,8,128]{3,2,1,0:T(8,128)S(1)} %get-tuple-element.42), channel_id=1, source_target_pairs={{8,0},{16,8},{24,16},{32,24},{40,32},{48,40},{56,48},{64,56},{72,6... | collective-permute-start | bytes 73736 | tf_op jit(solution)/shard_map/ppermute | solution.py:467
  6.0 0.0 collective-permute-done
  6.0 3.3 %collective-permute-done.1 = f32[2,3,8,128]{3,2,1,0:T(8,128)S(1)} collective-permute-done((f32[2,3,8,128]{3,2,1,0:T(8,128)S(1)}, f32[2,3,8,128]{3,2,1,0:T(8,128)S(1)}, u32[]{:S(2)}, u32[]{:S(2)}) %collective-permute-start.1) | collective-permute-done | bytes 24608 | tf_op jit(solution)/shard_map/ppermute | solution.py:467
  9.3 0.8 pad_maximum_fusion.2.mid_ref
  10.1 4.0 %collective-permute-start.3 = (f32[12,3,2,128]{3,2,1,0:T(2,128)S(1)}, f32[12,3,2,128]{3,2,1,0:T(2,128)S(1)}, u32[]{:S(2)}, u32[]{:S(2)}) collective-permute-start(f32[12,3,2,128]{3,2,1,0:T(2,128)S(1)} %get-tuple-element.39), channel_id=1, source_target_pairs={{1,0},{2,1},{3,2},{4,3},{5,4},{6,5},{7,6},{9,8},{10,9},{11,10},{12... | collective-permute-start | bytes 110600 | tf_op jit(solution)/shard_map/ppermute | solution.py:471
  14.2 3.1 %collective-permute-start.2 = (f32[12,3,2,128]{3,2,1,0:T(2,128)S(1)}, f32[12,3,2,128]{3,2,1,0:T(2,128)S(1)}, u32[]{:S(2)}, u32[]{:S(2)}) collective-permute-start(f32[12,3,2,128]{3,2,1,0:T(2,128)S(1)} %get-tuple-element.40), channel_id=1, source_target_pairs={{0,1},{1,2},{2,3},{3,4},{4,5},{5,6},{6,7},{8,9},{9,10},{10,11},{11... | collective-permute-start | bytes 110600 | tf_op jit(solution)/shard_map/ppermute | solution.py:470
  17.3 0.0 copy-start
  17.3 2.4 %copy-done = bf16[10,10,64,3,128]{4,2,3,1,0:T(8,128)(2,1)S(1)} copy-done((bf16[10,10,64,3,128]{4,2,3,1,0:T(8,128)(2,1)S(1)}, bf16[10,10,64,3,128]{4,2,3,1,0:T(8,128)(2,1)}, u32[]{:S(2)}) %copy-start) | copy-done | bytes 4915224
  19.7 3.1 %pack.1 = (bf16[3,10,3,64,128]{4,3,2,1,0:T(8,128)(2,1)}, bf16[3,6,3,64,128]{4,3,2,1,0:T(8,128)(2,1)}, bf16[10,3,3,64,128]{4,3,2,1,0:T(8,128)(2,1)}, bf16[10,3,3,64,128]{4,3,2,1,0:T(8,128)(2,1)}) custom-call(s32[1]{0:T(128)} %bitcast.odd_ref, bf16[10,10,3,64,128]{4,3,2,1,0:T(8,128)(2,1)S(1)} %bitcast.31), custom_call_target="tpu_custom_call" | custom-call | flops 1000 | bytes 1000 | tf_op jit(solution)/shard_map/pack/pallas_call | solution.py:490
  22.8 0.0 collective-permute-done.3.refs_5_.hi_ref
  22.8 2.4 %collective-permute-start.5 = (bf16[10,3,3,64,128]{4,3,2,1,0:T(8,128)(2,1)}, bf16[10,3,3,64,128]{4,3,2,1,0:T(8,128)(2,1)S(1)}, u32[]{:S(2)}, u32[]{:S(2)}) collective-permute-start(bf16[10,3,3,64,128]{4,3,2,1,0:T(8,128)(2,1)} %get-tuple-element.27), channel_id=1, source_target_pairs={{0,1},{1,2},{2,3},{3,4},{4,5},{5,6},{6,7},{8,9},{9,10},{10,11},{11... | collective-permute-start | bytes 4423688 | tf_op jit(solution)/shard_map/ppermute | solution.py:523
  25.3 2.0 %collective-permute-start.6 = (bf16[10,3,3,64,128]{4,3,2,1,0:T(8,128)(2,1)}, bf16[10,3,3,64,128]{4,3,2,1,0:T(8,128)(2,1)S(1)}, u32[]{:S(2)}, u32[]{:S(2)}) collective-permute-start(bf16[10,3,3,64,128]{4,3,2,1,0:T(8,128)(2,1)} %get-tuple-element.28), channel_id=1, source_target_pairs={{1,0},{2,1},{3,2},{4,3},{5,4},{6,5},{7,6},{9,8},{10,9},{11,10},{12... | collective-permute-start | bytes 4423688 | tf_op jit(solution)/shard_map/ppermute | solution.py:524
  27.3 4.3 %collective-permute-start.13 = (bf16[3,10,3,64,128]{4,3,2,1,0:T(8,128)(2,1)}, bf16[3,10,3,64,128]{4,3,2,1,0:T(8,128)(2,1)}, u32[]{:S(2)}, u32[]{:S(2)}) collective-permute-start(bf16[3,10,3,64,128]{4,3,2,1,0:T(8,128)(2,1)} %get-tuple-element.36), channel_id=1, source_target_pairs={{8,0},{16,8},{24,16},{32,24},{40,32},{48,40},{56,48},{64,56},{72,6... | collective-permute-start | bytes 4423688 | tf_op jit(solution)/shard_map/ppermute | solution.py:520
  31.5 1.3 %collective-permute-start.4 = (bf16[3,6,3,64,128]{4,3,2,1,0:T(8,128)(2,1)}, bf16[3,6,3,64,128]{4,3,2,1,0:T(8,128)(2,1)}, u32[]{:S(2)}, u32[]{:S(2)}) collective-permute-start(bf16[3,6,3,64,128]{4,3,2,1,0:T(8,128)(2,1)} %get-tuple-element.26), channel_id=1, source_target_pairs={{0,8},{8,16},{16,24},{24,32},{32,40},{40,48},{48,56},{56,64},{64,7... | collective-permute-start | bytes 2654216 | tf_op jit(solution)/shard_map/ppermute | solution.py:521
  32.9 16.4 %own_gram.1 = (f32[64,64]{1,0:T(8,128)S(1)}, f32[12,6,12,128]{3,2,1,0:T(8,128)S(1)}, bf16[10,128,1152]{2,1,0:T(8,128)(2,1)S(1)}, bf16[10,128,1152]{2,1,0:T(8,128)(2,1)S(1)}, bf16[3,128,3840]{2,1,0:T(8,128)(2,1)S(1)}) custom-call(s32[1]{0:T(128)} %bitcast.odd_ref, f32[12]{0:T(128)S(1)} %get-tuple-element.44.sx_ref, f32[12]{0:T(128)S(1)} %get-tuple-element.43.sy_ref, ...), custom_call_target="tpu_custom_call" | custom-call | flops 1000 | bytes 1000 | tf_op jit(solution)/shard_map/own_gram/pallas_call | solution.py:526
  49.2 0.0 collective-permute-done.5.south_ref
  49.2 0.0 collective-permute-done.6.north_ref
  49.3 8.4 %row_gram.1 = (f32[64,128]{1,0:T(8,128)S(1)}, bf16[2,2,128,3456]{3,2,1,0:T(8,128)(2,1)S(1)}) custom-call(bf16[10,3,3,64,128]{4,3,2,1,0:T(8,128)(2,1)S(1)} %collective-permute-done.5.south_ref, bf16[10,3,3,64,128]{4,3,2,1,0:T(8,128)(2,1)S(1)} %collective-permute-done.6.north_ref, bf16[10,128,1152]{2,1,0:T(8,128)(2,1)S(1)} %get-tuple-element.29.simg_hbm, ...), custom_call_target="tpu_custom_call" | custom-call | flops 1000 | bytes 1000 | tf_op jit(solution)/shard_map/row_gram/pallas_call | solution.py:548
  57.7 0.0 collective-permute-done.4.corner_ref
  57.7 2.0 %corner_gram.1 = (f32[64,256]{1,0:T(8,128)S(1)}, f32[64,64]{1,0:T(8,128)S(1)}) custom-call(s32[1]{0:T(128)} %bitcast.odd_ref, bf16[3,6,3,64,128]{4,3,2,1,0:T(8,128)(2,1)} %collective-permute-done.4.corner_ref, bf16[2,2,128,3456]{3,2,1,0:T(8,128)(2,1)S(1)} %get-tuple-element.32.cimg_ref, f32[64,64]{1,0:T(8,128)S(1)} %get-tuple-element.33.own_ref, ...), custom_call_target="tpu_custom_call" | custom-call | flops 1000 | bytes 1000 | tf_op jit(solution)/shard_map/corner_gram/pallas_call | solution.py:562
  59.7 6.6 %collective-permute-start.9 = (f32[64,256]{1,0:T(8,128)S(1)}, f32[64,256]{1,0:T(8,128)S(1)}, u32[]{:S(2)}, u32[]{:S(2)}) collective-permute-start(f32[64,256]{1,0:T(8,128)S(1)} %get-tuple-element.35), channel_id=1, source_target_pairs={{0,96},{8,104},{16,112},{24,120},{32,0},{40,8},{48,16},{56,24},{64... | collective-permute-start | bytes 196616 | tf_op jit(solution)/shard_map/ppermute | solution.py:455
  66.3 0.7 collective-permute-start.7
  67.0 2.3 %collective-permute-done.9 = f32[64,256]{1,0:T(8,128)S(1)} collective-permute-done((f32[64,256]{1,0:T(8,128)S(1)}, f32[64,256]{1,0:T(8,128)S(1)}, u32[]{:S(2)}, u32[]{:S(2)}) %collective-permute-start.9) | collective-permute-done | bytes 65568 | tf_op jit(solution)/shard_map/ppermute | solution.py:455
  69.2 2.3 %collective-permute-done.8 = f32[64,256]{1,0:T(8,128)S(1)} collective-permute-done((f32[64,256]{1,0:T(8,128)S(1)}, f32[64,256]{1,0:T(8,128)S(1)}, u32[]{:S(2)}, u32[]{:S(2)}) %collective-permute-start.8) | collective-permute-done | bytes 65568 | tf_op jit(solution)/shard_map/ppermute | solution.py:455
  71.5 1.2 %collective-permute-done.7 = f32[64,256]{1,0:T(8,128)S(1)} collective-permute-done((f32[64,256]{1,0:T(8,128)S(1)}, f32[64,256]{1,0:T(8,128)S(1)}, u32[]{:S(2)}, u32[]{:S(2)}) %collective-permute-start.7) | collective-permute-done | bytes 65568 | tf_op jit(solution)/shard_map/ppermute | solution.py:455
  72.7 0.2 collective-permute-start.12
  72.9 0.0 collective-permute-done.13.main_ref
  72.9 2.9 %column_gram.1 = f32[64,256]{1,0:T(8,128)S(1)} custom-call(s32[1]{0:T(128)} %bitcast.odd_ref, bf16[3,10,3,64,128]{4,3,2,1,0:T(8,128)(2,1)} %collective-permute-done.13.main_ref, bf16[3,128,3840]{2,1,0:T(8,128)(2,1)S(1)} %get-tuple-element.37.ximg_ref, bf16[2,2,128,3456]{3,2,1,0:T(8,128)(2,1)S(1)} %get-tuple-element.32.cimg_ref, ...), custom_call_target="tpu_custom_call" | custom-call | flops 1000 | bytes 1000 | tf_op jit(solution)/shard_map/column_gram/pallas_call | solution.py:571
  75.8 0.9 collective-permute-start.16
  76.7 2.4 %collective-permute-start.15 = (f32[64,256]{1,0:T(8,128)S(1)}, f32[64,256]{1,0:T(8,128)S(1)}, u32[]{:S(2)}, u32[]{:S(2)}) collective-permute-start(f32[64,256]{1,0:T(8,128)S(1)} %column_gram.1), channel_id=1, source_target_pairs={{0,16},{8,24},{16,0},{24,8},{32,48},{40,56},{48,32},{56,40},{64,80... | collective-permute-start | bytes 196616 | tf_op jit(solution)/shard_map/ppermute | solution.py:455
  79.0 0.0 collective-permute-start.14
  79.0 1.9 %collective-permute-start.11 = (f32[4,64,256]{2,1,0:T(8,128)S(1)}, f32[4,64,256]{2,1,0:T(8,128)S(1)}, u32[]{:S(2)}, u32[]{:S(2)}) collective-permute-start(f32[4,64,256]{2,1,0:T(8,128)S(1)} %pad_maximum_fusion.refs_0_), channel_id=1, source_target_pairs={{0,16},{8,24},{16,0},{24,8},{32,48},{40,56},{48,32},{56,40},{64,80... | collective-permute-start | bytes 786440 | tf_op jit(solution)/shard_map/ppermute | solution.py:455
  80.9 0.4 collective-permute-done.16
  81.3 1.0 collective-permute-start.10
  82.3 5.1 %collective-permute-done.14 = f32[64,256]{1,0:T(8,128)S(1)} collective-permute-done((f32[64,256]{1,0:T(8,128)S(1)}, f32[64,256]{1,0:T(8,128)S(1)}, u32[]{:S(2)}, u32[]{:S(2)}) %collective-permute-start.14) | collective-permute-done | bytes 65568 | tf_op jit(solution)/shard_map/ppermute | solution.py:455
  87.4 0.6 collective-permute-start.19
  88.0 0.2 collective-permute-start.18
  88.2 0.0 collective-permute-done.12.refs_3_
  88.2 0.8 collective-permute-start.17
  89.0 0.1 stack.125.slot_ref
  89.1 0.0 collective-permute-done.11.refs_2_
  89.1 6.0 %collective-permute-done.10.refs_1_ = f32[4,64,256]{2,1,0:T(8,128)S(1)} collective-permute-done((f32[4,64,256]{2,1,0:T(8,128)S(1)}, f32[4,64,256]{2,1,0:T(8,128)S(1)}, u32[]{:S(2)}, u32[]{:S(2)}) %collective-permute-start.10) | collective-permute-done | bytes 262176 | tf_op jit(solution)/shard_map/ppermute | solution.py:455
  95.1 0.0 collective-permute-done.19.refs_7_
  95.1 0.1 collective-permute-done.18.refs_6_
  95.2 8.1 %collective-permute-done.17.refs_5_ = f32[4,64,256]{2,1,0:T(8,128)S(1)} collective-permute-done((f32[4,64,256]{2,1,0:T(8,128)S(1)}, f32[4,64,256]{2,1,0:T(8,128)S(1)}, u32[]{:S(2)}, u32[]{:S(2)}) %collective-permute-start.17) | collective-permute-done | bytes 262176 | tf_op jit(solution)/shard_map/ppermute | solution.py:455
  103.4 6.7 %assemble.1 = f32[16,64,576]{2,1,0:T(8,128)} custom-call(s32[1]{0:T(128)} %bitcast.odd_ref, s32[32]{0:T(128)S(1)} %stack.125.slot_ref, f32[4,64,256]{2,1,0:T(8,128)S(1)} %pad_maximum_fusion.refs_0_, f32[4,64,256]{2,1,0:T(8,128)S(1)} %collective-permute-done.10.refs_1_, f32[4,64,256]{2,1,0:T(8,128)S(1)} %collective-permute-done.11.refs_2_, ...), custom_call_target="tpu_custom_call" | custom-call | flops 1000 | bytes 1000 | tf_op jit(solution)/shard_map/assemble/pallas_call | solution.py:596
  (8 shorter events, 0.1 us)
Async XLA Ops:
  0.8 5.2 %collective-permute-start = (f32[2,3,8,128]{3,2,1,0:T(8,128)S(1)}, f32[2,3,8,128]{3,2,1,0:T(8,128)S(1)}, u32[]{:S(2)}, u32[]{:S(2)}) collective-permute-start(f32[2,3,8,128]{3,2,1,0:T(8,128)S(1)} %get-tuple-element.41), channel_id=1, source_target_pairs={{0,8},{8,16},{16,24},{24,32},{32,40},{40,48},{48,56},{56,64},{64,7... | collective-permute-start | bytes 73736 | tf_op jit(solution)/shard_map/ppermute | solution.py:466
  4.7 4.6 %collective-permute-start.1 = (f32[2,3,8,128]{3,2,1,0:T(8,128)S(1)}, f32[2,3,8,128]{3,2,1,0:T(8,128)S(1)}, u32[]{:S(2)}, u32[]{:S(2)}) collective-permute-start(f32[2,3,8,128]{3,2,1,0:T(8,128)S(1)} %get-tuple-element.42), channel_id=1, source_target_pairs={{8,0},{16,8},{24,16},{32,24},{40,32},{48,40},{56,48},{64,56},{72,6... | collective-permute-start | bytes 73736 | tf_op jit(solution)/shard_map/ppermute | solution.py:467
  10.1 12.7 %collective-permute-start.3 = (f32[12,3,2,128]{3,2,1,0:T(2,128)S(1)}, f32[12,3,2,128]{3,2,1,0:T(2,128)S(1)}, u32[]{:S(2)}, u32[]{:S(2)}) collective-permute-start(f32[12,3,2,128]{3,2,1,0:T(2,128)S(1)} %get-tuple-element.39), channel_id=1, source_target_pairs={{1,0},{2,1},{3,2},{4,3},{5,4},{6,5},{7,6},{9,8},{10,9},{11,10},{12... | collective-permute-start | bytes 110600 | tf_op jit(solution)/shard_map/ppermute | solution.py:471
  14.2 8.7 %collective-permute-start.2 = (f32[12,3,2,128]{3,2,1,0:T(2,128)S(1)}, f32[12,3,2,128]{3,2,1,0:T(2,128)S(1)}, u32[]{:S(2)}, u32[]{:S(2)}) collective-permute-start(f32[12,3,2,128]{3,2,1,0:T(2,128)S(1)} %get-tuple-element.40), channel_id=1, source_target_pairs={{0,1},{1,2},{2,3},{3,4},{4,5},{5,6},{6,7},{8,9},{9,10},{10,11},{11... | collective-permute-start | bytes 110600 | tf_op jit(solution)/shard_map/ppermute | solution.py:470
  17.3 2.4 %copy-start = (bf16[10,10,64,3,128]{4,2,3,1,0:T(8,128)(2,1)S(1)}, bf16[10,10,64,3,128]{4,2,3,1,0:T(8,128)(2,1)}, u32[]{:S(2)}) copy-start(bf16[10,10,64,3,128]{4,2,3,1,0:T(8,128)(2,1)} %param.4) | copy-start | bytes 14745604
  22.8 26.4 %collective-permute-start.5 = (bf16[10,3,3,64,128]{4,3,2,1,0:T(8,128)(2,1)}, bf16[10,3,3,64,128]{4,3,2,1,0:T(8,128)(2,1)S(1)}, u32[]{:S(2)}, u32[]{:S(2)}) collective-permute-start(bf16[10,3,3,64,128]{4,3,2,1,0:T(8,128)(2,1)} %get-tuple-element.27), channel_id=1, source_target_pairs={{0,1},{1,2},{2,3},{3,4},{4,5},{5,6},{6,7},{8,9},{9,10},{10,11},{11... | collective-permute-start | bytes 4423688 | tf_op jit(solution)/shard_map/ppermute | solution.py:523
  25.3 24.0 %collective-permute-start.6 = (bf16[10,3,3,64,128]{4,3,2,1,0:T(8,128)(2,1)}, bf16[10,3,3,64,128]{4,3,2,1,0:T(8,128)(2,1)S(1)}, u32[]{:S(2)}, u32[]{:S(2)}) collective-permute-start(bf16[10,3,3,64,128]{4,3,2,1,0:T(8,128)(2,1)} %get-tuple-element.28), channel_id=1, source_target_pairs={{1,0},{2,1},{3,2},{4,3},{5,4},{6,5},{7,6},{9,8},{10,9},{11,10},{12... | collective-permute-start | bytes 4423688 | tf_op jit(solution)/shard_map/ppermute | solution.py:524
  27.3 45.6 %collective-permute-start.13 = (bf16[3,10,3,64,128]{4,3,2,1,0:T(8,128)(2,1)}, bf16[3,10,3,64,128]{4,3,2,1,0:T(8,128)(2,1)}, u32[]{:S(2)}, u32[]{:S(2)}) collective-permute-start(bf16[3,10,3,64,128]{4,3,2,1,0:T(8,128)(2,1)} %get-tuple-element.36), channel_id=1, source_target_pairs={{8,0},{16,8},{24,16},{32,24},{40,32},{48,40},{56,48},{64,56},{72,6... | collective-permute-start | bytes 4423688 | tf_op jit(solution)/shard_map/ppermute | solution.py:520
  31.5 26.2 %collective-permute-start.4 = (bf16[3,6,3,64,128]{4,3,2,1,0:T(8,128)(2,1)}, bf16[3,6,3,64,128]{4,3,2,1,0:T(8,128)(2,1)}, u32[]{:S(2)}, u32[]{:S(2)}) collective-permute-start(bf16[3,6,3,64,128]{4,3,2,1,0:T(8,128)(2,1)} %get-tuple-element.26), channel_id=1, source_target_pairs={{0,8},{8,16},{16,24},{24,32},{32,40},{40,48},{48,56},{56,64},{64,7... | collective-permute-start | bytes 2654216 | tf_op jit(solution)/shard_map/ppermute | solution.py:521
  59.7 9.6 %collective-permute-start.9 = (f32[64,256]{1,0:T(8,128)S(1)}, f32[64,256]{1,0:T(8,128)S(1)}, u32[]{:S(2)}, u32[]{:S(2)}) collective-permute-start(f32[64,256]{1,0:T(8,128)S(1)} %get-tuple-element.35), channel_id=1, source_target_pairs={{0,96},{8,104},{16,112},{24,120},{32,0},{40,8},{48,16},{56,24},{64... | collective-permute-start | bytes 196616 | tf_op jit(solution)/shard_map/ppermute | solution.py:455
  66.3 5.2 %collective-permute-start.8 = (f32[64,256]{1,0:T(8,128)S(1)}, f32[64,256]{1,0:T(8,128)S(1)}, u32[]{:S(2)}, u32[]{:S(2)}) collective-permute-start(f32[64,256]{1,0:T(8,128)S(1)} %get-tuple-element.35), channel_id=1, source_target_pairs={{0,64},{8,72},{16,80},{24,88},{32,96},{40,104},{48,112},{56,120},{... | collective-permute-start | bytes 196616 | tf_op jit(solution)/shard_map/ppermute | solution.py:455
  66.3 6.4 %collective-permute-start.7 = (f32[64,256]{1,0:T(8,128)S(1)}, f32[64,256]{1,0:T(8,128)S(1)}, u32[]{:S(2)}, u32[]{:S(2)}) collective-permute-start(f32[64,256]{1,0:T(8,128)S(1)} %get-tuple-element.35), channel_id=1, source_target_pairs={{0,32},{8,40},{16,48},{24,56},{32,64},{40,72},{48,80},{56,88},{64,... | collective-permute-start | bytes 196616 | tf_op jit(solution)/shard_map/ppermute | solution.py:455
  72.7 15.5 %collective-permute-start.12 = (f32[4,64,256]{2,1,0:T(8,128)S(1)}, f32[4,64,256]{2,1,0:T(8,128)S(1)}, u32[]{:S(2)}, u32[]{:S(2)}) collective-permute-start(f32[4,64,256]{2,1,0:T(8,128)S(1)} %pad_maximum_fusion.refs_0_), channel_id=1, source_target_pairs={{0,24},{8,0},{16,8},{24,16},{32,56},{40,32},{48,40},{56,48},{64,88... | collective-permute-start | bytes 786440 | tf_op jit(solution)/shard_map/ppermute | solution.py:455
  75.8 5.5 %collective-permute-start.16 = (f32[64,256]{1,0:T(8,128)S(1)}, f32[64,256]{1,0:T(8,128)S(1)}, u32[]{:S(2)}, u32[]{:S(2)}) collective-permute-start(f32[64,256]{1,0:T(8,128)S(1)} %column_gram.1), channel_id=1, source_target_pairs={{0,24},{8,0},{16,8},{24,16},{32,56},{40,32},{48,40},{56,48},{64,88... | collective-permute-start | bytes 196616 | tf_op jit(solution)/shard_map/ppermute | solution.py:455
  76.7 5.6 %collective-permute-start.15 = (f32[64,256]{1,0:T(8,128)S(1)}, f32[64,256]{1,0:T(8,128)S(1)}, u32[]{:S(2)}, u32[]{:S(2)}) collective-permute-start(f32[64,256]{1,0:T(8,128)S(1)} %column_gram.1), channel_id=1, source_target_pairs={{0,16},{8,24},{16,0},{24,8},{32,48},{40,56},{48,32},{56,40},{64,80... | collective-permute-start | bytes 196616 | tf_op jit(solution)/shard_map/ppermute | solution.py:455
  79.0 8.4 %collective-permute-start.14 = (f32[64,256]{1,0:T(8,128)S(1)}, f32[64,256]{1,0:T(8,128)S(1)}, u32[]{:S(2)}, u32[]{:S(2)}) collective-permute-start(f32[64,256]{1,0:T(8,128)S(1)} %column_gram.1), channel_id=1, source_target_pairs={{0,8},{8,16},{16,24},{24,0},{32,40},{40,48},{48,56},{56,32},{64,72... | collective-permute-start | bytes 196616 | tf_op jit(solution)/shard_map/ppermute | solution.py:455
  79.0 10.0 %collective-permute-start.11 = (f32[4,64,256]{2,1,0:T(8,128)S(1)}, f32[4,64,256]{2,1,0:T(8,128)S(1)}, u32[]{:S(2)}, u32[]{:S(2)}) collective-permute-start(f32[4,64,256]{2,1,0:T(8,128)S(1)} %pad_maximum_fusion.refs_0_), channel_id=1, source_target_pairs={{0,16},{8,24},{16,0},{24,8},{32,48},{40,56},{48,32},{56,40},{64,80... | collective-permute-start | bytes 786440 | tf_op jit(solution)/shard_map/ppermute | solution.py:455
  81.3 13.8 %collective-permute-start.10 = (f32[4,64,256]{2,1,0:T(8,128)S(1)}, f32[4,64,256]{2,1,0:T(8,128)S(1)}, u32[]{:S(2)}, u32[]{:S(2)}) collective-permute-start(f32[4,64,256]{2,1,0:T(8,128)S(1)} %pad_maximum_fusion.refs_0_), channel_id=1, source_target_pairs={{0,8},{8,16},{16,24},{24,0},{32,40},{40,48},{48,56},{56,32},{64,72... | collective-permute-start | bytes 786440 | tf_op jit(solution)/shard_map/ppermute | solution.py:455
  87.4 7.7 %collective-permute-start.19 = (f32[4,64,256]{2,1,0:T(8,128)S(1)}, f32[4,64,256]{2,1,0:T(8,128)S(1)}, u32[]{:S(2)}, u32[]{:S(2)}) collective-permute-start(f32[4,64,256]{2,1,0:T(8,128)S(1)} %pad_maximum_fusion.1.refs_4_), channel_id=1, source_target_pairs={{0,96},{8,104},{16,112},{24,120},{32,0},{40,8},{48,16},{56,24},{64... | collective-permute-start | bytes 786440 | tf_op jit(solution)/shard_map/ppermute | solution.py:455
  88.0 7.2 %collective-permute-start.18 = (f32[4,64,256]{2,1,0:T(8,128)S(1)}, f32[4,64,256]{2,1,0:T(8,128)S(1)}, u32[]{:S(2)}, u32[]{:S(2)}) collective-permute-start(f32[4,64,256]{2,1,0:T(8,128)S(1)} %pad_maximum_fusion.1.refs_4_), channel_id=1, source_target_pairs={{0,64},{8,72},{16,80},{24,88},{32,96},{40,104},{48,112},{56,120},{... | collective-permute-start | bytes 786440 | tf_op jit(solution)/shard_map/ppermute | solution.py:455
  88.2 15.2 %collective-permute-start.17 = (f32[4,64,256]{2,1,0:T(8,128)S(1)}, f32[4,64,256]{2,1,0:T(8,128)S(1)}, u32[]{:S(2)}, u32[]{:S(2)}) collective-permute-start(f32[4,64,256]{2,1,0:T(8,128)S(1)} %pad_maximum_fusion.1.refs_4_), channel_id=1, source_target_pairs={{0,32},{8,40},{16,48},{24,56},{32,64},{40,72},{48,80},{56,88},{64,... | collective-permute-start | bytes 786440 | tf_op jit(solution)/shard_map/ppermute | solution.py:455

commit v3 on v2

--- a/solution.py
+++ b/solution.py
@@ -12,6 +12,7 @@
 MID, LOW, UPP, DIA, VOL, OUT = range(6)
 NT = (((1,), (1,)), ((), ()))
 MIB = 1024 * 1024
+TOP = 1024.0
 
 
 def cover(start, length, cell, count, margin):
@@ -332,7 +333,7 @@
     keep_ref[...] = north
 
 
-def main_kernel(odd_ref, main_ref, ximg_ref, cimg_ref, keep_ref, out_ref):
+def main_kernel(odd_ref, main_ref, ximg_ref, cimg_ref, early_ref, keep_ref, out_ref):
     t = 1 - odd_ref[0]
     ext = main_ref.shape[1]
     total = None
@@ -342,30 +343,56 @@
         total = part if total is None else total + part
     south = corner_dot(lambda i, j, a: main_ref[i, j, a], cimg_ref[t, 0])
     north = corner_dot(lambda i, j, a: main_ref[i, ext - 3 + j, a], cimg_ref[t, 1])
-    out_ref[...] = side([south, fold_rows(total), north, keep_ref[...]])
-
-
-def final_kernel(odd_ref, slot_ref, *refs):
-    *pieces, out_hbm, e_ref, l_ref, o_ref, sems, out_sems = refs
-    copies = []
-    for h, ref in enumerate((e_ref, l_ref)):
-        for i in range(4):
-            for j in range(4):
-                at = h * 16 + i * 4 + j
-                copies.append(
-                    pltpu.make_async_copy(
-                        pieces[h * 4 + i].at[j], ref.at[slot_ref[at] + 1], sems.at[at]
-                    )
-                )
-    for copy in copies:
-        copy.start()
+    code = encode(side([early_ref[...], south, fold_rows(total), north, keep_ref[...]]))
+    for p in range(out_ref.shape[0]):
+        out_ref[p] = code
+
+
+def encode(rows):
+    top = jnp.max(jnp.abs(rows), axis=(0, 1), keepdims=True)
+    top = jnp.where(top > 0.0, jnp.maximum(top * 1.01, 2.0**-100), 1.0).astype(BF16).astype(F32)
+    value = rows * (TOP / top)
+    value2 = value * value
+    value4 = value2 * value2
+    power = value4 * value4 * value4
+    code = jnp.where(rows < 0.0, -power, power)
+    row = lax.broadcasted_iota(jnp.int32, rows.shape, 0)
+    lane = lax.broadcasted_iota(jnp.int32, rows.shape, 1)
+    return jnp.where((row == 0) & (lane == 1), top, code).astype(BF16)
+
+
+def decode(code):
+    value = code.astype(F32)
+    first = value[:8, :128]
+    row = lax.broadcasted_iota(jnp.int32, first.shape, 0)
+    lane = lax.broadcasted_iota(jnp.int32, first.shape, 1)
+
+    def pick(tile, i, j):
+        return jnp.sum(jnp.where((row == i) & (lane == j), tile, 0.0), axis=(0, 1), keepdims=True)
+
+    scale = pick(first, 0, 1) * (1.0 / TOP)
+    root = jnp.exp(jnp.log(jnp.abs(value)) * (1.0 / 12.0)) * scale
+    root = jnp.where(value < 0.0, -root, root)
+    head = root[:8, :128]
+    head = jnp.where((row == 0) & (lane == 1), pick(head, 1, 0), head)
+    return root, head
+
+
+def final_kernel(odd_ref, code_ref, out_hbm, e_ref, l_ref, o_ref, out_sems):
     odd = odd_ref[0]
     none = jnp.zeros(e_ref.shape[1:], F32)
     for ref in (e_ref, l_ref):
         ref[0] = none
         ref[17] = none
-    for copy in copies:
-        copy.wait()
+
+    def read(p, _):
+        root, head = decode(code_ref[p])
+        e_ref[p + 1] = root[:, :256]
+        l_ref[p + 1] = root[:, 256:]
+        e_ref[p + 1, pl.ds(0, 8), pl.ds(0, 128)] = head
+        return 0
+
+    lax.fori_loop(0, 16, read, 0, unroll=2)
 
     def put(p):
         return pltpu.make_async_copy(o_ref.at[p], out_hbm.at[p], out_sems.at[p])
@@ -420,6 +447,10 @@
     return pl.BlockSpec(memory_space=pl.ANY)
 
 
+def hbm_spec():
+    return pl.BlockSpec(memory_space=pltpu.HBM)
+
+
 def vmem_spec():
     return pl.BlockSpec(memory_space=pltpu.VMEM)
 
@@ -445,31 +476,535 @@
     )
 
 
+def gate(values, others):
+    count = len(values)
+    return pl.pallas_call(
+        gate_kernel,
+        out_shape=[shape(*x.shape, dtype=x.dtype) for x in values],
+        in_specs=[any_spec()] * (count + len(others)),
+        out_specs=[any_spec()] * count,
+        input_output_aliases={i: i for i in range(count)},
+        compiler_params=pltpu.CompilerParams(vmem_limit_bytes=MIB),
+        name="gate",
+    )(*values, *others)
+
+
+def gate(values, others):
+    count = len(values)
+    return pl.pallas_call(
+        gate_kernel,
+        out_shape=[shape(*x.shape, dtype=x.dtype) for x in values],
+        in_specs=[any_spec()] * (count + len(others)),
+        out_specs=[any_spec()] * count,
+        input_output_aliases={i: i for i in range(count)},
+        compiler_params=pltpu.CompilerParams(vmem_limit_bytes=MIB),
+        name="gate",
+    )(*values, *others)
+
+
 def along(nz, nx, dz, dx):
     return [
         (z * nx + x, (z + dz) % nz * nx + (x + dx) % nx) for z in range(nz) for x in range(nx)
     ]
 
 
-def ring(value, steps):
-    return [value] + [lax.ppermute(value, "sx", pairs) for pairs in steps]
-
-
 def neighbours(count):
     up = [(i, i + 1) for i in range(count - 1)]
     return up, [(b, a) for a, b in up]
 
 
-def coef_frame(centre, coupling, volume):
+def spread3(w):
+    return [w[0], w[0] + w[0] + w[1], w[0] + w[1] + w[1] + w[2]]
+
+
+def put_image(img_ref, slot, pos, chunk, image):
+    for a in range(3):
+        high = image[a].astype(BF16)
+        low = (image[a] - high.astype(F32)).astype(BF16)
+        lanes = pl.ds((pos * 3 + a) * 128, 128)
+        img_ref[slot, pl.ds(chunk * 16, 16), lanes] = high
+        img_ref[slot, pl.ds(64 + chunk * 16, 16), lanes] = low
+
+
+def cell_image(lines, values, rows):
+    if values is None:
+        return [-(rows[2] * lines[a]) for a in range(3)]
+    total = rows[1] * (values[0] + values[1] + values[2])
+    return [rows[0] * values[a] + total - rows[2] * lines[a] for a in range(3)]
+
+
+def coef_rows(coef_ref, x, y, names):
+    return [coef_ref[x, n, pl.ds(y, 1), :] for n in names]
+
+
+def depth_sum(raw, rows):
+    return (
+        raw.astype(F32) * rows[0]
+        + pltpu.roll(raw, 1, 1).astype(F32) * rows[1]
+        + pltpu.roll(raw, 127, 1).astype(F32) * rows[2]
+    )
+
+
+def side(blocks):
+    return jnp.concatenate(blocks, axis=1)
+
+
+def fold(total):
+    return total[:, :64] + total[:, 64:]
+
+
+def fold_rows(total):
+    return total[:64] + total[64:]
+
+
+def pack_kernel(odd_ref, m_hbm, main_ref, corner_ref, south_ref, north_ref, sems):
+    ext = m_hbm.shape[0]
+    odd = odd_ref[0]
+    here = jnp.where(odd == 1, ext - 3, 0)
+    there = jnp.where(odd == 1, 0, ext - 3)
+    copies = [
+        pltpu.make_async_copy(m_hbm.at[pl.ds(here, 3)], main_ref, sems.at[0]),
+        pltpu.make_async_copy(
+            m_hbm.at[pl.ds(there, 3), pl.ds(0, 3)], corner_ref.at[:, pl.ds(0, 3)], sems.at[1]
+        ),
+        pltpu.make_async_copy(
+            m_hbm.at[pl.ds(there, 3), pl.ds(ext - 3, 3)], corner_ref.at[:, pl.ds(3, 3)], sems.at[2]
+        ),
+        pltpu.make_async_copy(m_hbm.at[:, pl.ds(ext - 3, 3)], south_ref, sems.at[3]),
+        pltpu.make_async_copy(m_hbm.at[:, pl.ds(0, 3)], north_ref, sems.at[4]),
+    ]
+    for copy in copies:
+        copy.start()
+    for copy in copies:
+        copy.wait()
+
+
+def gate_kernel(*refs):
+    pass
+
+
+def own_kernel(
+    odd_ref, sx_ref, sy_ref, m_hbm, mid_ref, lo_ref, hi_ref,
+    out_ref, coef_ref, simg_hbm, nimg_hbm, ximg_hbm,
+    m_ref, q_ref, img_ref, acc_ref, sems, strip_sems,
+):
+    ext = m_hbm.shape[0]
+    frame = ext + 2
+    odd = odd_ref[0]
+
+    def load(x):
+        return pltpu.make_async_copy(m_hbm.at[x], m_ref.at[x + 1], sems.at[x])
+
+    for x in range(ext):
+        load(x).start()
+    none = jnp.zeros(m_ref.shape[1:], BF16)
+    for edge in (0, ext + 1, ext + 2):
+        m_ref[edge] = none
+    zero = jnp.zeros(q_ref.shape[1:], F32)
+    q_ref[0] = zero
+    q_ref[1] = zero
+    acc_ref[...] = jnp.zeros_like(acc_ref)
+
+    lane = lax.broadcasted_iota(jnp.int32, (frame, 128), 1)
+    place = lax.broadcasted_iota(jnp.int32, (frame, 128), 0)
+    share_y = jnp.zeros((frame, 128), F32)
+    for g in range(frame):
+        share_y = jnp.where(place == g, sy_ref[g], share_y)
+
+    def coefs(f, _):
+        share = share_y * sx_ref[f]
+        cen, cpl, vol = [
+            jnp.concatenate([lo_ref[f, n], mid_ref[f, n], hi_ref[f, n]], axis=0) for n in range(3)
+        ]
+        kap = cpl * share
+        vol = vol * share * share
+        coef_ref[f, MID] = kap + kap
+        coef_ref[f, LOW] = jnp.where(lane == 0, 0.0, pltpu.roll(kap, 1, 1))
+        coef_ref[f, UPP] = jnp.where(lane == 127, 0.0, pltpu.roll(kap, 127, 1))
+        coef_ref[f, DIA] = cen * share * share - vol + 0.5 * kap * kap
+        coef_ref[f, VOL] = vol
+        coef_ref[f, OUT] = kap * (1.0 / 16.0)
+        return 0
+
+    lax.fori_loop(0, frame, coefs, 0)
+
+    def strips(f):
+        return [
+            pltpu.make_async_copy(
+                img_ref.at[f, :, pl.ds(0, 1152)], simg_hbm.at[f - 1], strip_sems.at[0, f - 1]
+            ),
+            pltpu.make_async_copy(
+                img_ref.at[f, :, pl.ds((frame - 3) * 384, 1152)], nimg_hbm.at[f - 1], strip_sems.at[1, f - 1]
+            ),
+        ]
+
+    first_x = jnp.where(odd == 1, 0, frame - 3)
+
+    def strip_x(f):
+        return pltpu.make_async_copy(
+            img_ref.at[f, :, pl.ds(384, ext * 384)], ximg_hbm.at[f - first_x], strip_sems.at[2, f - first_x]
+        )
+
+    def line(f, last, edge):
+        if not last:
+            kaps = [coef_rows(coef_ref, f + 1, g, (MID, LOW, UPP)) for g in range(1, ext + 1)]
+            for a in range(3):
+                for chunk in range(4):
+                    rows = pl.ds(chunk * 16, 16)
+                    pair = None
+                    before = None
+                    for j in range(ext):
+                        w = depth_sum(m_ref[f + 1, j, a, rows, :], kaps[j])
+                        if j == 0:
+                            q_ref[f + 2, 0, a, rows, :] = w
+                            pair = w
+                        else:
+                            now = before + w
+                            q_ref[f + 2, j, a, rows, :] = now + pair
+                            pair = now
+                        before = w
+                    q_ref[f + 2, ext, a, rows, :] = pair + before
+                    q_ref[f + 2, ext + 1, a, rows, :] = before
+        total = acc_ref[...]
+        for g in range(frame):
+            rows_of = coef_rows(coef_ref, f, g, (DIA, VOL, OUT))
+            for chunk in range(4):
+                rows = pl.ds(chunk * 16, 16)
+                values = None
+                if 1 <= g <= ext and not edge:
+                    values = [m_ref[f, g - 1, a, rows, :].astype(F32) for a in range(3)]
+                lines = []
+                for a in range(3):
+                    mid = q_ref[f + 1, g, a, rows, :]
+                    if last:
+                        lines.append(q_ref[f, g, a, rows, :])
+                    else:
+                        lines.append(
+                            (q_ref[f, g, a, rows, :] + mid) + (mid + q_ref[f + 2, g, a, rows, :])
+                        )
+                put_image(img_ref, f, g, chunk, cell_image(lines, values, rows_of))
+            if g % 2 == 0 and 1 < g <= ext and not edge:
+                left = side([m_ref[f, i, a] for i in (g - 2, g - 1) for a in range(3)])
+                total = total + lax.dot_general(
+                    left, img_ref[f, :, pl.ds((g - 1) * 384, 768)], NT, preferred_element_type=F32
+                )
+        acc_ref[...] = total
+
+        @pl.when((f >= first_x) & (f < first_x + 3))
+        def _():
+            strip_x(f).start()
+
+        if not edge:
+            for copy in strips(f):
+                copy.start()
+
+    load(0).wait()
+    line(0, False, True)
+
+    def body(f, _):
+        @pl.when(f < ext)
+        def _():
+            load(f).wait()
+
+        line(f, False, False)
+        return 0
+
+    lax.fori_loop(1, ext + 1, body, 0)
+    line(ext + 1, True, True)
+    out_ref[...] = fold(acc_ref[...])
+    for f in range(1, ext + 1):
+        for copy in strips(f):
+            copy.wait()
+    for i in range(3):
+        strip_x(first_x + i).wait()
+
+
+def rows_kernel(
+    south_ref, north_ref, simg_hbm, nimg_hbm, coef_ref, out_ref, cimg_ref,
+    img_ref, z_ref, acc_ref, sems,
+):
+    ext = south_ref.shape[0]
+    raw_refs = (south_ref, north_ref)
+    images = [
+        pltpu.make_async_copy(ref, img_ref.at[s], sems.at[s])
+        for s, ref in enumerate((simg_hbm, nimg_hbm))
+    ]
+    for copy in images:
+        copy.start()
+    acc_ref[...] = jnp.zeros_like(acc_ref)
+    for s in range(2):
+        r_ref = raw_refs[s]
+        raw_y = (2, 1, 0) if s == 0 else (0, 1, 2)
+        raw_g = (2, 1, 0) if s == 0 else (9, 10, 11)
+        img_g = (3, 2, 1) if s == 0 else (8, 9, 10)
+        img_y = (2, 1, 0) if s == 0 else (0, 1, 2)
+        for t in range(2):
+            raw_x = (0, 1, 2) if t == 0 else (9, 8, 7)
+            raw_f = (1, 2, 3) if t == 0 else (10, 9, 8)
+            img_f = (0, 1, 2) if t == 0 else (11, 10, 9)
+            img_x = (0, 1, 2) if t == 0 else (2, 1, 0)
+
+            def chunked(chunk, _, s=s, t=t, r_ref=r_ref, raw_x=raw_x, raw_f=raw_f, img_f=img_f, img_x=img_x):
+                rows = pl.ds(pl.multiple_of(chunk * 16, 16), 16)
+                low_rows = pl.ds(pl.multiple_of(64 + chunk * 16, 16), 16)
+                for a in range(3):
+                    across = []
+                    for c in range(3):
+                        w = [
+                            depth_sum(
+                                r_ref[raw_x[c], raw_y[d], a, rows, :],
+                                coef_rows(coef_ref, raw_f[c], raw_g[d], (MID, LOW, UPP)),
+                            )
+                            for d in range(3)
+                        ]
+                        across.append(spread3(w))
+                    for e in range(3):
+                        for c, value in enumerate(spread3([across[i][e] for i in range(3)])):
+                            z_ref[c, e, a] = value
+                for c in range(3):
+                    for e in range(3):
+                        values = None
+                        if c > 0 and e > 0:
+                            values = [
+                                r_ref[raw_x[c - 1], raw_y[e - 1], a, rows, :].astype(F32)
+                                for a in range(3)
+                            ]
+                        image = cell_image(
+                            [z_ref[c, e, a] for a in range(3)], values,
+                            coef_rows(coef_ref, img_f[c], img_g[e], (DIA, VOL, OUT)),
+                        )
+                        for a in range(3):
+                            high = image[a].astype(BF16)
+                            low = (image[a] - high.astype(F32)).astype(BF16)
+                            lanes = pl.ds(((img_x[c] * 3 + img_y[e]) * 3 + a) * 128, 128)
+                            cimg_ref[t, s, rows, lanes] = high
+                            cimg_ref[t, s, low_rows, lanes] = low
+                return 0
+
+            lax.fori_loop(0, 4, chunked, 0)
+    for s in range(2):
+        images[s].wait()
+
+        def dots(x, _, s=s):
+            right = side([raw_refs[s][x, j, a] for j in range(3) for a in range(3)])
+            acc_ref[s] += lax.dot_general(img_ref[s, x], right, NT, preferred_element_type=F32)
+            return 0
+
+        lax.fori_loop(0, ext, dots, 0)
+    out_ref[...] = side([fold_rows(acc_ref[0]), fold_rows(acc_ref[1])])
+
+
+def corner_dot(raw, img):
+    left = side([raw(i, j, a) for i in range(3) for j in range(3) for a in range(3)])
+    return fold(lax.dot_general(left, img, NT, preferred_element_type=F32))
+
+
+def other_kernel(odd_ref, corner_ref, cimg_ref, own_ref, rows_ref, out_ref, keep_ref):
+    t = odd_ref[0]
+    south = corner_dot(lambda i, j, a: corner_ref[i, j, a], cimg_ref[t, 0])
+    north = corner_dot(lambda i, j, a: corner_ref[i, j + 3, a], cimg_ref[t, 1])
+    around = rows_ref[...]
+    out_ref[...] = side([own_ref[...], around[:, 64:], south, around[:, :64]])
+    keep_ref[...] = north
+
+
+def main_kernel(odd_ref, main_ref, ximg_ref, cimg_ref, early_ref, keep_ref, out_ref):
+    t = 1 - odd_ref[0]
+    ext = main_ref.shape[1]
+    total = None
+    for i in range(3):
+        right = side([main_ref[i, j, a] for j in range(ext) for a in range(3)])
+        part = lax.dot_general(ximg_ref[i], right, NT, preferred_element_type=F32)
+        total = part if total is None else total + part
+    south = corner_dot(lambda i, j, a: main_ref[i, j, a], cimg_ref[t, 0])
+    north = corner_dot(lambda i, j, a: main_ref[i, ext - 3 + j, a], cimg_ref[t, 1])
+    code = encode(side([early_ref[...], south, fold_rows(total), north, keep_ref[...]]))
+    for p in range(out_ref.shape[0]):
+        out_ref[p] = code
+
+
+def encode(rows):
+    top = jnp.max(jnp.abs(rows), axis=(0, 1), keepdims=True)
+    top = jnp.where(top > 0.0, jnp.maximum(top * 1.01, 2.0**-100), 1.0).astype(BF16).astype(F32)
+    value = rows * (TOP / top)
+    value2 = value * value
+    value4 = value2 * value2
+    power = value4 * value4 * value4
+    code = jnp.where(rows < 0.0, -power, power)
+    row = lax.broadcasted_iota(jnp.int32, rows.shape, 0)
+    lane = lax.broadcasted_iota(jnp.int32, rows.shape, 1)
+    return jnp.where((row == 0) & (lane == 1), top, code).astype(BF16)
+
+
+def decode(code):
+    value = code.astype(F32)
+    first = value[:8, :128]
+    row = lax.broadcasted_iota(jnp.int32, first.shape, 0)
+    lane = lax.broadcasted_iota(jnp.int32, first.shape, 1)
+
+    def pick(tile, i, j):
+        return jnp.sum(jnp.where((row == i) & (lane == j), tile, 0.0), axis=(0, 1), keepdims=True)
+
+    scale = pick(first, 0, 1) * (1.0 / TOP)
+    root = jnp.exp(jnp.log(jnp.abs(value)) * (1.0 / 12.0)) * scale
+    root = jnp.where(value < 0.0, -root, root)
+    head = root[:8, :128]
+    head = jnp.where((row == 0) & (lane == 1), pick(head, 1, 0), head)
+    return root, head
+
+
+def final_kernel(odd_ref, code_ref, out_hbm, e_ref, l_ref, o_ref, out_sems):
+    odd = odd_ref[0]
+    none = jnp.zeros(e_ref.shape[1:], F32)
+    for ref in (e_ref, l_ref):
+        ref[0] = none
+        ref[17] = none
+
+    def read(p, _):
+        root, head = decode(code_ref[p])
+        e_ref[p + 1] = root[:, :256]
+        l_ref[p + 1] = root[:, 256:]
+        e_ref[p + 1, pl.ds(0, 8), pl.ds(0, 128)] = head
+        return 0
+
+    lax.fori_loop(0, 16, read, 0, unroll=2)
+
+    def put(p):
+        return pltpu.make_async_copy(o_ref.at[p], out_hbm.at[p], out_sems.at[p])
+
+    low = lax.broadcasted_iota(jnp.int32, (64, 128), 1) < 64
+
+    def turned(tile):
+        return jnp.transpose(jnp.concatenate([tile, tile], axis=0))[64:]
+
+    def join(lower, upper):
+        return jnp.where(low, lower, upper)
+
+    def tiles(ref, p):
+        return ref[p, :, pl.ds(0, 128)], ref[p, :, pl.ds(128, 128)]
+
+    def even(p, _):
+        (e_one, e_two), (_, e_after) = tiles(e_ref, p + 1), tiles(e_ref, p + 2)
+        (b_one, b_two), (l_one, _), (_, l_after) = [tiles(l_ref, p + i) for i in range(3)]
+        o_ref[p, :, pl.ds(0, 512)] = side(
+            [join(b_one, turned(b_one)), join(b_two, e_two), e_one, join(e_after, l_one)]
+        )
+        o_ref[p, :, pl.ds(512, 64)] = l_after[:, 64:]
+        put(p).start()
+        return 0
+
+    def uneven(p, _):
+        (_, e_before), (e_one, e_two) = tiles(e_ref, p), tiles(e_ref, p + 1)
+        (_, b_two), (l_one, _), (a_one, a_two) = [tiles(l_ref, p + i) for i in range(3)]
+        o_ref[p, :, pl.ds(0, 512)] = side(
+            [
+                join(e_before, l_one), join(pltpu.roll(b_two, 64, 1), e_two), e_one,
+                join(a_one, turned(a_one)),
+            ]
+        )
+        o_ref[p, :, pl.ds(512, 64)] = a_two[:, :64]
+        put(p).start()
+        return 0
+
+    @pl.when(odd == 0)
+    def _():
+        lax.fori_loop(0, 16, even, 0)
+
+    @pl.when(odd == 1)
+    def _():
+        lax.fori_loop(0, 16, uneven, 0)
+
+    for p in range(16):
+        put(p).wait()
+
+
+def any_spec():
+    return pl.BlockSpec(memory_space=pl.ANY)
+
+
+def hbm_spec():
+    return pl.BlockSpec(memory_space=pltpu.HBM)
+
+
+def vmem_spec():
+    return pl.BlockSpec(memory_space=pltpu.VMEM)
+
+
+def smem_spec():
+    return pl.BlockSpec(memory_space=pltpu.SMEM)
+
+
+def shape(*dims, dtype=F32):
+    return jax.ShapeDtypeStruct(dims, dtype)
+
+
+def call(kernel, out_shape, in_specs, out_specs, scratch, mib, name):
+    return pl.pallas_call(
+        kernel,
+        out_shape=out_shape,
+        in_specs=in_specs,
+        out_specs=out_specs,
+        scratch_shapes=scratch,
+        compiler_params=pltpu.CompilerParams(vmem_limit_bytes=mib * MIB),
+        cost_estimate=pl.CostEstimate(flops=1000, bytes_accessed=1000, transcendentals=0),
+        name=name,
+    )
+
+
+def gate(values, others):
+    count = len(values)
+    return pl.pallas_call(
+        gate_kernel,
+        out_shape=[shape(*x.shape, dtype=x.dtype) for x in values],
+        in_specs=[any_spec()] * (count + len(others)),
+        out_specs=[any_spec()] * count,
+        input_output_aliases={i: i for i in range(count)},
+        compiler_params=pltpu.CompilerParams(vmem_limit_bytes=MIB),
+        name="gate",
+    )(*values, *others)
+
+
+def gate(values, others):
+    count = len(values)
+    return pl.pallas_call(
+        gate_kernel,
+        out_shape=[shape(*x.shape, dtype=x.dtype) for x in values],
+        in_specs=[any_spec()] * (count + len(others)),
+        out_specs=[any_spec()] * count,
+        input_output_aliases={i: i for i in range(count)},
+        compiler_params=pltpu.CompilerParams(vmem_limit_bytes=MIB),
+        name="gate",
+    )(*values, *others)
+
+
+def along(nz, nx, dz, dx):
+    return [
+        (z * nx + x, (z + dz) % nz * nx + (x + dx) % nx) for z in range(nz) for x in range(nx)
+    ]
+
+
+def ring(value, steps):
+    return [value] + [lax.ppermute(value, "sx", pairs) for pairs in steps]
+
+
+def neighbours(count):
+    up = [(i, i + 1) for i in range(count - 1)]
+    return up, [(b, a) for a, b in up]
+
+
+def coef_columns(centre, coupling, volume):
     own = jnp.stack([centre, coupling, volume], axis=1)
     up, down = neighbours(lax.axis_size("sx"))
     low = lax.ppermute(own[-2:], "sx", up)
     high = lax.ppermute(own[:2], "sx", down)
-    mid = jnp.concatenate([low, own, high], axis=0)
+    return jnp.concatenate([low, own, high], axis=0)
+
+
+def coef_edges(mid):
     up, down = neighbours(lax.axis_size("sy"))
     lo = lax.ppermute(mid[:, :, -2:], "sy", up)
     hi = lax.ppermute(mid[:, :, :2], "sy", down)
-    return mid, lo, hi
+    return lo, hi
 
 
 def local(modes, centre, coupling, volume):
@@ -483,7 +1018,7 @@
     odd = lax.rem(iy, 2).astype(jnp.int32).reshape(1)
     share_x = cover(ix * cell - margin - 1, ext + 2, cell, nx, margin)
     share_y = cover(iy * cell - margin - 1, ext + 2, cell, ny, margin)
-    mid, lo, hi = coef_frame(centre, coupling, volume)
+    mid = coef_columns(centre, coupling, volume)
     m = jnp.transpose(modes, (0, 1, 3, 2, 4))
     frame = ext + 2
 
@@ -495,22 +1030,13 @@
             shape(ext, 3, 3, 64, 128, dtype=BF16),
             shape(ext, 3, 3, 64, 128, dtype=BF16),
         ],
-        [smem_spec(), any_spec()],
+        [smem_spec(), hbm_spec()],
         [vmem_spec()] * 4,
         [pltpu.SemaphoreType.DMA((5,))],
-        8,
+        54,
         "pack",
     )(odd, m)
-    packed = (main, corner, south, north)
-    main, corner, south, north = pl.pallas_call(
-        gate_kernel,
-        out_shape=[shape(*x.shape, dtype=x.dtype) for x in packed],
-        in_specs=[any_spec()] * 6,
-        out_specs=[any_spec()] * 4,
-        input_output_aliases={i: i for i in range(4)},
-        compiler_params=pltpu.CompilerParams(vmem_limit_bytes=MIB),
-        name="gate",
-    )(*packed, lo, hi)
+    main, corner, south, north, mid = gate((main, corner, south, north, mid), ())
     main_pairs, other_pairs = [], []
     for y in range(ny):
         for x in range(nx - 1):
@@ -519,6 +1045,8 @@
             other_pairs.append((lower, higher) if y % 2 == 0 else (higher, lower))
     main = lax.ppermute(main, ("sx", "sy"), main_pairs)
     corner = lax.ppermute(corner, ("sx", "sy"), other_pairs)
+    lo, hi = coef_edges(mid)
+    south, north = gate((south, north), (lo, hi))
     up, down = neighbours(ny)
     south = lax.ppermute(south, "sy", up)
     north = lax.ppermute(north, "sy", down)
@@ -532,7 +1060,7 @@
             shape(ext, 128, 1152, dtype=BF16),
             shape(3, 128, ext * 384, dtype=BF16),
         ],
-        [smem_spec()] * 3 + [any_spec()] + [vmem_spec()] * 3,
+        [smem_spec()] * 3 + [hbm_spec()] + [vmem_spec()] * 3,
         [vmem_spec(), vmem_spec(), any_spec(), any_spec(), any_spec()],
         [
             pltpu.VMEM((ext + 3, ext, 3, 64, 128), BF16),
@@ -568,46 +1096,30 @@
         10,
         "corner_gram",
     )(odd, corner, cimg, own, around)
-    late = call(
+    code = call(
         main_kernel,
-        shape(64, 256),
-        [smem_spec()] + [vmem_spec()] * 4,
+        shape(nx, 64, 512, dtype=BF16),
+        [smem_spec()] + [vmem_spec()] * 5,
         vmem_spec(),
         [],
-        12,
+        14,
         "column_gram",
-    )(odd, main, ximg, cimg, keep)
-
-    nz, nw = 4, nx // 4
-    z_steps = [along(nz, nw, k, 0) for k in (1, 2, 3)]
-    x_steps = [along(nz, nw, 0, k) for k in (1, 2, 3)]
-    early = ring(jnp.stack(ring(early, z_steps)), x_steps)
-    late = ring(jnp.stack(ring(late, x_steps)), z_steps)
-    iz, iw = ix // nw, lax.rem(ix, nw)
-    slots = []
-    for i in range(4):
-        for j in range(4):
-            slots.append(lax.rem(iz - j + nz, nz) * nw + lax.rem(iw - i + nw, nw))
-    for i in range(4):
-        for j in range(4):
-            slots.append(lax.rem(iz - i + nz, nz) * nw + lax.rem(iw - j + nw, nw))
-    slot = jnp.stack(slots).astype(jnp.int32)
-    pieces = early + late
+    )(odd, main, ximg, cimg, early, keep)
+    code = lax.all_to_all(code, "sx", 0, 0)
     out = call(
         final_kernel,
         shape(nx, 64, 576),
-        [smem_spec(), smem_spec()] + [any_spec()] * len(pieces),
+        [smem_spec(), vmem_spec()],
         any_spec(),
         [
             pltpu.VMEM((nx + 2, 64, 256), F32),
             pltpu.VMEM((nx + 2, 64, 256), F32),
             pltpu.VMEM((nx, 64, 576), F32),
-            pltpu.SemaphoreType.DMA((32,)),
             pltpu.SemaphoreType.DMA((nx,)),
         ],
-        8,
+        12,
         "assemble",
-    )(odd, slot, *pieces)
+    )(odd, code)
     return out[None]
 
 

time: 111 us -> 93.1 us (0.84)
  the two profiles are of different devices: /device:TPU:1 before, /device:TPU:24 now
where the time goes in v3:
time: 93.1 us; the launch traced here: 92.3 us
  Pallas kernels  40.6 us (44%)
  blocking collectives  25.8 us (28%)
  starting transfers between devices  22 us (24%)
  waiting for transfers between devices  2.87 us (3%)
    all_to_all x1, blocking collectives, local(): code = lax.all_to_all(code, 'sx', 0, 0)  25.8 us
    pallas_call x1, Pallas kernels, local(): call(own_kernel, [shape(64, 64), shape(frame, 6, frame, 128), shape(ext,...  16.2 us
    pallas_call x1, Pallas kernels, local(): call(rows_kernel, [shape(64, 128), shape(2, 2, 128, 3456, dtype=BF16)], [...  9.85 us
    ppermute x1, starting transfers between devices, local(): corner = lax.ppermute(corner, ('sx', 'sy'), other_pairs)  6.11 us
    pallas_call x1, Pallas kernels, local(): call(final_kernel, shape(nx, 64, 576), [smem_spec(), vmem_spec()], any_sp...  5.87 us
    pallas_call x1, Pallas kernels, local(): call(pack_kernel, [shape(3, ext, 3, 64, 128, dtype=BF16), shape(3, 6, 3,...  4.97 us
    ppermute x1, starting transfers between devices, local(): north = lax.ppermute(north, 'sy', down)  3.64 us
    ppermute x1, starting transfers between devices, coef_columns(): low = lax.ppermute(own[-2:], 'sx', up)  3.38 us
  transfers between devices with their start and end apart: 8, of which 1 were waited for; matrix products, arithmetic and copies ran while one was open for 0% of the time, Pallas kernels for 36%

profile of v3, /device:TPU:24, one launch (start us, length us, event | category | flops | bytes accessed | tf_op | source)
XLA Modules:
  0.0 92.3 jit_solution(7081077923201957590)
XLA Ops:
  0.0 0.8 pad_maximum_fusion.3
  0.8 3.4 %collective-permute-start = (f32[2,3,8,128]{3,2,1,0:T(8,128)S(1)}, f32[2,3,8,128]{3,2,1,0:T(8,128)S(1)}, u32[]{:S(2)}, u32[]{:S(2)}) collective-permute-start(f32[2,3,8,128]{3,2,1,0:T(8,128)S(1)} %get-tuple-element.47), channel_id=1, source_target_pairs={{0,8},{8,16},{16,24},{24,32},{32,40},{40,48},{48,56},{56,64},{64,7... | collective-permute-start | bytes 73736 | tf_op jit(solution)/shard_map/ppermute | solution.py:998
  4.2 1.3 %collective-permute-start.1 = (f32[2,3,8,128]{3,2,1,0:T(8,128)S(1)}, f32[2,3,8,128]{3,2,1,0:T(8,128)S(1)}, u32[]{:S(2)}, u32[]{:S(2)}) collective-permute-start(f32[2,3,8,128]{3,2,1,0:T(8,128)S(1)} %get-tuple-element.48), channel_id=1, source_target_pairs={{8,0},{16,8},{24,16},{32,24},{40,32},{48,40},{56,48},{64,56},{72,6... | collective-permute-start | bytes 73736 | tf_op jit(solution)/shard_map/ppermute | solution.py:999
  5.5 0.0 copy-start
  5.5 0.0 copy-start.1
  5.5 0.0 copy-start.2
  5.5 5.0 %pack.1 = (bf16[3,10,3,64,128]{4,3,2,1,0:T(8,128)(2,1)}, bf16[3,6,3,64,128]{4,3,2,1,0:T(8,128)(2,1)}, bf16[10,3,3,64,128]{4,3,2,1,0:T(8,128)(2,1)}, bf16[10,3,3,64,128]{4,3,2,1,0:T(8,128)(2,1)}) custom-call(s32[1]{0:T(128)} %bitcast.odd_ref, bf16[10,10,3,64,128]{4,3,2,1,0:T(8,128)(2,1)} %bitcast.6), custom_call_target="tpu_custom_call" | custom-call | flops 1000 | bytes 1000 | tf_op jit(solution)/shard_map/pack/pallas_call | solution.py:1025
  10.5 0.0 collective-permute-done
  10.5 0.0 collective-permute-done.1
  10.5 0.0 copy-done
  10.5 0.0 copy-done.1
  10.5 0.0 copy-done.2
  10.6 1.9 %collective-permute-start.4 = (f32[12,3,2,128]{3,2,1,0:T(2,128)S(1)}, f32[12,3,2,128]{3,2,1,0:T(2,128)S(1)}, u32[]{:S(2)}, u32[]{:S(2)}) collective-permute-start(f32[12,3,2,128]{3,2,1,0:T(2,128)S(1)} %get-tuple-element.45), channel_id=1, source_target_pairs={{1,0},{2,1},{3,2},{4,3},{5,4},{6,5},{7,6},{9,8},{10,9},{11,10},{12... | collective-permute-start | bytes 110600 | tf_op jit(solution)/shard_map/ppermute | solution.py:1006
  12.5 2.4 %collective-permute-start.3 = (f32[12,3,2,128]{3,2,1,0:T(2,128)S(1)}, f32[12,3,2,128]{3,2,1,0:T(2,128)S(1)}, u32[]{:S(2)}, u32[]{:S(2)}) collective-permute-start(f32[12,3,2,128]{3,2,1,0:T(2,128)S(1)} %get-tuple-element.46), channel_id=1, source_target_pairs={{0,1},{1,2},{2,3},{3,4},{4,5},{5,6},{6,7},{8,9},{9,10},{10,11},{11... | collective-permute-start | bytes 110600 | tf_op jit(solution)/shard_map/ppermute | solution.py:1005
  15.0 0.0 collective-permute-done.4.hi_ref.refs_3_
  15.0 2.9 %collective-permute-done.3.lo_ref.refs_2_ = f32[12,3,2,128]{3,2,1,0:T(2,128)S(1)} collective-permute-done((f32[12,3,2,128]{3,2,1,0:T(2,128)S(1)}, f32[12,3,2,128]{3,2,1,0:T(2,128)S(1)}, u32[]{:S(2)}, u32[]{:S(2)}) %collective-permute-start.3) | collective-permute-done | bytes 36896 | tf_op jit(solution)/shard_map/ppermute | solution.py:1005
  17.8 1.9 %collective-permute-start.5 = (bf16[10,3,3,64,128]{4,3,2,1,0:T(8,128)(2,1)}, bf16[10,3,3,64,128]{4,3,2,1,0:T(8,128)(2,1)S(1)}, u32[]{:S(2)}, u32[]{:S(2)}) collective-permute-start(bf16[10,3,3,64,128]{4,3,2,1,0:T(8,128)(2,1)} %get-tuple-element.34), channel_id=1, source_target_pairs={{0,1},{1,2},{2,3},{3,4},{4,5},{5,6},{6,7},{8,9},{9,10},{10,11},{11... | collective-permute-start | bytes 4423688 | tf_op jit(solution)/shard_map/ppermute | solution.py:1051
  19.7 3.6 %collective-permute-start.6 = (bf16[10,3,3,64,128]{4,3,2,1,0:T(8,128)(2,1)}, bf16[10,3,3,64,128]{4,3,2,1,0:T(8,128)(2,1)}, u32[]{:S(2)}, u32[]{:S(2)}) collective-permute-start(bf16[10,3,3,64,128]{4,3,2,1,0:T(8,128)(2,1)} %get-tuple-element.35), channel_id=1, source_target_pairs={{1,0},{2,1},{3,2},{4,3},{5,4},{6,5},{7,6},{9,8},{10,9},{11,10},{12... | collective-permute-start | bytes 4423688 | tf_op jit(solution)/shard_map/ppermute | solution.py:1052
  23.4 1.3 %collective-permute-start.2 = (bf16[3,10,3,64,128]{4,3,2,1,0:T(8,128)(2,1)}, bf16[3,10,3,64,128]{4,3,2,1,0:T(8,128)(2,1)S(1)}, u32[]{:S(2)}, u32[]{:S(2)}) collective-permute-start(bf16[3,10,3,64,128]{4,3,2,1,0:T(8,128)(2,1)} %get-tuple-element.29), channel_id=1, source_target_pairs={{8,0},{16,8},{24,16},{32,24},{40,32},{48,40},{56,48},{64,56},{72,6... | collective-permute-start | bytes 4423688 | tf_op jit(solution)/shard_map/ppermute | solution.py:1046
  24.7 6.1 %collective-permute-start.7 = (bf16[3,6,3,64,128]{4,3,2,1,0:T(8,128)(2,1)}, bf16[3,6,3,64,128]{4,3,2,1,0:T(8,128)(2,1)}, u32[]{:S(2)}, u32[]{:S(2)}) collective-permute-start(bf16[3,6,3,64,128]{4,3,2,1,0:T(8,128)(2,1)} %get-tuple-element.40), channel_id=1, source_target_pairs={{0,8},{8,16},{16,24},{24,32},{32,40},{40,48},{48,56},{56,64},{64,7... | collective-permute-start | bytes 2654216 | tf_op jit(solution)/shard_map/ppermute | solution.py:1047
  30.8 16.2 %own_gram.1 = (f32[64,64]{1,0:T(8,128)S(1)}, f32[12,6,12,128]{3,2,1,0:T(8,128)S(1)}, bf16[10,128,1152]{2,1,0:T(8,128)(2,1)S(1)}, bf16[10,128,1152]{2,1,0:T(8,128)(2,1)S(1)}, bf16[3,128,3840]{2,1,0:T(8,128)(2,1)S(1)}) custom-call(s32[1]{0:T(128)} %bitcast.odd_ref, f32[12]{0:T(128)S(1)} %get-tuple-element.50.sx_ref, f32[12]{0:T(128)S(1)} %get-tuple-element.49.sy_ref, ...), custom_call_target="tpu_custom_call" | custom-call | flops 1000 | bytes 1000 | tf_op jit(solution)/shard_map/own_gram/pallas_call | solution.py:1054
  47.0 0.0 collective-permute-done.5.south_ref
  47.0 0.0 collective-permute-done.6.north_ref
  47.0 9.8 %row_gram.1 = (f32[64,128]{1,0:T(8,128)S(1)}, bf16[2,2,128,3456]{3,2,1,0:T(8,128)(2,1)S(1)}) custom-call(bf16[10,3,3,64,128]{4,3,2,1,0:T(8,128)(2,1)S(1)} %collective-permute-done.5.south_ref, bf16[10,3,3,64,128]{4,3,2,1,0:T(8,128)(2,1)} %collective-permute-done.6.north_ref, bf16[10,128,1152]{2,1,0:T(8,128)(2,1)S(1)} %get-tuple-element.36.simg_hbm, ...), custom_call_target="tpu_custom_call" | custom-call | flops 1000 | bytes 1000 | tf_op jit(solution)/shard_map/row_gram/pallas_call | solution.py:1076
  56.9 0.0 collective-permute-done.7.corner_ref
  56.9 2.0 %corner_gram.1 = (f32[64,256]{1,0:T(8,128)S(1)}, f32[64,64]{1,0:T(8,128)S(1)}) custom-call(s32[1]{0:T(128)} %bitcast.odd_ref, bf16[3,6,3,64,128]{4,3,2,1,0:T(8,128)(2,1)} %collective-permute-done.7.corner_ref, bf16[2,2,128,3456]{3,2,1,0:T(8,128)(2,1)S(1)} %get-tuple-element.39.cimg_ref, f32[64,64]{1,0:T(8,128)S(1)} %get-tuple-element.41.own_ref, ...), custom_call_target="tpu_custom_call" | custom-call | flops 1000 | bytes 1000 | tf_op jit(solution)/shard_map/corner_gram/pallas_call | solution.py:1090
  58.9 0.0 collective-permute-done.2.main_ref
  58.9 1.8 %column_gram.1 = bf16[16,64,512]{2,1,0:T(8,128)(2,1)S(1)} custom-call(s32[1]{0:T(128)} %bitcast.odd_ref, bf16[3,10,3,64,128]{4,3,2,1,0:T(8,128)(2,1)S(1)} %collective-permute-done.2.main_ref, bf16[3,128,3840]{2,1,0:T(8,128)(2,1)S(1)} %get-tuple-element.31.ximg_ref, bf16[2,2,128,3456]{3,2,1,0:T(8,128)(2,1)S(1)} %get-tuple-element.39.cimg_ref, ...), custom_call_target="tpu_custom_call" | custom-call | flops 1000 | bytes 1000 | tf_op jit(solution)/shard_map/column_gram/pallas_call | solution.py:1099
  60.6 25.8 %all_to_all.5.code_ref = bf16[16,64,512]{2,1,0:T(8,128)(2,1)S(1)} all-to-all(bf16[16,64,512]{2,1,0:T(8,128)(2,1)S(1)} %column_gram.1), channel_id=1, replica_groups=mesh['sx'=16,'sy'=8] {'sx'}, dimensions={0} | all-to-all | bytes 2097152 | tf_op jit(solution)/shard_map/all_to_all | solution.py:1108
  86.4 5.9 %assemble.1 = f32[16,64,576]{2,1,0:T(8,128)} custom-call(s32[1]{0:T(128)} %bitcast.odd_ref, bf16[16,64,512]{2,1,0:T(8,128)(2,1)S(1)} %all_to_all.5.code_ref), custom_call_target="tpu_custom_call" | custom-call | flops 1000 | bytes 1000 | tf_op jit(solution)/shard_map/assemble/pallas_call | solution.py:1109
  (5 shorter events, 0.1 us)
Async XLA Ops:
  0.8 9.7 %collective-permute-start = (f32[2,3,8,128]{3,2,1,0:T(8,128)S(1)}, f32[2,3,8,128]{3,2,1,0:T(8,128)S(1)}, u32[]{:S(2)}, u32[]{:S(2)}) collective-permute-start(f32[2,3,8,128]{3,2,1,0:T(8,128)S(1)} %get-tuple-element.47), channel_id=1, source_target_pairs={{0,8},{8,16},{16,24},{24,32},{32,40},{40,48},{48,56},{56,64},{64,7... | collective-permute-start | bytes 73736 | tf_op jit(solution)/shard_map/ppermute | solution.py:998
  4.2 6.3 %collective-permute-start.1 = (f32[2,3,8,128]{3,2,1,0:T(8,128)S(1)}, f32[2,3,8,128]{3,2,1,0:T(8,128)S(1)}, u32[]{:S(2)}, u32[]{:S(2)}) collective-permute-start(f32[2,3,8,128]{3,2,1,0:T(8,128)S(1)} %get-tuple-element.48), channel_id=1, source_target_pairs={{8,0},{16,8},{24,16},{32,24},{40,32},{48,40},{56,48},{64,56},{72,6... | collective-permute-start | bytes 73736 | tf_op jit(solution)/shard_map/ppermute | solution.py:999
  5.5 5.0 %copy-start = (f32[8,8,128]{2,1,0:T(8,128)S(1)}, f32[8,8,128]{2,1,0:T(8,128)}, u32[]{:S(2)}) copy-start(f32[8,8,128]{2,1,0:T(8,128)} %param.7) | copy-start | bytes 98308
  5.5 5.0 %copy-start.1 = (f32[8,8,128]{2,1,0:T(8,128)S(1)}, f32[8,8,128]{2,1,0:T(8,128)}, u32[]{:S(2)}) copy-start(f32[8,8,128]{2,1,0:T(8,128)} %param.6) | copy-start | bytes 98308
  5.5 5.0 %copy-start.2 = (f32[8,8,128]{2,1,0:T(8,128)S(1)}, f32[8,8,128]{2,1,0:T(8,128)}, u32[]{:S(2)}) copy-start(f32[8,8,128]{2,1,0:T(8,128)} %param.5) | copy-start | bytes 98308
  10.6 4.3 %collective-permute-start.4 = (f32[12,3,2,128]{3,2,1,0:T(2,128)S(1)}, f32[12,3,2,128]{3,2,1,0:T(2,128)S(1)}, u32[]{:S(2)}, u32[]{:S(2)}) collective-permute-start(f32[12,3,2,128]{3,2,1,0:T(2,128)S(1)} %get-tuple-element.45), channel_id=1, source_target_pairs={{1,0},{2,1},{3,2},{4,3},{5,4},{6,5},{7,6},{9,8},{10,9},{11,10},{12... | collective-permute-start | bytes 110600 | tf_op jit(solution)/shard_map/ppermute | solution.py:1006
  12.5 5.3 %collective-permute-start.3 = (f32[12,3,2,128]{3,2,1,0:T(2,128)S(1)}, f32[12,3,2,128]{3,2,1,0:T(2,128)S(1)}, u32[]{:S(2)}, u32[]{:S(2)}) collective-permute-start(f32[12,3,2,128]{3,2,1,0:T(2,128)S(1)} %get-tuple-element.46), channel_id=1, source_target_pairs={{0,1},{1,2},{2,3},{3,4},{4,5},{5,6},{6,7},{8,9},{9,10},{10,11},{11... | collective-permute-start | bytes 110600 | tf_op jit(solution)/shard_map/ppermute | solution.py:1005
  17.8 29.2 %collective-permute-start.5 = (bf16[10,3,3,64,128]{4,3,2,1,0:T(8,128)(2,1)}, bf16[10,3,3,64,128]{4,3,2,1,0:T(8,128)(2,1)S(1)}, u32[]{:S(2)}, u32[]{:S(2)}) collective-permute-start(bf16[10,3,3,64,128]{4,3,2,1,0:T(8,128)(2,1)} %get-tuple-element.34), channel_id=1, source_target_pairs={{0,1},{1,2},{2,3},{3,4},{4,5},{5,6},{6,7},{8,9},{9,10},{10,11},{11... | collective-permute-start | bytes 4423688 | tf_op jit(solution)/shard_map/ppermute | solution.py:1051
  19.7 27.3 %collective-permute-start.6 = (bf16[10,3,3,64,128]{4,3,2,1,0:T(8,128)(2,1)}, bf16[10,3,3,64,128]{4,3,2,1,0:T(8,128)(2,1)}, u32[]{:S(2)}, u32[]{:S(2)}) collective-permute-start(bf16[10,3,3,64,128]{4,3,2,1,0:T(8,128)(2,1)} %get-tuple-element.35), channel_id=1, source_target_pairs={{1,0},{2,1},{3,2},{4,3},{5,4},{6,5},{7,6},{9,8},{10,9},{11,10},{12... | collective-permute-start | bytes 4423688 | tf_op jit(solution)/shard_map/ppermute | solution.py:1052
  23.4 35.5 %collective-permute-start.2 = (bf16[3,10,3,64,128]{4,3,2,1,0:T(8,128)(2,1)}, bf16[3,10,3,64,128]{4,3,2,1,0:T(8,128)(2,1)S(1)}, u32[]{:S(2)}, u32[]{:S(2)}) collective-permute-start(bf16[3,10,3,64,128]{4,3,2,1,0:T(8,128)(2,1)} %get-tuple-element.29), channel_id=1, source_target_pairs={{8,0},{16,8},{24,16},{32,24},{40,32},{48,40},{56,48},{64,56},{72,6... | collective-permute-start | bytes 4423688 | tf_op jit(solution)/shard_map/ppermute | solution.py:1046
  24.7 32.2 %collective-permute-start.7 = (bf16[3,6,3,64,128]{4,3,2,1,0:T(8,128)(2,1)}, bf16[3,6,3,64,128]{4,3,2,1,0:T(8,128)(2,1)}, u32[]{:S(2)}, u32[]{:S(2)}) collective-permute-start(bf16[3,6,3,64,128]{4,3,2,1,0:T(8,128)(2,1)} %get-tuple-element.40), channel_id=1, source_target_pairs={{0,8},{8,16},{16,24},{24,32},{32,40},{40,48},{48,56},{56,64},{64,7... | collective-permute-start | bytes 2654216 | tf_op jit(solution)/shard_map/ppermute | solution.py:1047

commit v4 on v2

v4 whole, which is shorter than its diff:
```python
import functools

import jax
import jax.numpy as jnp
from jax import lax
from jax.experimental import pallas as pl
from jax.experimental.pallas import tpu as pltpu
from jax.sharding import PartitionSpec as P

F32 = jnp.float32
BF16 = jnp.bfloat16
MID, LOW, UPP, DIA, VOL, OUT = range(6)
NT = (((1,), (1,)), ((), ()))
MIB = 1024 * 1024
TOP = 1024.0
OWN_MIB = 20


def cover(start, length, cell, count, margin):
    places = start + jnp.arange(length, dtype=jnp.int32)
    base = jnp.floor_divide(places, cell)
    total = jnp.zeros((length,), jnp.int32)
    for step_off in (-1, 0, 1):
        owner = base + step_off
        inside = (
            (owner >= 0)
            & (owner < count)
            & (places >= owner * cell - margin)
            & (places < owner * cell + cell + margin)
        )
        total = total + inside.astype(jnp.int32)
    in_grid = (places >= 0) & (places < cell * count)
    safe = jnp.maximum(total, 1).astype(F32)
    return jnp.where(in_grid & (total > 0), 1.0 / safe, 0.0)


def neighbours(count):
    up = [(i, (i + 1) % count) for i in range(count)]
    return up, [(b, a) for a, b in up]


def spread3(w):
    return [w[0], w[0] + w[0] + w[1], w[0] + w[1] + w[1] + w[2]]


def cell_image(lines, values, rows):
    if values is None:
        return [-(rows[2] * lines[a]) for a in range(3)]
    total = rows[1] * (values[0] + values[1] + values[2])
    return [rows[0] * values[a] + total - rows[2] * lines[a] for a in range(3)]


def coef_rows(coef_ref, x, y, names):
    return [coef_ref[x, n, pl.ds(y, 1), :] for n in names]


def depth_sum(raw, rows):
    return (
        raw.astype(F32) * rows[0]
        + pltpu.roll(raw, 1, 1).astype(F32) * rows[1]
        + pltpu.roll(raw, 127, 1).astype(F32) * rows[2]
    )


def side(blocks):
    return jnp.concatenate(blocks, axis=1)


def fold(total):
    return total[:, :64] + total[:, 64:]


def fold_rows(total):
    return total[:64] + total[64:]


def pack_kernel(odd_ref, m_hbm, main_ref, corner_ref, south_ref, north_ref, sems):
    ext = m_hbm.shape[0]
    odd = odd_ref[0]
    here = jnp.where(odd == 1, ext - 3, 0)
    there = jnp.where(odd == 1, 0, ext - 3)
    copies = [
        pltpu.make_async_copy(m_hbm.at[pl.ds(here, 3)], main_ref, sems.at[0]),
        pltpu.make_async_copy(
            m_hbm.at[pl.ds(there, 3), pl.ds(0, 3)], corner_ref.at[:, pl.ds(0, 3)], sems.at[1]
        ),
        pltpu.make_async_copy(
            m_hbm.at[pl.ds(there, 3), pl.ds(ext - 3, 3)], corner_ref.at[:, pl.ds(3, 3)], sems.at[2]
        ),
        pltpu.make_async_copy(m_hbm.at[:, pl.ds(ext - 3, 3)], south_ref, sems.at[3]),
        pltpu.make_async_copy(m_hbm.at[:, pl.ds(0, 3)], north_ref, sems.at[4]),
    ]
    for copy in copies:
        copy.start()
    for copy in copies:
        copy.wait()


def gate_kernel(*refs):
    pass


def own_kernel(
    odd_ref, sx_ref, sy_ref, m_ref, mid_ref, lo_ref, hi_ref,
    out_ref, coef_ref, img_ref, q_ref, acc_ref,
):
    ext = m_ref.shape[0]
    frame = ext + 2
    odd = odd_ref[0]

    zero = jnp.zeros(q_ref.shape[1:], F32)
    for edge in (0, ext + 1):
        q_ref[edge] = zero

    lane = lax.broadcasted_iota(jnp.int32, (frame, 128), 1)
    place = lax.broadcasted_iota(jnp.int32, (frame, 128), 0)
    share_y = jnp.zeros((frame, 128), F32)
    for g in range(frame):
        share_y = jnp.where(place == g, sy_ref[g], share_y)

    def coefs(f, _):
        share = share_y * sx_ref[f]
        cen, cpl, vol = [
            jnp.concatenate([lo_ref[f, n], mid_ref[f, n], hi_ref[f, n]], axis=0) for n in range(3)
        ]
        kap = cpl * share
        vol = vol * share * share
        coef_ref[f, MID] = kap + kap
        coef_ref[f, LOW] = jnp.where(lane == 0, 0.0, pltpu.roll(kap, 1, 1))
        coef_ref[f, UPP] = jnp.where(lane == 127, 0.0, pltpu.roll(kap, 127, 1))
        coef_ref[f, DIA] = cen * share * share - vol + 0.5 * kap * kap
        coef_ref[f, VOL] = vol
        coef_ref[f, OUT] = kap * (1.0 / 16.0)
        return 0

    lax.fori_loop(0, frame, coefs, 0)

    def first(f, chunk):
        rows = pl.ds(pl.multiple_of(chunk * 16, 16), 16)
        kaps = [coef_rows(coef_ref, f, g, (MID, LOW, UPP)) for g in range(1, ext + 1)]
        for a in range(3):
            before = pair = None
            for j in range(ext):
                w = depth_sum(m_ref[f - 1, j * 3 + a, rows, :], kaps[j])
                if j == 0:
                    q_ref[f, 0, a, rows, :] = w
                    pair = w
                else:
                    now = before + w
                    q_ref[f, j, a, rows, :] = now + pair
                    pair = now
                before = w
            q_ref[f, ext, a, rows, :] = pair + before
            q_ref[f, ext + 1, a, rows, :] = before

    def image(f, chunk, edge, inward=None):
        rows = pl.ds(pl.multiple_of(chunk * 16, 16), 16)
        low_rows = pl.ds(pl.multiple_of(64 + chunk * 16, 16), 16)
        for g in range(frame):
            values = None
            if 1 <= g <= ext and not edge:
                values = [m_ref[f - 1, (g - 1) * 3 + a, rows, :].astype(F32) for a in range(3)]
            lines = []
            for a in range(3):
                if edge:
                    lines.append(q_ref[inward, g, a, rows, :])
                    continue
                mid = q_ref[f, g, a, rows, :]
                lines.append((q_ref[f - 1, g, a, rows, :] + mid) + (mid + q_ref[f + 1, g, a, rows, :]))
            result = cell_image(lines, values, coef_rows(coef_ref, f, g, (DIA, VOL, OUT)))
            for a in range(3):
                high = result[a].astype(BF16)
                lanes = pl.ds((g * 3 + a) * 128, 128)
                img_ref[f, rows, lanes] = high
                img_ref[f, low_rows, lanes] = (result[a] - high.astype(F32)).astype(BF16)

    def dot(f, chunk):
        base = jnp.minimum(chunk * 8, ext * 3 - 8)
        tiles = [m_ref[jnp.maximum(f - 1, 0), base + i] for i in range(8)]
        for i in range(2):
            tiles[i] = jnp.where(chunk == 3, jnp.zeros_like(tiles[i]), tiles[i])
        lanes = pl.ds(pl.multiple_of(base * 128 + 384, 128), 1024)
        acc_ref[...] += lax.dot_general(
            side(tiles), img_ref[f, :, lanes], NT, preferred_element_type=F32
        )

    def chunks(body):
        def step(chunk, _):
            body(chunk)
            return 0

        lax.fori_loop(0, 4, step, 0)

    chunks(lambda chunk: first(1, chunk))

    def inner(f, chunk):
        dot(f - 1, chunk)
        first(f + 1, chunk)
        image(f, chunk, False)

    def line(f, _):
        chunks(lambda chunk: inner(f, chunk))

        @pl.when(f == 1)
        def _():
            acc_ref[...] = jnp.zeros_like(acc_ref)

        return 0

    lax.fori_loop(1, ext, line, 0)

    def inner_last(chunk):
        dot(ext - 1, chunk)
        image(ext, chunk, False)

    chunks(inner_last)
    rim = jnp.where(odd == 1, 0, ext + 1)
    inward = jnp.where(odd == 1, 1, ext)

    def inner_rim(chunk):
        dot(ext, chunk)
        image(rim, chunk, True, inward)

    chunks(inner_rim)
    out_ref[...] = fold(acc_ref[...])


def rows_kernel(
    south_ref, north_ref, img_ref, coef_ref, out_ref, cimg_ref, z_ref, acc_ref
):
    ext = south_ref.shape[0]
    raw_refs = (south_ref, north_ref)
    acc_ref[...] = jnp.zeros_like(acc_ref)
    for s in range(2):
        r_ref = raw_refs[s]
        raw_y = (2, 1, 0) if s == 0 else (0, 1, 2)
        raw_g = (2, 1, 0) if s == 0 else (9, 10, 11)
        img_g = (3, 2, 1) if s == 0 else (8, 9, 10)
        img_y = (2, 1, 0) if s == 0 else (0, 1, 2)
        for t in range(2):
            raw_x = (0, 1, 2) if t == 0 else (9, 8, 7)
            raw_f = (1, 2, 3) if t == 0 else (10, 9, 8)
            img_f = (0, 1, 2) if t == 0 else (11, 10, 9)
            img_x = (0, 1, 2) if t == 0 else (2, 1, 0)

            def chunked(chunk, _, s=s, t=t, r_ref=r_ref, raw_x=raw_x, raw_f=raw_f, img_f=img_f, img_x=img_x):
                rows = pl.ds(pl.multiple_of(chunk * 16, 16), 16)
                low_rows = pl.ds(pl.multiple_of(64 + chunk * 16, 16), 16)
                for a in range(3):
                    across = []
                    for c in range(3):
                        w = [
                            depth_sum(
                                r_ref[raw_x[c], raw_y[d], a, rows, :],
                                coef_rows(coef_ref, raw_f[c], raw_g[d], (MID, LOW, UPP)),
                            )
                            for d in range(3)
                        ]
                        across.append(spread3(w))
                    for e in range(3):
                        for c, value in enumerate(spread3([across[i][e] for i in range(3)])):
                            z_ref[c, e, a] = value
                for c in range(3):
                    for e in range(3):
                        values = None
                        if c > 0 and e > 0:
                            values = [
                                r_ref[raw_x[c - 1], raw_y[e - 1], a, rows, :].astype(F32)
                                for a in range(3)
                            ]
                        image = cell_image(
                            [z_ref[c, e, a] for a in range(3)], values,
                            coef_rows(coef_ref, img_f[c], img_g[e], (DIA, VOL, OUT)),
                        )
                        for a in range(3):
                            high = image[a].astype(BF16)
                            low = (image[a] - high.astype(F32)).astype(BF16)
                            lanes = pl.ds(((img_x[c] * 3 + img_y[e]) * 3 + a) * 128, 128)
                            cimg_ref[t, s, rows, lanes] = high
                            cimg_ref[t, s, low_rows, lanes] = low
                return 0

            lax.fori_loop(0, 4, chunked, 0)
    for s in range(2):

        def dots(x, _, s=s):
            right = side([raw_refs[s][x, j, a] for j in range(3) for a in range(3)])
            lines = img_ref[x + 1, :, pl.ds(s * (ext - 1) * 384, 1152)]
            acc_ref[s] += lax.dot_general(lines, right, NT, preferred_element_type=F32)
            return 0

        lax.fori_loop(0, ext, dots, 0)
    out_ref[...] = side([fold_rows(acc_ref[0]), fold_rows(acc_ref[1])])


def masked(there, block):
    return jnp.where(there, block, jnp.zeros_like(block))


def corner_dot(raw, img):
    left = side([raw(i, j, a) for i in range(3) for j in range(3) for a in range(3)])
    return fold(lax.dot_general(left, img, NT, preferred_element_type=F32))


def other_kernel(odd_ref, there_ref, corner_ref, cimg_ref, own_ref, rows_ref, out_ref, keep_ref):
    t = odd_ref[0]
    low, high = there_ref[0] == 1, there_ref[1] == 1
    beside = there_ref[3] == 1
    south = corner_dot(lambda i, j, a: corner_ref[i, j, a], cimg_ref[t, 0])
    north = corner_dot(lambda i, j, a: corner_ref[i, j + 3, a], cimg_ref[t, 1])
    around = rows_ref[...]
    out_ref[...] = side(
        [
            own_ref[...], masked(high, around[:, 64:]), masked(low & beside, south),
            masked(low, around[:, :64]),
        ]
    )
    keep_ref[...] = masked(high & beside, north)


def main_kernel(odd_ref, there_ref, main_ref, img_ref, cimg_ref, early_ref, keep_ref, out_ref):
    t = 1 - odd_ref[0]
    ext = main_ref.shape[1]
    start = jnp.where(odd_ref[0] == 1, 0, ext - 1)
    total = None
    for i in range(3):
        right = side([main_ref[i, j, a] for j in range(ext) for a in range(3)])
        lines = img_ref[start + i, :, pl.ds(384, ext * 384)]
        part = lax.dot_general(lines, right, NT, preferred_element_type=F32)
        total = part if total is None else total + part
    south = corner_dot(lambda i, j, a: main_ref[i, j, a], cimg_ref[t, 0])
    north = corner_dot(lambda i, j, a: main_ref[i, ext - 3 + j, a], cimg_ref[t, 1])
    low, high = there_ref[0] == 1, there_ref[1] == 1
    beside = there_ref[2] == 1
    blocks = [
        masked(low & beside, south), masked(beside, fold_rows(total)), masked(high & beside, north)
    ]
    code = encode(side([early_ref[...]] + blocks + [keep_ref[...]]))
    for p in range(out_ref.shape[0]):
        out_ref[p] = code


def encode(rows):
    top = jnp.max(jnp.abs(rows), axis=(0, 1), keepdims=True)
    top = jnp.where(top > 0.0, jnp.maximum(top * 1.01, 2.0**-100), 1.0).astype(BF16).astype(F32)
    value = rows * (TOP / top)
    value2 = value * value
    value4 = value2 * value2
    power = value4 * value4 * value4
    code = jnp.where(rows < 0.0, -power, power)
    row = lax.broadcasted_iota(jnp.int32, rows.shape, 0)
    lane = lax.broadcasted_iota(jnp.int32, rows.shape, 1)
    return jnp.where((row == 0) & (lane == 1), top, code).astype(BF16)


def decode(code):
    value = code.astype(F32)
    first = value[:8, :128]
    row = lax.broadcasted_iota(jnp.int32, first.shape, 0)
    lane = lax.broadcasted_iota(jnp.int32, first.shape, 1)

    def pick(tile, i, j):
        return jnp.sum(jnp.where((row == i) & (lane == j), tile, 0.0), axis=(0, 1), keepdims=True)

    scale = pick(first, 0, 1) * (1.0 / TOP)
    root = jnp.exp(jnp.log(jnp.abs(value)) * (1.0 / 12.0)) * scale
    root = jnp.where(value < 0.0, -root, root)
    head = root[:8, :128]
    head = jnp.where((row == 0) & (lane == 1), pick(head, 1, 0), head)
    return root, head


def final_kernel(odd_ref, code_ref, out_hbm, e_ref, l_ref, o_ref, out_sems):
    odd = odd_ref[0]
    none = jnp.zeros(e_ref.shape[1:], F32)
    for ref in (e_ref, l_ref):
        ref[0] = none
        ref[17] = none

    def read(p, _):
        root, head = decode(code_ref[p])
        e_ref[p + 1] = root[:, :256]
        l_ref[p + 1] = root[:, 256:]
        e_ref[p + 1, pl.ds(0, 8), pl.ds(0, 128)] = head
        return 0

    lax.fori_loop(0, 16, read, 0, unroll=2)

    def put(p):
        return pltpu.make_async_copy(o_ref.at[p], out_hbm.at[p], out_sems.at[p])

    low = lax.broadcasted_iota(jnp.int32, (64, 128), 1) < 64

    def turned(tile):
        return jnp.transpose(jnp.concatenate([tile, tile], axis=0))[64:]

    def join(lower, upper):
        return jnp.where(low, lower, upper)

    def tiles(ref, p):
        return ref[p, :, pl.ds(0, 128)], ref[p, :, pl.ds(128, 128)]

    def even(p, _):
        (e_one, e_two), (_, e_after) = tiles(e_ref, p + 1), tiles(e_ref, p + 2)
        (b_one, b_two), (l_one, _), (_, l_after) = [tiles(l_ref, p + i) for i in range(3)]
        o_ref[p, :, pl.ds(0, 512)] = side(
            [join(b_one, turned(b_one)), join(b_two, e_two), e_one, join(e_after, l_one)]
        )
        o_ref[p, :, pl.ds(512, 64)] = l_after[:, 64:]
        put(p).start()
        return 0

    def uneven(p, _):
        (_, e_before), (e_one, e_two) = tiles(e_ref, p), tiles(e_ref, p + 1)
        (_, b_two), (l_one, _), (a_one, a_two) = [tiles(l_ref, p + i) for i in range(3)]
        o_ref[p, :, pl.ds(0, 512)] = side(
            [
                join(e_before, l_one), join(pltpu.roll(b_two, 64, 1), e_two), e_one,
                join(a_one, turned(a_one)),
            ]
        )
        o_ref[p, :, pl.ds(512, 64)] = a_two[:, :64]
        put(p).start()
        return 0

    @pl.when(odd == 0)
    def _():
        lax.fori_loop(0, 16, even, 0)

    @pl.when(odd == 1)
    def _():
        lax.fori_loop(0, 16, uneven, 0)

    for p in range(16):
        put(p).wait()


def any_spec():
    return pl.BlockSpec(memory_space=pl.ANY)


def vmem_spec():
    return pl.BlockSpec(memory_space=pltpu.VMEM)


def smem_spec():
    return pl.BlockSpec(memory_space=pltpu.SMEM)


def shape(*dims, dtype=F32):
    return jax.ShapeDtypeStruct(dims, dtype)


def call(kernel, out_shape, in_specs, out_specs, scratch, mib, name):
    return pl.pallas_call(
        kernel,
        out_shape=out_shape,
        in_specs=in_specs,
        out_specs=out_specs,
        scratch_shapes=scratch,
        compiler_params=pltpu.CompilerParams(vmem_limit_bytes=mib * MIB),
        cost_estimate=pl.CostEstimate(flops=1000, bytes_accessed=1000, transcendentals=0),
        name=name,
    )


def gate(values, others):
    count = len(values)
    return pl.pallas_call(
        gate_kernel,
        out_shape=[shape(*x.shape, dtype=x.dtype) for x in values],
        in_specs=[any_spec()] * (count + len(others)),
        out_specs=[any_spec()] * count,
        input_output_aliases={i: i for i in range(count)},
        compiler_params=pltpu.CompilerParams(vmem_limit_bytes=MIB),
        name="gate",
    )(*values, *others)


def coef_columns(centre, coupling, volume):
    own = jnp.stack([centre, coupling, volume], axis=1)
    up, down = neighbours(lax.axis_size("sx"))
    low = lax.ppermute(own[-2:], "sx", up)
    high = lax.ppermute(own[:2], "sx", down)
    return jnp.concatenate([low, own, high], axis=0)


def coef_edges(mid):
    up, down = neighbours(lax.axis_size("sy"))
    lo = lax.ppermute(mid[:, :, -2:], "sy", up)
    hi = lax.ppermute(mid[:, :, :2], "sy", down)
    return lo, hi


def local(modes, centre, coupling, volume):
    ext = modes.shape[0]
    cell = centre.shape[0]
    margin = (ext - cell) // 2
    nx = lax.axis_size("sx")
    ny = lax.axis_size("sy")
    ix = lax.axis_index("sx")
    iy = lax.axis_index("sy")
    odd = lax.rem(iy, 2).astype(jnp.int32).reshape(1)
    share_x = cover(ix * cell - margin - 1, ext + 2, cell, nx, margin)
    share_y = cover(iy * cell - margin - 1, ext + 2, cell, ny, margin)
    first_x, last_x = ix > 0, ix < nx - 1
    is_odd = odd[0] == 1
    there = jnp.stack(
        [
            iy > 0, iy < ny - 1, jnp.where(is_odd, first_x, last_x),
            jnp.where(is_odd, last_x, first_x),
        ]
    ).astype(jnp.int32)
    mid = coef_columns(centre, coupling, volume)
    m = jnp.transpose(modes, (0, 1, 3, 2, 4))
    frame = ext + 2

    main, corner, south, north = call(
        pack_kernel,
        [
            shape(3, ext, 3, 64, 128, dtype=BF16),
            shape(3, 6, 3, 64, 128, dtype=BF16),
            shape(ext, 3, 3, 64, 128, dtype=BF16),
            shape(ext, 3, 3, 64, 128, dtype=BF16),
        ],
        [smem_spec(), vmem_spec()],
        [vmem_spec()] * 4,
        [pltpu.SemaphoreType.DMA((5,))],
        8,
        "pack",
    )(odd, m)
    main, corner, south, north, mid = gate((main, corner, south, north, mid), ())
    main_pairs, other_pairs = [], []
    for y in range(ny):
        for x in range(nx):
            lower, higher = x * ny + y, (x + 1) % nx * ny + y
            main_pairs.append((higher, lower) if y % 2 == 0 else (lower, higher))
            other_pairs.append((lower, higher) if y % 2 == 0 else (higher, lower))
    main = lax.ppermute(main, ("sx", "sy"), main_pairs)
    corner = lax.ppermute(corner, ("sx", "sy"), other_pairs)
    lo, hi = coef_edges(mid)
    south, north = gate((south, north), (lo, hi))
    up, down = neighbours(ny)
    south = lax.ppermute(south, "sy", up)
    north = lax.ppermute(north, "sy", down)

    own, coef, img = call(
        own_kernel,
        [
            shape(64, 64),
            shape(frame, 6, frame, 128),
            shape(frame, 128, frame * 384, dtype=BF16),
        ],
        [smem_spec()] * 3 + [vmem_spec()] * 4,
        [vmem_spec()] * 3,
        [
            pltpu.VMEM((frame, frame, 3, 64, 128), F32),
            pltpu.VMEM((64, 128), F32),
        ],
        OWN_MIB,
        "own_gram",
    )(odd, share_x, share_y, m.reshape(ext, ext * 3, 64, 128), mid, lo, hi)
    around, cimg = call(
        rows_kernel,
        [shape(64, 128), shape(2, 2, 128, 3456, dtype=BF16)],
        [vmem_spec()] * 4,
        [vmem_spec(), vmem_spec()],
        [
            pltpu.VMEM((3, 3, 3, 16, 128), F32),
            pltpu.VMEM((2, 128, 64), F32),
        ],
        24,
        "row_gram",
    )(south, north, img, coef)
    early, keep = call(
        other_kernel,
        [shape(64, 256), shape(64, 64)],
        [smem_spec()] * 2 + [vmem_spec()] * 4,
        [vmem_spec()] * 2,
        [],
        10,
        "corner_gram",
    )(odd, there, corner, cimg, own, around)
    code = call(
        main_kernel,
        shape(nx, 64, 512, dtype=BF16),
        [smem_spec()] * 2 + [vmem_spec()] * 5,
        vmem_spec(),
        [],
        28,
        "column_gram",
    )(odd, there, main, img, cimg, early, keep)
    code = lax.all_to_all(code, "sx", 0, 0)
    out = call(
        final_kernel,
        shape(nx, 64, 576),
        [smem_spec(), vmem_spec()],
        any_spec(),
        [
            pltpu.VMEM((nx + 2, 64, 256), F32),
            pltpu.VMEM((nx + 2, 64, 256), F32),
            pltpu.VMEM((nx, 64, 576), F32),
            pltpu.SemaphoreType.DMA((nx,)),
        ],
        12,
        "assemble",
    )(odd, code)
    return out[None]


def solution(mesh):
    in_specs = (
        P("sx", "sy", None, None, None),
        P("sx", "sy", None),
        P("sx", "sy", None),
        P("sx", "sy", None),
    )
    out_specs = P("sy", None, None, None)
    return jax.shard_map(local, mesh=mesh, in_specs=in_specs, out_specs=out_specs, check_vma=False)
```

time: 111 us -> 84.3 us (0.76)
  the two profiles are of different devices: /device:TPU:1 before, /device:TPU:24 now
where the time goes in v4:
time: 84.3 us; the launch traced here: 83.6 us
  Pallas kernels  39.2 us (47%)
  blocking collectives  24.5 us (29%)
  starting transfers between devices  11.2 us (13%)
  local copies, waits for them, and re-layouts  4.82 us (6%)
  waiting for transfers between devices  2.91 us (3%)
  other arithmetic  0.9 us (1%)
    all_to_all x1, blocking collectives, local(): code = lax.all_to_all(code, 'sx', 0, 0)  24.5 us
    pallas_call x1, Pallas kernels, local(): call(own_kernel, [shape(64, 64), shape(frame, 6, frame, 128), shape(frame...  16.4 us
    pallas_call x1, Pallas kernels, local(): call(rows_kernel, [shape(64, 128), shape(2, 2, 128, 3456, dtype=BF16)], [...  9.65 us
    pallas_call x1, Pallas kernels, local(): call(final_kernel, shape(nx, 64, 576), [smem_spec(), vmem_spec()], any_sp...  5.87 us
    ppermute x1, starting transfers between devices, coef_columns(): high = lax.ppermute(own[:2], 'sx', down)  4.82 us
    unnamed x10, local copies, waits for them, and re-layouts  4.79 us
    pallas_call x1, Pallas kernels, local(): call(main_kernel, shape(nx, 64, 512, dtype=BF16), [smem_spec()] * 2 + [vm...  3.17 us
    ppermute x1, starting transfers between devices, local(): main = lax.ppermute(main, ('sx', 'sy'), main_pairs)  2.54 us
  transfers between devices with their start and end apart: 8, of which 2 were waited for; matrix products, arithmetic and copies ran while one was open for 0% of the time, Pallas kernels for 36%

profile of v4, /device:TPU:24, one launch (start us, length us, event | category | flops | bytes accessed | tf_op | source)
XLA Modules:
  0.0 83.6 jit_solution(17667272812817821071)
XLA Ops:
  0.0 0.8 pad_maximum_fusion.3
  0.8 1.5 %collective-permute-start = (f32[2,3,8,128]{3,2,1,0:T(8,128)S(1)}, f32[2,3,8,128]{3,2,1,0:T(8,128)S(1)}, u32[]{:S(2)}, u32[]{:S(2)}) collective-permute-start(f32[2,3,8,128]{3,2,1,0:T(8,128)S(1)} %get-tuple-element.43), channel_id=1, source_target_pairs={{0,8},{8,16},{16,24},{24,32},{32,40},{40,48},{48,56},{56,64},{64,7... | collective-permute-start | bytes 73736 | tf_op jit(solution)/shard_map/ppermute | solution.py:483
  2.3 4.8 %collective-permute-start.1 = (f32[2,3,8,128]{3,2,1,0:T(8,128)S(1)}, f32[2,3,8,128]{3,2,1,0:T(8,128)S(1)}, u32[]{:S(2)}, u32[]{:S(2)}) collective-permute-start(f32[2,3,8,128]{3,2,1,0:T(8,128)S(1)} %get-tuple-element.44), channel_id=1, source_target_pairs={{8,0},{16,8},{24,16},{32,24},{40,32},{48,40},{56,48},{64,56},{72,6... | collective-permute-start | bytes 73736 | tf_op jit(solution)/shard_map/ppermute | solution.py:484
  7.1 0.0 copy-start
  7.1 2.4 %copy-done = bf16[10,10,64,3,128]{4,2,3,1,0:T(8,128)(2,1)S(1)} copy-done((bf16[10,10,64,3,128]{4,2,3,1,0:T(8,128)(2,1)S(1)}, bf16[10,10,64,3,128]{4,2,3,1,0:T(8,128)(2,1)}, u32[]{:S(2)}) %copy-start) | copy-done | bytes 4915224
  9.5 0.0 copy-start.2
  9.5 0.0 copy-start.3
  9.5 0.0 copy-start.4
  9.5 2.2 %pack.1 = (bf16[3,10,3,64,128]{4,3,2,1,0:T(8,128)(2,1)}, bf16[3,6,3,64,128]{4,3,2,1,0:T(8,128)(2,1)}, bf16[10,3,3,64,128]{4,3,2,1,0:T(8,128)(2,1)S(1)}, bf16[10,3,3,64,128]{4,3,2,1,0:T(8,128)(2,1)S(1)}) custom-call(s32[1]{0:T(128)} %bitcast.odd_ref, bf16[10,10,3,64,128]{4,3,2,1,0:T(8,128)(2,1)S(1)} %bitcast.12), custom_call_target="tpu_custom_call" | custom-call | flops 1000 | bytes 1000 | tf_op jit(solution)/shard_map/pack/pallas_call | solution.py:518
  11.7 0.0 collective-permute-done
  11.7 0.0 collective-permute-done.1
  11.7 0.0 copy-done.2
  11.7 0.0 copy-done.3
  11.7 0.0 copy-done.4
  11.8 0.0 collective-permute-start.4
  11.8 0.5 collective-permute-start.3
  12.3 1.1 %collective-permute-done.4.hi_ref.refs_3_ = f32[12,3,2,128]{3,2,1,0:T(2,128)S(1)} collective-permute-done((f32[12,3,2,128]{3,2,1,0:T(2,128)S(1)}, f32[12,3,2,128]{3,2,1,0:T(2,128)S(1)}, u32[]{:S(2)}, u32[]{:S(2)}) %collective-permute-start.4) | collective-permute-done | bytes 36896 | tf_op jit(solution)/shard_map/ppermute | solution.py:491
  13.5 1.8 %collective-permute-done.3.lo_ref.refs_2_ = f32[12,3,2,128]{3,2,1,0:T(2,128)S(1)} collective-permute-done((f32[12,3,2,128]{3,2,1,0:T(2,128)S(1)}, f32[12,3,2,128]{3,2,1,0:T(2,128)S(1)}, u32[]{:S(2)}, u32[]{:S(2)}) %collective-permute-start.3) | collective-permute-done | bytes 36896 | tf_op jit(solution)/shard_map/ppermute | solution.py:490
  15.2 0.7 collective-permute-start.5
  16.0 1.0 %collective-permute-start.6 = (bf16[10,3,3,64,128]{4,3,2,1,0:T(8,128)(2,1)S(1)}, bf16[10,3,3,64,128]{4,3,2,1,0:T(8,128)(2,1)}, u32[]{:S(2)}, u32[]{:S(2)}) collective-permute-start(bf16[10,3,3,64,128]{4,3,2,1,0:T(8,128)(2,1)S(1)} %get-tuple-element.33), channel_id=1, source_target_pairs={{1,0},{2,1},{3,2},{4,3},{5,4},{6,5},{7,6},{0,7},{9,8},{10,9},{11,1... | collective-permute-start | bytes 4423688 | tf_op jit(solution)/shard_map/ppermute | solution.py:545
  17.0 2.5 %collective-permute-start.2 = (bf16[3,10,3,64,128]{4,3,2,1,0:T(8,128)(2,1)}, bf16[3,10,3,64,128]{4,3,2,1,0:T(8,128)(2,1)}, u32[]{:S(2)}, u32[]{:S(2)}) collective-permute-start(bf16[3,10,3,64,128]{4,3,2,1,0:T(8,128)(2,1)} %get-tuple-element.27), channel_id=1, source_target_pairs={{8,0},{16,8},{24,16},{32,24},{40,32},{48,40},{56,48},{64,56},{72,6... | collective-permute-start | bytes 4423688 | tf_op jit(solution)/shard_map/ppermute | solution.py:539
  19.5 0.0 collective-permute-start.7
  19.5 0.1 add_convert_fusion.there_ref
  19.6 0.0 copy-start.1
  19.7 2.4 %copy-done.1 = bf16[10,10,64,3,128]{4,2,3,1,0:T(8,128)(2,1)S(1)} copy-done((bf16[10,10,64,3,128]{4,2,3,1,0:T(8,128)(2,1)S(1)}, bf16[10,10,64,3,128]{4,2,3,1,0:T(8,128)(2,1)}, u32[]{:S(2)}) %copy-start.1) | copy-done | bytes 4915224
  22.0 16.4 %own_gram.1 = (f32[64,64]{1,0:T(8,128)S(1)}, f32[12,6,12,128]{3,2,1,0:T(8,128)S(1)}, bf16[12,128,4608]{2,1,0:T(8,128)(2,1)S(1)}) custom-call(s32[1]{0:T(128)} %bitcast.odd_ref, f32[12]{0:T(128)S(1)} %get-tuple-element.46.sx_ref, f32[12]{0:T(128)S(1)} %get-tuple-element.45.sy_ref, bf16[10,30,64,128]{3,2,1,0:T(8,128)(2,1)S(1)} %bitcast.13, ...), custom_call_target="tpu_custom_call" | custom-call | flops 1000 | bytes 1000 | tf_op jit(solution)/shard_map/own_gram/pallas_call | solution.py:547
  38.4 0.0 collective-permute-done.5.south_ref
  38.5 0.0 collective-permute-done.6.north_ref
  38.5 9.6 %row_gram.1 = (f32[64,128]{1,0:T(8,128)S(1)}, bf16[2,2,128,3456]{3,2,1,0:T(8,128)(2,1)S(1)}) custom-call(bf16[10,3,3,64,128]{4,3,2,1,0:T(8,128)(2,1)} %collective-permute-done.5.south_ref, bf16[10,3,3,64,128]{4,3,2,1,0:T(8,128)(2,1)} %collective-permute-done.6.north_ref, bf16[12,128,4608]{2,1,0:T(8,128)(2,1)S(1)} %get-tuple-element.29.img_ref, ...), custom_call_target="tpu_custom_call" | custom-call | flops 1000 | bytes 1000 | tf_op jit(solution)/shard_map/row_gram/pallas_call | solution.py:563
  48.1 0.0 collective-permute-done.7.corner_ref
  48.1 2.0 %corner_gram.1 = (f32[64,256]{1,0:T(8,128)S(1)}, f32[64,64]{1,0:T(8,128)S(1)}) custom-call(s32[1]{0:T(128)} %bitcast.odd_ref, s32[4]{0:T(128)S(1)} %add_convert_fusion.there_ref, bf16[3,6,3,64,128]{4,3,2,1,0:T(8,128)(2,1)} %collective-permute-done.7.corner_ref, bf16[2,2,128,3456]{3,2,1,0:T(8,128)(2,1)S(1)} %get-tuple-element.35.cimg_ref, ...), custom_call_target="tpu_custom_call" | custom-call | flops 1000 | bytes 1000 | tf_op jit(solution)/shard_map/corner_gram/pallas_call | solution.py:575
  50.1 0.0 collective-permute-done.2.main_ref
  50.1 3.2 %column_gram.1 = bf16[16,64,512]{2,1,0:T(8,128)(2,1)S(1)} custom-call(s32[1]{0:T(128)} %bitcast.odd_ref, s32[4]{0:T(128)S(1)} %add_convert_fusion.there_ref, bf16[3,10,3,64,128]{4,3,2,1,0:T(8,128)(2,1)} %collective-permute-done.2.main_ref, bf16[12,128,4608]{2,1,0:T(8,128)(2,1)S(1)} %get-tuple-element.29.img_ref, ...), custom_call_target="tpu_custom_call" | custom-call | flops 1000 | bytes 1000 | tf_op jit(solution)/shard_map/column_gram/pallas_call | solution.py:584
  53.3 24.5 %all_to_all.5.code_ref = bf16[16,64,512]{2,1,0:T(8,128)(2,1)S(1)} all-to-all(bf16[16,64,512]{2,1,0:T(8,128)(2,1)S(1)} %column_gram.1), channel_id=1, replica_groups=mesh['sx'=16,'sy'=8] {'sx'}, dimensions={0} | all-to-all | bytes 2097152 | tf_op jit(solution)/shard_map/all_to_all | solution.py:593
  77.8 5.9 %assemble.1 = f32[16,64,576]{2,1,0:T(8,128)} custom-call(s32[1]{0:T(128)} %bitcast.odd_ref, bf16[16,64,512]{2,1,0:T(8,128)(2,1)S(1)} %all_to_all.5.code_ref), custom_call_target="tpu_custom_call" | custom-call | flops 1000 | bytes 1000 | tf_op jit(solution)/shard_map/assemble/pallas_call | solution.py:594
  (5 shorter events, 0.1 us)
Async XLA Ops:
  0.8 10.9 %collective-permute-start = (f32[2,3,8,128]{3,2,1,0:T(8,128)S(1)}, f32[2,3,8,128]{3,2,1,0:T(8,128)S(1)}, u32[]{:S(2)}, u32[]{:S(2)}) collective-permute-start(f32[2,3,8,128]{3,2,1,0:T(8,128)S(1)} %get-tuple-element.43), channel_id=1, source_target_pairs={{0,8},{8,16},{16,24},{24,32},{32,40},{40,48},{48,56},{56,64},{64,7... | collective-permute-start | bytes 73736 | tf_op jit(solution)/shard_map/ppermute | solution.py:483
  2.3 9.4 %collective-permute-start.1 = (f32[2,3,8,128]{3,2,1,0:T(8,128)S(1)}, f32[2,3,8,128]{3,2,1,0:T(8,128)S(1)}, u32[]{:S(2)}, u32[]{:S(2)}) collective-permute-start(f32[2,3,8,128]{3,2,1,0:T(8,128)S(1)} %get-tuple-element.44), channel_id=1, source_target_pairs={{8,0},{16,8},{24,16},{32,24},{40,32},{48,40},{56,48},{64,56},{72,6... | collective-permute-start | bytes 73736 | tf_op jit(solution)/shard_map/ppermute | solution.py:484
  7.1 2.4 %copy-start = (bf16[10,10,64,3,128]{4,2,3,1,0:T(8,128)(2,1)S(1)}, bf16[10,10,64,3,128]{4,2,3,1,0:T(8,128)(2,1)}, u32[]{:S(2)}) copy-start(bf16[10,10,64,3,128]{4,2,3,1,0:T(8,128)(2,1)} %param.4) | copy-start | bytes 14745604
  9.5 2.2 %copy-start.2 = (f32[8,8,128]{2,1,0:T(8,128)S(1)}, f32[8,8,128]{2,1,0:T(8,128)}, u32[]{:S(2)}) copy-start(f32[8,8,128]{2,1,0:T(8,128)} %param.7) | copy-start | bytes 98308
  9.5 2.2 %copy-start.3 = (f32[8,8,128]{2,1,0:T(8,128)S(1)}, f32[8,8,128]{2,1,0:T(8,128)}, u32[]{:S(2)}) copy-start(f32[8,8,128]{2,1,0:T(8,128)} %param.6) | copy-start | bytes 98308
  9.5 2.2 %copy-start.4 = (f32[8,8,128]{2,1,0:T(8,128)S(1)}, f32[8,8,128]{2,1,0:T(8,128)}, u32[]{:S(2)}) copy-start(f32[8,8,128]{2,1,0:T(8,128)} %param.5) | copy-start | bytes 98308
  11.8 1.7 %collective-permute-start.4 = (f32[12,3,2,128]{3,2,1,0:T(2,128)S(1)}, f32[12,3,2,128]{3,2,1,0:T(2,128)S(1)}, u32[]{:S(2)}, u32[]{:S(2)}) collective-permute-start(f32[12,3,2,128]{3,2,1,0:T(2,128)S(1)} %get-tuple-element.41), channel_id=1, source_target_pairs={{1,0},{2,1},{3,2},{4,3},{5,4},{6,5},{7,6},{0,7},{9,8},{10,9},{11,1... | collective-permute-start | bytes 110600 | tf_op jit(solution)/shard_map/ppermute | solution.py:491
  11.8 3.4 %collective-permute-start.3 = (f32[12,3,2,128]{3,2,1,0:T(2,128)S(1)}, f32[12,3,2,128]{3,2,1,0:T(2,128)S(1)}, u32[]{:S(2)}, u32[]{:S(2)}) collective-permute-start(f32[12,3,2,128]{3,2,1,0:T(2,128)S(1)} %get-tuple-element.42), channel_id=1, source_target_pairs={{0,1},{1,2},{2,3},{3,4},{4,5},{5,6},{6,7},{7,0},{8,9},{9,10},{10,1... | collective-permute-start | bytes 110600 | tf_op jit(solution)/shard_map/ppermute | solution.py:490
  15.2 23.2 %collective-permute-start.5 = (bf16[10,3,3,64,128]{4,3,2,1,0:T(8,128)(2,1)S(1)}, bf16[10,3,3,64,128]{4,3,2,1,0:T(8,128)(2,1)}, u32[]{:S(2)}, u32[]{:S(2)}) collective-permute-start(bf16[10,3,3,64,128]{4,3,2,1,0:T(8,128)(2,1)S(1)} %get-tuple-element.32), channel_id=1, source_target_pairs={{0,1},{1,2},{2,3},{3,4},{4,5},{5,6},{6,7},{7,0},{8,9},{9,10},{10,1... | collective-permute-start | bytes 4423688 | tf_op jit(solution)/shard_map/ppermute | solution.py:544
  16.0 22.5 %collective-permute-start.6 = (bf16[10,3,3,64,128]{4,3,2,1,0:T(8,128)(2,1)S(1)}, bf16[10,3,3,64,128]{4,3,2,1,0:T(8,128)(2,1)}, u32[]{:S(2)}, u32[]{:S(2)}) collective-permute-start(bf16[10,3,3,64,128]{4,3,2,1,0:T(8,128)(2,1)S(1)} %get-tuple-element.33), channel_id=1, source_target_pairs={{1,0},{2,1},{3,2},{4,3},{5,4},{6,5},{7,6},{0,7},{9,8},{10,9},{11,1... | collective-permute-start | bytes 4423688 | tf_op jit(solution)/shard_map/ppermute | solution.py:545
  17.0 33.1 %collective-permute-start.2 = (bf16[3,10,3,64,128]{4,3,2,1,0:T(8,128)(2,1)}, bf16[3,10,3,64,128]{4,3,2,1,0:T(8,128)(2,1)}, u32[]{:S(2)}, u32[]{:S(2)}) collective-permute-start(bf16[3,10,3,64,128]{4,3,2,1,0:T(8,128)(2,1)} %get-tuple-element.27), channel_id=1, source_target_pairs={{8,0},{16,8},{24,16},{32,24},{40,32},{48,40},{56,48},{64,56},{72,6... | collective-permute-start | bytes 4423688 | tf_op jit(solution)/shard_map/ppermute | solution.py:539
  19.5 28.6 %collective-permute-start.7 = (bf16[3,6,3,64,128]{4,3,2,1,0:T(8,128)(2,1)}, bf16[3,6,3,64,128]{4,3,2,1,0:T(8,128)(2,1)}, u32[]{:S(2)}, u32[]{:S(2)}) collective-permute-start(bf16[3,6,3,64,128]{4,3,2,1,0:T(8,128)(2,1)} %get-tuple-element.36), channel_id=1, source_target_pairs={{0,8},{8,16},{16,24},{24,32},{32,40},{40,48},{48,56},{56,64},{64,7... | collective-permute-start | bytes 2654216 | tf_op jit(solution)/shard_map/ppermute | solution.py:540
  19.6 2.4 %copy-start.1 = (bf16[10,10,64,3,128]{4,2,3,1,0:T(8,128)(2,1)S(1)}, bf16[10,10,64,3,128]{4,2,3,1,0:T(8,128)(2,1)}, u32[]{:S(2)}) copy-start(bf16[10,10,64,3,128]{4,2,3,1,0:T(8,128)(2,1)} %param.4) | copy-start | bytes 14745604

commit v5 on v4

v5 whole, which is shorter than its diff:
```python
import functools

import jax
import jax.numpy as jnp
from jax import lax
from jax.experimental import pallas as pl
from jax.experimental.pallas import tpu as pltpu
from jax.sharding import PartitionSpec as P

F32 = jnp.float32
BF16 = jnp.bfloat16
MID, LOW, UPP, DIA, VOL, OUT = range(6)
NT = (((1,), (1,)), ((), ()))
MIB = 1024 * 1024
TOP = 1024.0
OWN_MIB = 10


def cover(local, index, cell, count, margin):
    places = index * cell + local
    base = index + (local >= cell).astype(jnp.int32) - (local < 0).astype(jnp.int32)
    total = jnp.zeros(local.shape, jnp.int32)
    for step_off in (-1, 0, 1):
        owner = base + step_off
        inside = (
            (owner >= 0)
            & (owner < count)
            & (places >= owner * cell - margin)
            & (places < owner * cell + cell + margin)
        )
        total = total + inside.astype(jnp.int32)
    in_grid = (places >= 0) & (places < cell * count)
    safe = jnp.maximum(total, 1).astype(F32)
    return jnp.where(in_grid & (total > 0), 1.0 / safe, 0.0)


def is_odd():
    return lax.rem(lax.axis_index("sy"), 2) == 1


def has_y(step):
    place = lax.axis_index("sy") + step
    return (place >= 0) & (place < lax.axis_size("sy"))


def has_x(main):
    step = jnp.where(is_odd() == main, -1, 1)
    place = lax.axis_index("sx") + step
    return (place >= 0) & (place < lax.axis_size("sx"))


def neighbours(count):
    up = [(i, (i + 1) % count) for i in range(count)]
    return up, [(b, a) for a, b in up]


def spread3(w):
    return [w[0], w[0] + w[0] + w[1], w[0] + w[1] + w[1] + w[2]]


def cell_image(lines, values, rows):
    if values is None:
        return [-(rows[2] * lines[a]) for a in range(3)]
    total = rows[1] * (values[0] + values[1] + values[2])
    return [rows[0] * values[a] + total - rows[2] * lines[a] for a in range(3)]


def coef_rows(coef_ref, x, y, names):
    return [coef_ref[x, n, pl.ds(y, 1), :] for n in names]


def depth_sum(raw, rows):
    return (
        raw.astype(F32) * rows[0]
        + pltpu.roll(raw, 1, 1).astype(F32) * rows[1]
        + pltpu.roll(raw, 127, 1).astype(F32) * rows[2]
    )


def side(blocks):
    return jnp.concatenate(blocks, axis=1)


def fold(total):
    return total[:, :64] + total[:, 64:]


def fold_rows(total):
    return total[:64] + total[64:]


def pack_kernel(m_hbm, main_ref, corner_ref, south_ref, north_ref, sems):
    ext = m_hbm.shape[0]
    here = jnp.where(is_odd(), ext - 3, 0)
    there = jnp.where(is_odd(), 0, ext - 3)
    copies = [
        pltpu.make_async_copy(m_hbm.at[pl.ds(here, 3)], main_ref, sems.at[0]),
        pltpu.make_async_copy(
            m_hbm.at[pl.ds(there, 3), pl.ds(0, 3)], corner_ref.at[:, pl.ds(0, 3)], sems.at[1]
        ),
        pltpu.make_async_copy(
            m_hbm.at[pl.ds(there, 3), pl.ds(ext - 3, 3)], corner_ref.at[:, pl.ds(3, 3)], sems.at[2]
        ),
        pltpu.make_async_copy(m_hbm.at[:, pl.ds(ext - 3, 3)], south_ref, sems.at[3]),
        pltpu.make_async_copy(m_hbm.at[:, pl.ds(0, 3)], north_ref, sems.at[4]),
    ]
    for copy in copies:
        copy.start()
    for copy in copies:
        copy.wait()


def gate_kernel(*refs):
    pass


def own_kernel(
    m_ref, mid_ref, lo_ref, hi_ref,
    out_ref, coef_ref, img_ref, q_ref, acc_ref,
):
    ext = m_ref.shape[0]
    frame = ext + 2
    cell = mid_ref.shape[2]
    margin = (ext - cell) // 2
    odd = is_odd()

    q_ref[0] = jnp.zeros(q_ref.shape[1:], F32)
    lane = lax.broadcasted_iota(jnp.int32, (frame, 128), 1)
    place = lax.broadcasted_iota(jnp.int32, (frame, 128), 0)
    share_y = cover(
        place - margin - 1, lax.axis_index("sy"), cell, lax.axis_size("sy"), margin
    )

    def coefs(f, _):
        at = jnp.zeros((1, 128), jnp.int32) + (f - margin - 1)
        share = share_y * cover(at, lax.axis_index("sx"), cell, lax.axis_size("sx"), margin)
        cen, cpl, vol = [
            jnp.concatenate([lo_ref[f, n], mid_ref[f, n], hi_ref[f, n]], axis=0) for n in range(3)
        ]
        kap = cpl * share
        vol = vol * share * share
        coef_ref[f, MID] = kap + kap
        coef_ref[f, LOW] = jnp.where(lane == 0, 0.0, pltpu.roll(kap, 1, 1))
        coef_ref[f, UPP] = jnp.where(lane == 127, 0.0, pltpu.roll(kap, 127, 1))
        coef_ref[f, DIA] = cen * share * share - vol + 0.5 * kap * kap
        coef_ref[f, VOL] = vol
        coef_ref[f, OUT] = kap * (1.0 / 16.0)
        return 0

    lax.fori_loop(0, frame, coefs, 0)

    def first(f, chunk):
        rows = pl.ds(pl.multiple_of(chunk * 16, 16), 16)
        kaps = [coef_rows(coef_ref, f, g, (MID, LOW, UPP)) for g in range(1, ext + 1)]
        slot = f & 3
        for a in range(3):
            before = pair = None
            for j in range(ext):
                w = depth_sum(m_ref[f - 1, j * 3 + a, rows, :], kaps[j])
                if j == 0:
                    q_ref[slot, 0, a, rows, :] = w
                    pair = w
                else:
                    now = before + w
                    q_ref[slot, j, a, rows, :] = now + pair
                    pair = now
                before = w
            q_ref[slot, ext, a, rows, :] = pair + before
            q_ref[slot, ext + 1, a, rows, :] = before

    def image(f, chunk, edge=None, last=False):
        rows = pl.ds(pl.multiple_of(chunk * 16, 16), 16)
        low_rows = pl.ds(pl.multiple_of(64 + chunk * 16, 16), 16)
        for g in range(frame):
            values = None
            if 1 <= g <= ext and edge is None:
                values = [m_ref[f - 1, (g - 1) * 3 + a, rows, :].astype(F32) for a in range(3)]
            lines = []
            for a in range(3):
                if edge is not None:
                    lines.append(q_ref[edge & 3, g, a, rows, :])
                    continue
                mid = q_ref[f & 3, g, a, rows, :]
                one = q_ref[(f - 1) & 3, g, a, rows, :] + mid
                lines.append(one + (mid if last else mid + q_ref[(f + 1) & 3, g, a, rows, :]))
            result = cell_image(lines, values, coef_rows(coef_ref, f, g, (DIA, VOL, OUT)))
            for a in range(3):
                high = result[a].astype(BF16)
                img_ref[f, g * 3 + a, rows, :] = high
                img_ref[f, g * 3 + a, low_rows, :] = (result[a] - high.astype(F32)).astype(BF16)

    def dot(f, chunk):
        base = jnp.minimum(chunk * 8, ext * 3 - 8)
        tiles = [m_ref[jnp.maximum(f - 1, 0), base + i] for i in range(8)]
        for i in range(2):
            tiles[i] = jnp.where(chunk == 3, jnp.zeros_like(tiles[i]), tiles[i])
        lines = side([img_ref[f, base + 3 + i] for i in range(8)])
        acc_ref[...] += lax.dot_general(side(tiles), lines, NT, preferred_element_type=F32)

    def chunks(body):
        def step(chunk, _):
            body(chunk)
            return 0

        lax.fori_loop(0, 4, step, 0)

    chunks(lambda chunk: first(1, chunk))

    @pl.when(odd)
    def _():
        chunks(lambda chunk: image(0, chunk, 1))

    def inner(f, chunk):
        dot(f - 1, chunk)
        first(f + 1, chunk)
        image(f, chunk)

    def line(f, _):
        chunks(lambda chunk: inner(f, chunk))

        @pl.when(f == 1)
        def _():
            acc_ref[...] = jnp.zeros_like(acc_ref)

        return 0

    lax.fori_loop(1, ext, line, 0)

    def inner_last(chunk):
        dot(ext - 1, chunk)
        image(ext, chunk, None, True)

    chunks(inner_last)
    chunks(lambda chunk: dot(ext, chunk))

    @pl.when(jnp.logical_not(odd))
    def _():
        chunks(lambda chunk: image(ext + 1, chunk, ext))

    out_ref[...] = fold(acc_ref[...])


def rows_kernel(
    south_ref, north_ref, img_ref, coef_ref, out_ref, cimg_ref, z_ref, acc_ref
):
    ext = south_ref.shape[0]
    raw_refs = (south_ref, north_ref)
    acc_ref[...] = jnp.zeros_like(acc_ref)

    def dots(x):
        for s in range(2):
            right = side([raw_refs[s][x, j, a] for j in range(3) for a in range(3)])
            lines = side([img_ref[x + 1, s * (ext - 1) * 3 + i] for i in range(9)])
            acc_ref[s] += lax.dot_general(lines, right, NT, preferred_element_type=F32)

    def corner(s, t, chunk):
        raw_y = (2, 1, 0) if s == 0 else (0, 1, 2)
        raw_g = (2, 1, 0) if s == 0 else (9, 10, 11)
        img_g = (3, 2, 1) if s == 0 else (8, 9, 10)
        img_y = (2, 1, 0) if s == 0 else (0, 1, 2)
        raw_x = (0, 1, 2) if t == 0 else (9, 8, 7)
        raw_f = (1, 2, 3) if t == 0 else (10, 9, 8)
        img_f = (0, 1, 2) if t == 0 else (11, 10, 9)
        img_x = (0, 1, 2) if t == 0 else (2, 1, 0)
        rows = pl.ds(pl.multiple_of(chunk * 16, 16), 16)
        low_rows = pl.ds(pl.multiple_of(64 + chunk * 16, 16), 16)
        for a in range(3):
            across = []
            for c in range(3):
                w = [
                    depth_sum(
                        raw_refs[s][raw_x[c], raw_y[d], a, rows, :],
                        coef_rows(coef_ref, raw_f[c], raw_g[d], (MID, LOW, UPP)),
                    )
                    for d in range(3)
                ]
                across.append(spread3(w))
            for e in range(3):
                for c, value in enumerate(spread3([across[i][e] for i in range(3)])):
                    z_ref[s, c, e, a] = value
        for c in range(3):
            for e in range(3):
                values = None
                if c > 0 and e > 0:
                    values = [
                        raw_refs[s][raw_x[c - 1], raw_y[e - 1], a, rows, :].astype(F32)
                        for a in range(3)
                    ]
                image = cell_image(
                    [z_ref[s, c, e, a] for a in range(3)], values,
                    coef_rows(coef_ref, img_f[c], img_g[e], (DIA, VOL, OUT)),
                )
                for a in range(3):
                    tile = (img_x[c] * 3 + img_y[e]) * 3 + a
                    high = image[a].astype(BF16)
                    cimg_ref[t, s, tile, rows, :] = high
                    cimg_ref[t, s, tile, low_rows, :] = (image[a] - high.astype(F32)).astype(BF16)

    for t in range(2):

        def step(chunk, _, t=t):
            dots(t * 4 + chunk)
            corner(0, t, chunk)
            corner(1, t, chunk)
            return 0

        lax.fori_loop(0, 4, step, 0)
    for x in range(8, ext):
        dots(x)
    out_ref[...] = side([fold_rows(acc_ref[0]), fold_rows(acc_ref[1])])


def masked(there, block):
    return jnp.where(there, block, jnp.zeros_like(block))


def corner_dot(raw, img):
    left = side([raw(i, j, a) for i in range(3) for j in range(3) for a in range(3)])
    lines = side([img(i) for i in range(27)])
    return fold(lax.dot_general(left, lines, NT, preferred_element_type=F32))


def other_kernel(corner_ref, cimg_ref, own_ref, rows_ref, out_ref, keep_ref):
    t = is_odd().astype(jnp.int32)
    low, high, beside = has_y(-1), has_y(1), has_x(False)
    south = corner_dot(lambda i, j, a: corner_ref[i, j, a], lambda i: cimg_ref[t, 0, i])
    north = corner_dot(lambda i, j, a: corner_ref[i, j + 3, a], lambda i: cimg_ref[t, 1, i])
    around = rows_ref[...]
    out_ref[...] = side(
        [
            own_ref[...], masked(high, around[:, 64:]), masked(low & beside, south),
            masked(low, around[:, :64]),
        ]
    )
    keep_ref[...] = masked(high & beside, north)


def main_kernel(main_ref, img_ref, cimg_ref, early_ref, keep_ref, out_ref):
    t = 1 - is_odd().astype(jnp.int32)
    ext = main_ref.shape[1]
    start = jnp.where(is_odd(), 0, ext - 1)
    total = None
    for i in range(3):
        right = side([main_ref[i, j, a] for j in range(ext) for a in range(3)])
        lines = side([img_ref[start + i, 3 + j] for j in range(ext * 3)])
        part = lax.dot_general(lines, right, NT, preferred_element_type=F32)
        total = part if total is None else total + part
    south = corner_dot(lambda i, j, a: main_ref[i, j, a], lambda i: cimg_ref[t, 0, i])
    north = corner_dot(lambda i, j, a: main_ref[i, ext - 3 + j, a], lambda i: cimg_ref[t, 1, i])
    low, high, beside = has_y(-1), has_y(1), has_x(True)
    blocks = [
        masked(low & beside, south), masked(beside, fold_rows(total)), masked(high & beside, north)
    ]
    code = encode(side([early_ref[...]] + blocks + [keep_ref[...]]))
    for p in range(out_ref.shape[0]):
        out_ref[p] = code


def encode(rows):
    top = jnp.max(jnp.abs(rows), axis=(0, 1), keepdims=True)
    top = jnp.where(top > 0.0, jnp.maximum(top * 1.01, 2.0**-100), 1.0).astype(BF16).astype(F32)
    value = rows * (TOP / top)
    value2 = value * value
    value4 = value2 * value2
    power = value4 * value4 * value4
    code = jnp.where(rows < 0.0, -power, power)
    row = lax.broadcasted_iota(jnp.int32, rows.shape, 0)
    lane = lax.broadcasted_iota(jnp.int32, rows.shape, 1)
    return jnp.where((row == 0) & (lane == 1), top, code).astype(BF16)


def decode(code):
    value = code.astype(F32)
    first = value[:8, :128]
    row = lax.broadcasted_iota(jnp.int32, first.shape, 0)
    lane = lax.broadcasted_iota(jnp.int32, first.shape, 1)

    def pick(tile, i, j):
        return jnp.sum(jnp.where((row == i) & (lane == j), tile, 0.0), axis=(0, 1), keepdims=True)

    scale = pick(first, 0, 1) * (1.0 / TOP)
    root = jnp.exp(jnp.log(jnp.abs(value)) * (1.0 / 12.0)) * scale
    root = jnp.where(value < 0.0, -root, root)
    head = root[:8, :128]
    head = jnp.where((row == 0) & (lane == 1), pick(head, 1, 0), head)
    return root, head


def final_kernel(code_ref, out_hbm, e_ref, l_ref, o_ref, out_sems):
    odd = is_odd()
    none = jnp.zeros(e_ref.shape[1:], F32)
    for ref in (e_ref, l_ref):
        ref[0] = none
        ref[17] = none

    def read(p, _):
        root, head = decode(code_ref[p])
        e_ref[p + 1] = root[:, :256]
        l_ref[p + 1] = root[:, 256:]
        e_ref[p + 1, pl.ds(0, 8), pl.ds(0, 128)] = head
        return 0

    read(0, 0)

    def put(p):
        return pltpu.make_async_copy(o_ref.at[p], out_hbm.at[p], out_sems.at[p])

    low = lax.broadcasted_iota(jnp.int32, (64, 128), 1) < 64

    def turned(tile):
        return jnp.transpose(jnp.concatenate([tile, tile], axis=0))[64:]

    def join(lower, upper):
        return jnp.where(low, lower, upper)

    def tiles(ref, p):
        return ref[p, :, pl.ds(0, 128)], ref[p, :, pl.ds(128, 128)]

    def ahead(p):
        read(jnp.minimum(p + 1, 15), 0)

    def even(p, _):
        ahead(p)
        (e_one, e_two), (_, e_after) = tiles(e_ref, p + 1), tiles(e_ref, p + 2)
        (b_one, b_two), (l_one, _), (_, l_after) = [tiles(l_ref, p + i) for i in range(3)]
        o_ref[p, :, pl.ds(0, 512)] = side(
            [join(b_one, turned(b_one)), join(b_two, e_two), e_one, join(e_after, l_one)]
        )
        o_ref[p, :, pl.ds(512, 64)] = l_after[:, 64:]
        put(p).start()
        return 0

    def uneven(p, _):
        ahead(p)
        (_, e_before), (e_one, e_two) = tiles(e_ref, p), tiles(e_ref, p + 1)
        (_, b_two), (l_one, _), (a_one, a_two) = [tiles(l_ref, p + i) for i in range(3)]
        o_ref[p, :, pl.ds(0, 512)] = side(
            [
                join(e_before, l_one), join(pltpu.roll(b_two, 64, 1), e_two), e_one,
                join(a_one, turned(a_one)),
            ]
        )
        o_ref[p, :, pl.ds(512, 64)] = a_two[:, :64]
        put(p).start()
        return 0

    @pl.when(jnp.logical_not(odd))
    def _():
        lax.fori_loop(0, 16, even, 0, unroll=2)

    @pl.when(odd)
    def _():
        lax.fori_loop(0, 16, uneven, 0, unroll=2)

    for p in range(16):
        put(p).wait()


def any_spec():
    return pl.BlockSpec(memory_space=pl.ANY)


def vmem_spec():
    return pl.BlockSpec(memory_space=pltpu.VMEM)


def shape(*dims, dtype=F32):
    return jax.ShapeDtypeStruct(dims, dtype)


def call(kernel, out_shape, in_specs, out_specs, scratch, mib, name):
    return pl.pallas_call(
        kernel,
        out_shape=out_shape,
        in_specs=in_specs,
        out_specs=out_specs,
        scratch_shapes=scratch,
        compiler_params=pltpu.CompilerParams(vmem_limit_bytes=mib * MIB),
        cost_estimate=pl.CostEstimate(flops=1000, bytes_accessed=1000, transcendentals=0),
        name=name,
    )


def gate(values, others):
    count = len(values)
    return pl.pallas_call(
        gate_kernel,
        out_shape=[shape(*x.shape, dtype=x.dtype) for x in values],
        in_specs=[any_spec()] * (count + len(others)),
        out_specs=[any_spec()] * count,
        input_output_aliases={i: i for i in range(count)},
        compiler_params=pltpu.CompilerParams(vmem_limit_bytes=MIB),
        name="gate",
    )(*values, *others)


def coef_columns(centre, coupling, volume):
    own = jnp.stack([centre, coupling, volume], axis=1)
    up, down = neighbours(lax.axis_size("sx"))
    low = lax.ppermute(own[-2:], "sx", up)
    high = lax.ppermute(own[:2], "sx", down)
    return jnp.concatenate([low, own, high], axis=0)


def coef_edges(mid):
    up, down = neighbours(lax.axis_size("sy"))
    lo = lax.ppermute(mid[:, :, -2:], "sy", up)
    hi = lax.ppermute(mid[:, :, :2], "sy", down)
    return lo, hi


def local(modes, centre, coupling, volume):
    ext = modes.shape[0]
    nx = lax.axis_size("sx")
    ny = lax.axis_size("sy")
    mid = coef_columns(centre, coupling, volume)
    m = jnp.transpose(modes, (0, 1, 3, 2, 4))
    frame = ext + 2

    main, corner, south, north = call(
        pack_kernel,
        [
            shape(3, ext, 3, 64, 128, dtype=BF16),
            shape(3, 6, 3, 64, 128, dtype=BF16),
            shape(ext, 3, 3, 64, 128, dtype=BF16),
            shape(ext, 3, 3, 64, 128, dtype=BF16),
        ],
        [vmem_spec()],
        [vmem_spec()] * 4,
        [pltpu.SemaphoreType.DMA((5,))],
        8,
        "pack",
    )(m)
    main, corner, south, north, mid = gate((main, corner, south, north, mid), ())
    main_pairs, other_pairs = [], []
    for y in range(ny):
        for x in range(nx):
            lower, higher = x * ny + y, (x + 1) % nx * ny + y
            main_pairs.append((higher, lower) if y % 2 == 0 else (lower, higher))
            other_pairs.append((lower, higher) if y % 2 == 0 else (higher, lower))
    main = lax.ppermute(main, ("sx", "sy"), main_pairs)
    corner = lax.ppermute(corner, ("sx", "sy"), other_pairs)
    lo, hi = coef_edges(mid)
    south, north = gate((south, north), (lo, hi))
    up, down = neighbours(ny)
    south = lax.ppermute(south, "sy", up)
    north = lax.ppermute(north, "sy", down)

    own, coef, img = call(
        own_kernel,
        [
            shape(64, 64),
            shape(frame, 6, frame, 128),
            shape(frame, frame * 3, 128, 128, dtype=BF16),
        ],
        [vmem_spec()] * 4,
        [vmem_spec()] * 3,
        [
            pltpu.VMEM((4, frame, 3, 64, 128), F32),
            pltpu.VMEM((64, 128), F32),
        ],
        OWN_MIB,
        "own_gram",
    )(m.reshape(ext, ext * 3, 64, 128), mid, lo, hi)
    around, cimg = call(
        rows_kernel,
        [shape(64, 128), shape(2, 2, 27, 128, 128, dtype=BF16)],
        [vmem_spec()] * 4,
        [vmem_spec(), vmem_spec()],
        [
            pltpu.VMEM((2, 3, 3, 3, 16, 128), F32),
            pltpu.VMEM((2, 128, 64), F32),
        ],
        8,
        "row_gram",
    )(south, north, img, coef)
    early, keep = call(
        other_kernel,
        [shape(64, 256), shape(64, 64)],
        [vmem_spec()] * 4,
        [vmem_spec()] * 2,
        [],
        10,
        "corner_gram",
    )(corner, cimg, own, around)
    code = call(
        main_kernel,
        shape(nx, 64, 512, dtype=BF16),
        [vmem_spec()] * 5,
        vmem_spec(),
        [],
        8,
        "column_gram",
    )(main, img, cimg, early, keep)
    code = lax.all_to_all(code, "sx", 0, 0)
    out = call(
        final_kernel,
        shape(nx, 64, 576),
        [vmem_spec()],
        any_spec(),
        [
            pltpu.VMEM((nx + 2, 64, 256), F32),
            pltpu.VMEM((nx + 2, 64, 256), F32),
            pltpu.VMEM((nx, 64, 576), F32),
            pltpu.SemaphoreType.DMA((nx,)),
        ],
        12,
        "assemble",
    )(code)
    return out[None]


def solution(mesh):
    in_specs = (
        P("sx", "sy", None, None, None),
        P("sx", "sy", None),
        P("sx", "sy", None),
        P("sx", "sy", None),
    )
    out_specs = P("sy", None, None, None)
    return jax.shard_map(local, mesh=mesh, in_specs=in_specs, out_specs=out_specs, check_vma=False)
```

time: 84.3 us -> 75.6 us (0.90)
  Pallas kernels: 39.2 us -> 26.2 us
  waiting for transfers between devices: 2.91 us -> 10.3 us
  local copies, waits for them, and re-layouts: 4.82 us -> 2.44 us
  blocking collectives: 24.5 us -> 22.9 us
  starting transfers between devices: 11.2 us -> 12.6 us
    pallas_call x4, Pallas kernels: 20.7 us -> 10.7 us  [the longest x1 4.35 us: local(): call(final_kernel, shape(nx, 64, 576), [vmem_spec()], any_spec(), [pltpu....]
    ppermute x1, waiting for transfers between devices: 0.01 us -> 7.37 us  [local(): corner = lax.ppermute(corner, ('sx', 'sy'), other_pairs)]
    unnamed x10 -> x12, local copies, waits for them, and re-layouts: 4.79 us -> 2.42 us
    pallas_call x1, Pallas kernels: 16.4 us -> 14.7 us  [local(): call(own_kernel, [shape(64, 64), shape(frame, 6, frame, 128), shape(frame...]
    all_to_all x1, blocking collectives: 24.5 us -> 22.9 us  [local(): code = lax.all_to_all(code, 'sx', 0, 0)]
    pallas_call x1, Pallas kernels: 2.16 us -> 0.75 us  [local(): call(pack_kernel, [shape(3, ext, 3, 64, 128, dtype=BF16), shape(3, 6, 3,...]
    ppermute x1, starting transfers between devices: 2.54 us -> 3.95 us  [local(): main = lax.ppermute(main, ('sx', 'sy'), main_pairs)]
  transfers between devices with their start and end apart: 8 -> 8, of which waited for: 2 -> 3; matrix products, arithmetic and copies ran while one was open for 0% -> 0% of each run, Pallas kernels for 36% -> 27%
where the time goes in v5:
time: 75.6 us; the launch traced here: 75.3 us
  Pallas kernels  26.2 us (35%)
  blocking collectives  22.9 us (30%)
  starting transfers between devices  12.6 us (17%)
  waiting for transfers between devices  10.3 us (14%)
  local copies, waits for them, and re-layouts  2.44 us (3%)
  other arithmetic  0.8 us (1%)
    all_to_all x1, blocking collectives, local(): code = lax.all_to_all(code, 'sx', 0, 0)  22.9 us
    pallas_call x1, Pallas kernels, local(): call(own_kernel, [shape(64, 64), shape(frame, 6, frame, 128), shape(frame...  14.7 us
    ppermute x1, waiting for transfers between devices, local(): corner = lax.ppermute(corner, ('sx', 'sy'), other_pairs)  7.37 us
    ppermute x1, starting transfers between devices, coef_columns(): high = lax.ppermute(own[:2], 'sx', down)  4.82 us
    pallas_call x1, Pallas kernels, local(): call(final_kernel, shape(nx, 64, 576), [vmem_spec()], any_spec(), [pltpu....  4.35 us
    ppermute x1, starting transfers between devices, local(): main = lax.ppermute(main, ('sx', 'sy'), main_pairs)  3.95 us
    pallas_call x1, Pallas kernels, local(): call(rows_kernel, [shape(64, 128), shape(2, 2, 27, 128, 128, dtype=BF16)]...  3.76 us
    unnamed x12, local copies, waits for them, and re-layouts  2.42 us
  transfers between devices with their start and end apart: 8, of which 3 were waited for; matrix products, arithmetic and copies ran while one was open for 0% of the time, Pallas kernels for 27%

profile of v5, /device:TPU:24, one launch (start us, length us, event | category | flops | bytes accessed | tf_op | source)
XLA Modules:
  0.0 75.3 jit_solution(6681609621032618761)
XLA Ops:
  0.0 0.8 %pad_maximum_fusion.3 = (f32[2,3,8,128]{3,2,1,0:T(8,128)S(1)}, f32[2,3,8,128]{3,2,1,0:T(8,128)S(1)}) fusion(f32[8,1,8,128]{3,2,1,0:T(8,128)} %bitcast.11, f32[8,1,8,128]{3,2,1,0:T(8,128)} %bitcast.13, f32[8,1,8,128]{3,2,1,0:T(8,128)} %bitcast.15), kind=kLoop, calls=%fused_computation.3 | loop fusion | flops 24576 | bytes 147456 | tf_op jit(solution)/shard_map/slice | solution.py:500
  0.8 1.5 %collective-permute-start = (f32[2,3,8,128]{3,2,1,0:T(8,128)S(1)}, f32[2,3,8,128]{3,2,1,0:T(8,128)S(1)}, u32[]{:S(2)}, u32[]{:S(2)}) collective-permute-start(f32[2,3,8,128]{3,2,1,0:T(8,128)S(1)} %get-tuple-element.43), channel_id=1, source_target_pairs={{0,8},{8,16},{16,24},{24,32},{32,40},{40,48},{48,56},{56,64},{64,7... | collective-permute-start | bytes 73736 | tf_op jit(solution)/shard_map/ppermute | solution.py:500
  2.3 4.8 %collective-permute-start.1 = (f32[2,3,8,128]{3,2,1,0:T(8,128)S(1)}, f32[2,3,8,128]{3,2,1,0:T(8,128)S(1)}, u32[]{:S(2)}, u32[]{:S(2)}) collective-permute-start(f32[2,3,8,128]{3,2,1,0:T(8,128)S(1)} %get-tuple-element.44), channel_id=1, source_target_pairs={{8,0},{16,8},{24,16},{32,24},{40,32},{48,40},{56,48},{64,56},{72,6... | collective-permute-start | bytes 73736 | tf_op jit(solution)/shard_map/ppermute | solution.py:501
  7.1 0.0 copy-start
  7.1 2.4 %copy-done = bf16[10,10,64,3,128]{4,2,3,1,0:T(8,128)(2,1)S(1)} copy-done((bf16[10,10,64,3,128]{4,2,3,1,0:T(8,128)(2,1)S(1)}, bf16[10,10,64,3,128]{4,2,3,1,0:T(8,128)(2,1)}, u32[]{:S(2)}) %copy-start) | copy-done | bytes 4915224
  9.5 0.0 copy-start.1
  9.5 0.0 copy-start.2
  9.5 0.0 copy-start.3
  9.5 0.7 pack.1
  10.3 0.0 collective-permute-done
  10.3 0.0 collective-permute-done.1
  10.3 0.0 copy-done.1
  10.3 0.0 copy-done.2
  10.3 0.0 copy-done.3
  10.3 0.0 slice-start
  10.4 0.0 slice-start.1
  10.4 0.0 collective-permute-start.4
  10.5 0.5 collective-permute-start.3
  11.0 1.1 %collective-permute-done.4.hi_ref.refs_3_ = f32[12,3,2,128]{3,2,1,0:T(2,128)S(1)} collective-permute-done((f32[12,3,2,128]{3,2,1,0:T(2,128)S(1)}, f32[12,3,2,128]{3,2,1,0:T(2,128)S(1)}, u32[]{:S(2)}, u32[]{:S(2)}) %collective-permute-start.4) | collective-permute-done | bytes 36896 | tf_op jit(solution)/shard_map/ppermute | solution.py:508
  12.1 1.8 %collective-permute-done.3.lo_ref.refs_2_ = f32[12,3,2,128]{3,2,1,0:T(2,128)S(1)} collective-permute-done((f32[12,3,2,128]{3,2,1,0:T(2,128)S(1)}, f32[12,3,2,128]{3,2,1,0:T(2,128)S(1)}, u32[]{:S(2)}, u32[]{:S(2)}) %collective-permute-start.3) | collective-permute-done | bytes 36896 | tf_op jit(solution)/shard_map/ppermute | solution.py:507
  13.9 0.7 collective-permute-start.5
  14.6 1.0 %collective-permute-start.6 = (bf16[10,3,3,64,128]{4,3,2,1,0:T(8,128)(2,1)S(1)}, bf16[10,3,3,64,128]{4,3,2,1,0:T(8,128)(2,1)S(1)}, u32[]{:S(2)}, u32[]{:S(2)}) collective-permute-start(bf16[10,3,3,64,128]{4,3,2,1,0:T(8,128)(2,1)S(1)} %get-tuple-element.33), channel_id=1, source_target_pairs={{1,0},{2,1},{3,2},{4,3},{5,4},{6,5},{7,6},{0,7},{9,8},{10,9},{11,1... | collective-permute-start | bytes 4423688 | tf_op jit(solution)/shard_map/ppermute | solution.py:547
  15.6 4.0 %collective-permute-start.2 = (bf16[3,10,3,64,128]{4,3,2,1,0:T(8,128)(2,1)S(1)}, bf16[3,10,3,64,128]{4,3,2,1,0:T(8,128)(2,1)S(1)}, u32[]{:S(2)}, u32[]{:S(2)}) collective-permute-start(bf16[3,10,3,64,128]{4,3,2,1,0:T(8,128)(2,1)S(1)} %get-tuple-element.27), channel_id=1, source_target_pairs={{8,0},{16,8},{24,16},{32,24},{40,32},{48,40},{56,48},{64,56},{72,6... | collective-permute-start | bytes 4423688 | tf_op jit(solution)/shard_map/ppermute | solution.py:541
  19.6 0.0 collective-permute-start.7
  19.6 0.0 slice-done
  19.6 0.0 slice-done.1
  19.6 14.7 %own_gram.1 = (f32[64,64]{1,0:T(8,128)S(1)}, f32[12,6,12,128]{3,2,1,0:T(8,128)S(1)}, bf16[12,36,128,128]{3,2,1,0:T(8,128)(2,1)S(1)}) custom-call(bf16[10,30,64,128]{3,2,1,0:T(8,128)(2,1)S(1)} %bitcast.10, f32[12,3,8,128]{3,2,1,0:T(8,128)S(1)} %get-tuple-element.28.mid_ref, f32[12,3,2,128]{3,2,1,0:T(2,128)S(1)} %collective-permute-done.3.lo_ref.refs_2_, ...), custom_call_target="tpu_custom_call" | custom-call | flops 1000 | bytes 1000 | tf_op jit(solution)/shard_map/own_gram/pallas_call | solution.py:549
  34.3 0.0 collective-permute-done.5.south_ref
  34.3 0.0 collective-permute-done.6.north_ref
  34.3 3.8 %row_gram.1 = (f32[64,128]{1,0:T(8,128)S(1)}, bf16[2,2,27,128,128]{4,3,2,1,0:T(8,128)(2,1)S(1)}) custom-call(bf16[10,3,3,64,128]{4,3,2,1,0:T(8,128)(2,1)S(1)} %collective-permute-done.5.south_ref, bf16[10,3,3,64,128]{4,3,2,1,0:T(8,128)(2,1)S(1)} %collective-permute-done.6.north_ref, bf16[12,36,128,128]{3,2,1,0:T(8,128)(2,1)S(1)} %get-tuple-element.29.img_ref, ...), custom_call_target="tpu_custom_call" | custom-call | flops 1000 | bytes 1000 | tf_op jit(solution)/shard_map/row_gram/pallas_call | solution.py:565
  38.1 7.4 %collective-permute-done.7.corner_ref = bf16[3,6,3,64,128]{4,3,2,1,0:T(8,128)(2,1)S(1)} collective-permute-done((bf16[3,6,3,64,128]{4,3,2,1,0:T(8,128)(2,1)S(1)}, bf16[3,6,3,64,128]{4,3,2,1,0:T(8,128)(2,1)S(1)}, u32[]{:S(2)}, u32[]{:S(2)}) %collective-permute-start.7) | collective-permute-done | bytes 884768 | tf_op jit(solution)/shard_map/ppermute | solution.py:542
  45.5 0.8 %corner_gram.1 = (f32[64,256]{1,0:T(8,128)S(1)}, f32[64,64]{1,0:T(8,128)S(1)}) custom-call(bf16[3,6,3,64,128]{4,3,2,1,0:T(8,128)(2,1)S(1)} %collective-permute-done.7.corner_ref, bf16[2,2,27,128,128]{4,3,2,1,0:T(8,128)(2,1)S(1)} %get-tuple-element.35.cimg_ref, f32[64,64]{1,0:T(8,128)S(1)} %get-tuple-element.37.own_ref, f32[64,128]{1,0:T(8,128)S(1)} %get-tuple-element.38.rows_ref), custom_call_target="tpu_custom_call" | custom-call | flops 1000 | bytes 1000 | tf_op jit(solution)/shard_map/corner_gram/pallas_call | solution.py:577
  46.3 0.0 collective-permute-done.2.main_ref
  46.3 1.8 %column_gram.1 = bf16[16,64,512]{2,1,0:T(8,128)(2,1)S(1)} custom-call(bf16[3,10,3,64,128]{4,3,2,1,0:T(8,128)(2,1)S(1)} %collective-permute-done.2.main_ref, bf16[12,36,128,128]{3,2,1,0:T(8,128)(2,1)S(1)} %get-tuple-element.29.img_ref, bf16[2,2,27,128,128]{4,3,2,1,0:T(8,128)(2,1)S(1)} %get-tuple-element.35.cimg_ref, ...), custom_call_target="tpu_custom_call" | custom-call | flops 1000 | bytes 1000 | tf_op jit(solution)/shard_map/column_gram/pallas_call | solution.py:586
  48.1 22.9 %all_to_all.5.code_ref = bf16[16,64,512]{2,1,0:T(8,128)(2,1)S(1)} all-to-all(bf16[16,64,512]{2,1,0:T(8,128)(2,1)S(1)} %column_gram.1), channel_id=1, replica_groups=mesh['sx'=16,'sy'=8] {'sx'}, dimensions={0} | all-to-all | bytes 2097152 | tf_op jit(solution)/shard_map/all_to_all | solution.py:595
  70.9 4.4 %assemble.1 = f32[16,64,576]{2,1,0:T(8,128)} custom-call(bf16[16,64,512]{2,1,0:T(8,128)(2,1)S(1)} %all_to_all.5.code_ref), custom_call_target="tpu_custom_call" | custom-call | flops 1000 | bytes 1000 | tf_op jit(solution)/shard_map/assemble/pallas_call | solution.py:596
  (5 shorter events, 0.0 us)
Async XLA Ops:
  0.8 9.5 %collective-permute-start = (f32[2,3,8,128]{3,2,1,0:T(8,128)S(1)}, f32[2,3,8,128]{3,2,1,0:T(8,128)S(1)}, u32[]{:S(2)}, u32[]{:S(2)}) collective-permute-start(f32[2,3,8,128]{3,2,1,0:T(8,128)S(1)} %get-tuple-element.43), channel_id=1, source_target_pairs={{0,8},{8,16},{16,24},{24,32},{32,40},{40,48},{48,56},{56,64},{64,7... | collective-permute-start | bytes 73736 | tf_op jit(solution)/shard_map/ppermute | solution.py:500
  2.3 8.0 %collective-permute-start.1 = (f32[2,3,8,128]{3,2,1,0:T(8,128)S(1)}, f32[2,3,8,128]{3,2,1,0:T(8,128)S(1)}, u32[]{:S(2)}, u32[]{:S(2)}) collective-permute-start(f32[2,3,8,128]{3,2,1,0:T(8,128)S(1)} %get-tuple-element.44), channel_id=1, source_target_pairs={{8,0},{16,8},{24,16},{32,24},{40,32},{48,40},{56,48},{64,56},{72,6... | collective-permute-start | bytes 73736 | tf_op jit(solution)/shard_map/ppermute | solution.py:501
  7.1 2.4 %copy-start = (bf16[10,10,64,3,128]{4,2,3,1,0:T(8,128)(2,1)S(1)}, bf16[10,10,64,3,128]{4,2,3,1,0:T(8,128)(2,1)}, u32[]{:S(2)}) copy-start(bf16[10,10,64,3,128]{4,2,3,1,0:T(8,128)(2,1)} %param.4) | copy-start | bytes 14745604
  9.5 0.8 %copy-start.1 = (f32[8,8,128]{2,1,0:T(8,128)S(1)}, f32[8,8,128]{2,1,0:T(8,128)}, u32[]{:S(2)}) copy-start(f32[8,8,128]{2,1,0:T(8,128)} %param.7) | copy-start | bytes 98308
  9.5 0.8 %copy-start.2 = (f32[8,8,128]{2,1,0:T(8,128)S(1)}, f32[8,8,128]{2,1,0:T(8,128)}, u32[]{:S(2)}) copy-start(f32[8,8,128]{2,1,0:T(8,128)} %param.6) | copy-start | bytes 98308
  9.5 0.8 %copy-start.3 = (f32[8,8,128]{2,1,0:T(8,128)S(1)}, f32[8,8,128]{2,1,0:T(8,128)}, u32[]{:S(2)}) copy-start(f32[8,8,128]{2,1,0:T(8,128)} %param.5) | copy-start | bytes 98308
  10.3 9.2 %slice-start = ((s8[4915200]{0:T(1024)(128)(4,1)}), s8[4194304]{0:T(1024)(128)(4,1)S(1)}, s32[]{:S(2)}) async-start(s8[4915200]{0:T(1024)(128)(4,1)} %bitcast.8), calls=%async_computation.1 | async-start | bytes 8388608
  10.4 9.2 %slice-start.1 = ((s8[4915200]{0:T(1024)(128)(4,1)}), s8[720896]{0:T(1024)(128)(4,1)S(1)}, s32[]{:S(2)}) async-start(s8[4915200]{0:T(1024)(128)(4,1)} %bitcast.8), calls=%async_computation.2 | async-start | bytes 1441792
  10.4 1.7 %collective-permute-start.4 = (f32[12,3,2,128]{3,2,1,0:T(2,128)S(1)}, f32[12,3,2,128]{3,2,1,0:T(2,128)S(1)}, u32[]{:S(2)}, u32[]{:S(2)}) collective-permute-start(f32[12,3,2,128]{3,2,1,0:T(2,128)S(1)} %get-tuple-element.41), channel_id=1, source_target_pairs={{1,0},{2,1},{3,2},{4,3},{5,4},{6,5},{7,6},{0,7},{9,8},{10,9},{11,1... | collective-permute-start | bytes 110600 | tf_op jit(solution)/shard_map/ppermute | solution.py:508
  10.5 3.4 %collective-permute-start.3 = (f32[12,3,2,128]{3,2,1,0:T(2,128)S(1)}, f32[12,3,2,128]{3,2,1,0:T(2,128)S(1)}, u32[]{:S(2)}, u32[]{:S(2)}) collective-permute-start(f32[12,3,2,128]{3,2,1,0:T(2,128)S(1)} %get-tuple-element.42), channel_id=1, source_target_pairs={{0,1},{1,2},{2,3},{3,4},{4,5},{5,6},{6,7},{7,0},{8,9},{9,10},{10,1... | collective-permute-start | bytes 110600 | tf_op jit(solution)/shard_map/ppermute | solution.py:507
  13.9 20.5 %collective-permute-start.5 = (bf16[10,3,3,64,128]{4,3,2,1,0:T(8,128)(2,1)S(1)}, bf16[10,3,3,64,128]{4,3,2,1,0:T(8,128)(2,1)S(1)}, u32[]{:S(2)}, u32[]{:S(2)}) collective-permute-start(bf16[10,3,3,64,128]{4,3,2,1,0:T(8,128)(2,1)S(1)} %get-tuple-element.32), channel_id=1, source_target_pairs={{0,1},{1,2},{2,3},{3,4},{4,5},{5,6},{6,7},{7,0},{8,9},{9,10},{10,1... | collective-permute-start | bytes 4423688 | tf_op jit(solution)/shard_map/ppermute | solution.py:546
  14.6 19.7 %collective-permute-start.6 = (bf16[10,3,3,64,128]{4,3,2,1,0:T(8,128)(2,1)S(1)}, bf16[10,3,3,64,128]{4,3,2,1,0:T(8,128)(2,1)S(1)}, u32[]{:S(2)}, u32[]{:S(2)}) collective-permute-start(bf16[10,3,3,64,128]{4,3,2,1,0:T(8,128)(2,1)S(1)} %get-tuple-element.33), channel_id=1, source_target_pairs={{1,0},{2,1},{3,2},{4,3},{5,4},{6,5},{7,6},{0,7},{9,8},{10,9},{11,1... | collective-permute-start | bytes 4423688 | tf_op jit(solution)/shard_map/ppermute | solution.py:547
  15.6 30.7 %collective-permute-start.2 = (bf16[3,10,3,64,128]{4,3,2,1,0:T(8,128)(2,1)S(1)}, bf16[3,10,3,64,128]{4,3,2,1,0:T(8,128)(2,1)S(1)}, u32[]{:S(2)}, u32[]{:S(2)}) collective-permute-start(bf16[3,10,3,64,128]{4,3,2,1,0:T(8,128)(2,1)S(1)} %get-tuple-element.27), channel_id=1, source_target_pairs={{8,0},{16,8},{24,16},{32,24},{40,32},{48,40},{56,48},{64,56},{72,6... | collective-permute-start | bytes 4423688 | tf_op jit(solution)/shard_map/ppermute | solution.py:541
  19.6 25.9 %collective-permute-start.7 = (bf16[3,6,3,64,128]{4,3,2,1,0:T(8,128)(2,1)S(1)}, bf16[3,6,3,64,128]{4,3,2,1,0:T(8,128)(2,1)S(1)}, u32[]{:S(2)}, u32[]{:S(2)}) collective-permute-start(bf16[3,6,3,64,128]{4,3,2,1,0:T(8,128)(2,1)S(1)} %get-tuple-element.36), channel_id=1, source_target_pairs={{0,8},{8,16},{16,24},{24,32},{32,40},{40,48},{48,56},{56,64},{64,7... | collective-permute-start | bytes 2654216 | tf_op jit(solution)/shard_map/ppermute | solution.py:542

commit v6 on v5

--- a/solution.py
+++ b/solution.py
@@ -96,13 +96,10 @@
     copies = [
         pltpu.make_async_copy(m_hbm.at[pl.ds(here, 3)], main_ref, sems.at[0]),
         pltpu.make_async_copy(
-            m_hbm.at[pl.ds(there, 3), pl.ds(0, 3)], corner_ref.at[:, pl.ds(0, 3)], sems.at[1]
+            m_hbm.at[pl.ds(there, 3), pl.ds(ext - 3, 3)], corner_ref, sems.at[1]
         ),
-        pltpu.make_async_copy(
-            m_hbm.at[pl.ds(there, 3), pl.ds(ext - 3, 3)], corner_ref.at[:, pl.ds(3, 3)], sems.at[2]
-        ),
-        pltpu.make_async_copy(m_hbm.at[:, pl.ds(ext - 3, 3)], south_ref, sems.at[3]),
-        pltpu.make_async_copy(m_hbm.at[:, pl.ds(0, 3)], north_ref, sems.at[4]),
+        pltpu.make_async_copy(m_hbm.at[:, pl.ds(ext - 3, 3)], south_ref, sems.at[2]),
+        pltpu.make_async_copy(m_hbm.at[:, pl.ds(0, 3)], north_ref, sems.at[3]),
     ]
     for copy in copies:
         copy.start()
@@ -147,7 +144,7 @@
         coef_ref[f, OUT] = kap * (1.0 / 16.0)
         return 0
 
-    lax.fori_loop(0, frame, coefs, 0)
+    lax.fori_loop(0, frame, coefs, 0, unroll=4)
 
     def first(f, chunk):
         rows = pl.ds(pl.multiple_of(chunk * 16, 16), 16)
@@ -202,7 +199,7 @@
             body(chunk)
             return 0
 
-        lax.fori_loop(0, 4, step, 0)
+        lax.fori_loop(0, 4, step, 0, unroll=4)
 
     chunks(lambda chunk: first(1, chunk))
 
@@ -304,7 +301,7 @@
             corner(1, t, chunk)
             return 0
 
-        lax.fori_loop(0, 4, step, 0)
+        lax.fori_loop(0, 4, step, 0, unroll=2)
     for x in range(8, ext):
         dots(x)
     out_ref[...] = side([fold_rows(acc_ref[0]), fold_rows(acc_ref[1])])
@@ -320,22 +317,19 @@
     return fold(lax.dot_general(left, lines, NT, preferred_element_type=F32))
 
 
-def other_kernel(corner_ref, cimg_ref, own_ref, rows_ref, out_ref, keep_ref):
+def other_kernel(corner_ref, cimg_ref, keep_ref, turned_ref):
     t = is_odd().astype(jnp.int32)
-    low, high, beside = has_y(-1), has_y(1), has_x(False)
-    south = corner_dot(lambda i, j, a: corner_ref[i, j, a], lambda i: cimg_ref[t, 0, i])
-    north = corner_dot(lambda i, j, a: corner_ref[i, j + 3, a], lambda i: cimg_ref[t, 1, i])
-    around = rows_ref[...]
-    out_ref[...] = side(
-        [
-            own_ref[...], masked(high, around[:, 64:]), masked(low & beside, south),
-            masked(low, around[:, :64]),
-        ]
+    there = has_y(1) & has_x(False)
+    cells = [(i, j, a) for i in range(3) for j in range(3) for a in range(3)]
+    raw = side([corner_ref[c] for c in cells])
+    lines = side([cimg_ref[t, 1, i] for i in range(27)])
+    keep_ref[...] = masked(there, fold(lax.dot_general(raw, lines, NT, preferred_element_type=F32)))
+    turned_ref[...] = masked(
+        there, fold_rows(lax.dot_general(lines, raw, NT, preferred_element_type=F32))
     )
-    keep_ref[...] = masked(high & beside, north)
-
-
-def main_kernel(main_ref, img_ref, cimg_ref, early_ref, keep_ref, out_ref):
+
+
+def main_kernel(main_ref, img_ref, cimg_ref, own_ref, rows_ref, below_ref, keep_ref, out_ref):
     t = 1 - is_odd().astype(jnp.int32)
     ext = main_ref.shape[1]
     start = jnp.where(is_odd(), 0, ext - 1)
@@ -348,10 +342,13 @@
     south = corner_dot(lambda i, j, a: main_ref[i, j, a], lambda i: cimg_ref[t, 0, i])
     north = corner_dot(lambda i, j, a: main_ref[i, ext - 3 + j, a], lambda i: cimg_ref[t, 1, i])
     low, high, beside = has_y(-1), has_y(1), has_x(True)
+    around = rows_ref[...]
     blocks = [
-        masked(low & beside, south), masked(beside, fold_rows(total)), masked(high & beside, north)
+        own_ref[...], masked(high, around[:, 64:]), below_ref[...], masked(low, around[:, :64]),
+        masked(low & beside, south), masked(beside, fold_rows(total)),
+        masked(high & beside, north), keep_ref[...],
     ]
-    code = encode(side([early_ref[...]] + blocks + [keep_ref[...]]))
+    code = encode(side(blocks))
     for p in range(out_ref.shape[0]):
         out_ref[p] = code
 
@@ -421,10 +418,10 @@
 
     def even(p, _):
         ahead(p)
-        (e_one, e_two), (_, e_after) = tiles(e_ref, p + 1), tiles(e_ref, p + 2)
+        e_one, e_two = tiles(e_ref, p + 1)
         (b_one, b_two), (l_one, _), (_, l_after) = [tiles(l_ref, p + i) for i in range(3)]
         o_ref[p, :, pl.ds(0, 512)] = side(
-            [join(b_one, turned(b_one)), join(b_two, e_two), e_one, join(e_after, l_one)]
+            [join(b_one, turned(b_one)), join(b_two, e_two), e_one, join(e_two, l_one)]
         )
         o_ref[p, :, pl.ds(512, 64)] = l_after[:, 64:]
         put(p).start()
@@ -432,11 +429,11 @@
 
     def uneven(p, _):
         ahead(p)
-        (_, e_before), (e_one, e_two) = tiles(e_ref, p), tiles(e_ref, p + 1)
+        e_one, e_two = tiles(e_ref, p + 1)
         (_, b_two), (l_one, _), (a_one, a_two) = [tiles(l_ref, p + i) for i in range(3)]
         o_ref[p, :, pl.ds(0, 512)] = side(
             [
-                join(e_before, l_one), join(pltpu.roll(b_two, 64, 1), e_two), e_one,
+                join(e_two, l_one), join(pltpu.roll(b_two, 64, 1), e_two), e_one,
                 join(a_one, turned(a_one)),
             ]
         )
@@ -521,13 +518,13 @@
         pack_kernel,
         [
             shape(3, ext, 3, 64, 128, dtype=BF16),
-            shape(3, 6, 3, 64, 128, dtype=BF16),
+            shape(3, 3, 3, 64, 128, dtype=BF16),
             shape(ext, 3, 3, 64, 128, dtype=BF16),
             shape(ext, 3, 3, 64, 128, dtype=BF16),
         ],
         [vmem_spec()],
         [vmem_spec()] * 4,
-        [pltpu.SemaphoreType.DMA((5,))],
+        [pltpu.SemaphoreType.DMA((4,))],
         8,
         "pack",
     )(m)
@@ -574,24 +571,25 @@
         8,
         "row_gram",
     )(south, north, img, coef)
-    early, keep = call(
+    keep, turned = call(
         other_kernel,
-        [shape(64, 256), shape(64, 64)],
-        [vmem_spec()] * 4,
+        [shape(64, 64), shape(64, 64)],
+        [vmem_spec()] * 2,
         [vmem_spec()] * 2,
         [],
-        10,
+        8,
         "corner_gram",
-    )(corner, cimg, own, around)
+    )(corner, cimg)
+    below = lax.ppermute(turned, "sy", up)
     code = call(
         main_kernel,
         shape(nx, 64, 512, dtype=BF16),
-        [vmem_spec()] * 5,
+        [vmem_spec()] * 7,
         vmem_spec(),
         [],
         8,
         "column_gram",
-    )(main, img, cimg, early, keep)
+    )(main, img, cimg, own, around, below, keep)
     code = lax.all_to_all(code, "sx", 0, 0)
     out = call(
         final_kernel,

time: 75.6 us -> 71.5 us (0.946)
  waiting for transfers between devices: 10.3 us -> 4.32 us
  starting transfers between devices: 12.6 us -> 17.5 us
  Pallas kernels: 26.2 us -> 23.4 us
    ppermute x1, waiting for transfers between devices: 7.37 us -> 0.01 us  [local(): corner = lax.ppermute(corner, ('sx', 'sy'), other_pairs)]
    ppermute x0 -> x1, starting transfers between devices: none -> 4.92 us  [local(): below = lax.ppermute(turned, 'sy', up)]
    pallas_call x1, Pallas kernels: 14.7 us -> 12.5 us  [local(): call(own_kernel, [shape(64, 64), shape(frame, 6, frame, 128), shape(frame...]
    ppermute x0 -> x1, waiting for transfers between devices: none -> 0.86 us  [local(): below = lax.ppermute(turned, 'sy', up)]
  transfers between devices with their start and end apart: 8 -> 9, of which waited for: 3 -> 4; matrix products, arithmetic and copies ran while one was open for 0% -> 0% of each run, Pallas kernels for 27% -> 24%
where the time goes in v6:
time: 71.5 us; the launch traced here: 71.2 us
  Pallas kernels  23.4 us (33%)
  blocking collectives  22.6 us (32%)
  starting transfers between devices  17.5 us (24%)
  waiting for transfers between devices  4.32 us (6%)
  local copies, waits for them, and re-layouts  2.51 us (4%)
  other arithmetic  0.8 us (1%)
    all_to_all x1, blocking collectives, local(): code = lax.all_to_all(code, 'sx', 0, 0)  22.6 us
    pallas_call x1, Pallas kernels, local(): call(own_kernel, [shape(64, 64), shape(frame, 6, frame, 128), shape(frame...  12.5 us
    ppermute x1, starting transfers between devices, local(): below = lax.ppermute(turned, 'sy', up)  4.92 us
    ppermute x1, starting transfers between devices, coef_columns(): high = lax.ppermute(own[:2], 'sx', down)  4.82 us
    pallas_call x1, Pallas kernels, local(): call(final_kernel, shape(nx, 64, 576), [vmem_spec()], any_spec(), [pltpu....  4.33 us
    ppermute x1, starting transfers between devices, local(): main = lax.ppermute(main, ('sx', 'sy'), main_pairs)  3.98 us
    pallas_call x1, Pallas kernels, local(): call(rows_kernel, [shape(64, 128), shape(2, 2, 27, 128, 128, dtype=BF16)]...  3.38 us
    unnamed x12, local copies, waits for them, and re-layouts  2.48 us
  transfers between devices with their start and end apart: 9, of which 4 were waited for; matrix products, arithmetic and copies ran while one was open for 0% of the time, Pallas kernels for 24%

profile of v6, /device:TPU:24, one launch (start us, length us, event | category | flops | bytes accessed | tf_op | source)
XLA Modules:
  0.0 71.2 jit_solution(13715879348307018728)
XLA Ops:
  0.0 0.8 %pad_maximum_fusion.3 = (f32[2,3,8,128]{3,2,1,0:T(8,128)S(1)}, f32[2,3,8,128]{3,2,1,0:T(8,128)S(1)}) fusion(f32[8,1,8,128]{3,2,1,0:T(8,128)} %bitcast.11, f32[8,1,8,128]{3,2,1,0:T(8,128)} %bitcast.13, f32[8,1,8,128]{3,2,1,0:T(8,128)} %bitcast.15), kind=kLoop, calls=%fused_computation.3 | loop fusion | flops 24576 | bytes 147456 | tf_op jit(solution)/shard_map/slice | solution.py:497
  0.8 1.5 %collective-permute-start = (f32[2,3,8,128]{3,2,1,0:T(8,128)S(1)}, f32[2,3,8,128]{3,2,1,0:T(8,128)S(1)}, u32[]{:S(2)}, u32[]{:S(2)}) collective-permute-start(f32[2,3,8,128]{3,2,1,0:T(8,128)S(1)} %get-tuple-element.43), channel_id=1, source_target_pairs={{0,8},{8,16},{16,24},{24,32},{32,40},{40,48},{48,56},{56,64},{64,7... | collective-permute-start | bytes 73736 | tf_op jit(solution)/shard_map/ppermute | solution.py:497
  2.3 4.8 %collective-permute-start.1 = (f32[2,3,8,128]{3,2,1,0:T(8,128)S(1)}, f32[2,3,8,128]{3,2,1,0:T(8,128)S(1)}, u32[]{:S(2)}, u32[]{:S(2)}) collective-permute-start(f32[2,3,8,128]{3,2,1,0:T(8,128)S(1)} %get-tuple-element.44), channel_id=1, source_target_pairs={{8,0},{16,8},{24,16},{32,24},{40,32},{48,40},{56,48},{64,56},{72,6... | collective-permute-start | bytes 73736 | tf_op jit(solution)/shard_map/ppermute | solution.py:498
  7.1 0.0 copy-start
  7.1 2.4 %copy-done = bf16[10,10,64,3,128]{4,2,3,1,0:T(8,128)(2,1)S(1)} copy-done((bf16[10,10,64,3,128]{4,2,3,1,0:T(8,128)(2,1)S(1)}, bf16[10,10,64,3,128]{4,2,3,1,0:T(8,128)(2,1)}, u32[]{:S(2)}) %copy-start) | copy-done | bytes 4915224
  9.5 0.0 copy-start.1
  9.5 0.0 copy-start.2
  9.5 0.0 copy-start.3
  9.5 0.0 slice-start
  9.5 0.7 pack.1
  10.2 0.0 collective-permute-done
  10.2 0.0 collective-permute-done.1
  10.2 0.0 copy-done.1
  10.3 0.0 copy-done.2
  10.3 0.0 copy-done.3
  10.3 0.0 slice-start.1
  10.4 0.0 collective-permute-start.4
  10.4 0.5 collective-permute-start.3
  10.9 1.1 %collective-permute-done.4.hi_ref.refs_3_ = f32[12,3,2,128]{3,2,1,0:T(2,128)S(1)} collective-permute-done((f32[12,3,2,128]{3,2,1,0:T(2,128)S(1)}, f32[12,3,2,128]{3,2,1,0:T(2,128)S(1)}, u32[]{:S(2)}, u32[]{:S(2)}) %collective-permute-start.4) | collective-permute-done | bytes 36896 | tf_op jit(solution)/shard_map/ppermute | solution.py:505
  12.0 1.8 %collective-permute-done.3.lo_ref.refs_2_ = f32[12,3,2,128]{3,2,1,0:T(2,128)S(1)} collective-permute-done((f32[12,3,2,128]{3,2,1,0:T(2,128)S(1)}, f32[12,3,2,128]{3,2,1,0:T(2,128)S(1)}, u32[]{:S(2)}, u32[]{:S(2)}) %collective-permute-start.3) | collective-permute-done | bytes 36896 | tf_op jit(solution)/shard_map/ppermute | solution.py:504
  13.8 0.7 %collective-permute-start.5 = (bf16[10,3,3,64,128]{4,3,2,1,0:T(8,128)(2,1)S(1)}, bf16[10,3,3,64,128]{4,3,2,1,0:T(8,128)(2,1)S(1)}, u32[]{:S(2)}, u32[]{:S(2)}) collective-permute-start(bf16[10,3,3,64,128]{4,3,2,1,0:T(8,128)(2,1)S(1)} %get-tuple-element.32), channel_id=1, source_target_pairs={{0,1},{1,2},{2,3},{3,4},{4,5},{5,6},{6,7},{7,0},{8,9},{9,10},{10,1... | collective-permute-start | bytes 4423688 | tf_op jit(solution)/shard_map/ppermute | solution.py:543
  14.6 1.0 %collective-permute-start.6 = (bf16[10,3,3,64,128]{4,3,2,1,0:T(8,128)(2,1)S(1)}, bf16[10,3,3,64,128]{4,3,2,1,0:T(8,128)(2,1)S(1)}, u32[]{:S(2)}, u32[]{:S(2)}) collective-permute-start(bf16[10,3,3,64,128]{4,3,2,1,0:T(8,128)(2,1)S(1)} %get-tuple-element.33), channel_id=1, source_target_pairs={{1,0},{2,1},{3,2},{4,3},{5,4},{6,5},{7,6},{0,7},{9,8},{10,9},{11,1... | collective-permute-start | bytes 4423688 | tf_op jit(solution)/shard_map/ppermute | solution.py:544
  15.6 4.0 %collective-permute-start.2 = (bf16[3,10,3,64,128]{4,3,2,1,0:T(8,128)(2,1)S(1)}, bf16[3,10,3,64,128]{4,3,2,1,0:T(8,128)(2,1)S(1)}, u32[]{:S(2)}, u32[]{:S(2)}) collective-permute-start(bf16[3,10,3,64,128]{4,3,2,1,0:T(8,128)(2,1)S(1)} %get-tuple-element.27), channel_id=1, source_target_pairs={{8,0},{16,8},{24,16},{32,24},{40,32},{48,40},{56,48},{64,56},{72,6... | collective-permute-start | bytes 4423688 | tf_op jit(solution)/shard_map/ppermute | solution.py:538
  19.5 0.0 collective-permute-start.7
  19.5 0.0 slice-done
  19.5 0.0 slice-done.1
  19.6 12.5 %own_gram.1 = (f32[64,64]{1,0:T(8,128)S(1)}, f32[12,6,12,128]{3,2,1,0:T(8,128)S(1)}, bf16[12,36,128,128]{3,2,1,0:T(8,128)(2,1)S(1)}) custom-call(bf16[10,30,64,128]{3,2,1,0:T(8,128)(2,1)S(1)} %bitcast.10, f32[12,3,8,128]{3,2,1,0:T(8,128)S(1)} %get-tuple-element.28.mid_ref, f32[12,3,2,128]{3,2,1,0:T(2,128)S(1)} %collective-permute-done.3.lo_ref.refs_2_, ...), custom_call_target="tpu_custom_call" | custom-call | flops 1000 | bytes 1000 | tf_op jit(solution)/shard_map/own_gram/pallas_call | solution.py:546
  32.0 0.6 collective-permute-done.5.south_ref
  32.6 0.0 collective-permute-done.6.north_ref
  32.6 3.4 %row_gram.1 = (f32[64,128]{1,0:T(8,128)S(1)}, bf16[2,2,27,128,128]{4,3,2,1,0:T(8,128)(2,1)S(1)}) custom-call(bf16[10,3,3,64,128]{4,3,2,1,0:T(8,128)(2,1)S(1)} %collective-permute-done.5.south_ref, bf16[10,3,3,64,128]{4,3,2,1,0:T(8,128)(2,1)S(1)} %collective-permute-done.6.north_ref, bf16[12,36,128,128]{3,2,1,0:T(8,128)(2,1)S(1)} %get-tuple-element.29.img_ref, ...), custom_call_target="tpu_custom_call" | custom-call | flops 1000 | bytes 1000 | tf_op jit(solution)/shard_map/row_gram/pallas_call | solution.py:562
  36.0 0.0 collective-permute-done.7.corner_ref
  36.0 0.7 %corner_gram.1 = (f32[64,64]{1,0:T(8,128)S(1)}, f32[64,64]{1,0:T(8,128)S(1)}) custom-call(bf16[3,3,3,64,128]{4,3,2,1,0:T(8,128)(2,1)S(1)} %collective-permute-done.7.corner_ref, bf16[2,2,27,128,128]{4,3,2,1,0:T(8,128)(2,1)S(1)} %get-tuple-element.35.cimg_ref), custom_call_target="tpu_custom_call" | custom-call | flops 1000 | bytes 1000 | tf_op jit(solution)/shard_map/corner_gram/pallas_call | solution.py:574
  36.7 4.9 %collective-permute-start.8 = (f32[64,64]{1,0:T(8,128)S(1)}, f32[64,64]{1,0:T(8,128)S(1)}, u32[]{:S(2)}, u32[]{:S(2)}) collective-permute-start(f32[64,64]{1,0:T(8,128)S(1)} %get-tuple-element.39), channel_id=1, source_target_pairs={{0,1},{1,2},{2,3},{3,4},{4,5},{5,6},{6,7},{7,0},{8,9},{9,10},{10,1... | collective-permute-start | bytes 49160 | tf_op jit(solution)/shard_map/ppermute | solution.py:583
  41.6 0.0 collective-permute-done.2.main_ref
  41.6 0.9 %collective-permute-done.8.below_ref = f32[64,64]{1,0:T(8,128)S(1)} collective-permute-done((f32[64,64]{1,0:T(8,128)S(1)}, f32[64,64]{1,0:T(8,128)S(1)}, u32[]{:S(2)}, u32[]{:S(2)}) %collective-permute-start.8) | collective-permute-done | bytes 16416 | tf_op jit(solution)/shard_map/ppermute | solution.py:583
  42.5 1.8 %column_gram.1 = bf16[16,64,512]{2,1,0:T(8,128)(2,1)S(1)} custom-call(bf16[3,10,3,64,128]{4,3,2,1,0:T(8,128)(2,1)S(1)} %collective-permute-done.2.main_ref, bf16[12,36,128,128]{3,2,1,0:T(8,128)(2,1)S(1)} %get-tuple-element.29.img_ref, bf16[2,2,27,128,128]{4,3,2,1,0:T(8,128)(2,1)S(1)} %get-tuple-element.35.cimg_ref, f32[64,64]{1,0:T(8,128)S(1)} %get-tuple-element.36.own_ref, ...), custom_call_target="tpu_custom_call" | custom-call | flops 1000 | bytes 1000 | tf_op jit(solution)/shard_map/column_gram/pallas_call | solution.py:584
  44.3 22.6 %all_to_all.5.code_ref = bf16[16,64,512]{2,1,0:T(8,128)(2,1)S(1)} all-to-all(bf16[16,64,512]{2,1,0:T(8,128)(2,1)S(1)} %column_gram.1), channel_id=1, replica_groups=mesh['sx'=16,'sy'=8] {'sx'}, dimensions={0} | all-to-all | bytes 2097152 | tf_op jit(solution)/shard_map/all_to_all | solution.py:593
  66.9 4.3 %assemble.1 = f32[16,64,576]{2,1,0:T(8,128)} custom-call(bf16[16,64,512]{2,1,0:T(8,128)(2,1)S(1)} %all_to_all.5.code_ref), custom_call_target="tpu_custom_call" | custom-call | flops 1000 | bytes 1000 | tf_op jit(solution)/shard_map/assemble/pallas_call | solution.py:594
  (5 shorter events, 0.0 us)
Async XLA Ops:
  0.8 9.4 %collective-permute-start = (f32[2,3,8,128]{3,2,1,0:T(8,128)S(1)}, f32[2,3,8,128]{3,2,1,0:T(8,128)S(1)}, u32[]{:S(2)}, u32[]{:S(2)}) collective-permute-start(f32[2,3,8,128]{3,2,1,0:T(8,128)S(1)} %get-tuple-element.43), channel_id=1, source_target_pairs={{0,8},{8,16},{16,24},{24,32},{32,40},{40,48},{48,56},{56,64},{64,7... | collective-permute-start | bytes 73736 | tf_op jit(solution)/shard_map/ppermute | solution.py:497
  2.3 7.9 %collective-permute-start.1 = (f32[2,3,8,128]{3,2,1,0:T(8,128)S(1)}, f32[2,3,8,128]{3,2,1,0:T(8,128)S(1)}, u32[]{:S(2)}, u32[]{:S(2)}) collective-permute-start(f32[2,3,8,128]{3,2,1,0:T(8,128)S(1)} %get-tuple-element.44), channel_id=1, source_target_pairs={{8,0},{16,8},{24,16},{32,24},{40,32},{48,40},{56,48},{64,56},{72,6... | collective-permute-start | bytes 73736 | tf_op jit(solution)/shard_map/ppermute | solution.py:498
  7.1 2.4 %copy-start = (bf16[10,10,64,3,128]{4,2,3,1,0:T(8,128)(2,1)S(1)}, bf16[10,10,64,3,128]{4,2,3,1,0:T(8,128)(2,1)}, u32[]{:S(2)}) copy-start(bf16[10,10,64,3,128]{4,2,3,1,0:T(8,128)(2,1)} %param.4) | copy-start | bytes 14745604
  9.5 0.8 %copy-start.1 = (f32[8,8,128]{2,1,0:T(8,128)S(1)}, f32[8,8,128]{2,1,0:T(8,128)}, u32[]{:S(2)}) copy-start(f32[8,8,128]{2,1,0:T(8,128)} %param.7) | copy-start | bytes 98308
  9.5 0.8 %copy-start.2 = (f32[8,8,128]{2,1,0:T(8,128)S(1)}, f32[8,8,128]{2,1,0:T(8,128)}, u32[]{:S(2)}) copy-start(f32[8,8,128]{2,1,0:T(8,128)} %param.6) | copy-start | bytes 98308
  9.5 0.8 %copy-start.3 = (f32[8,8,128]{2,1,0:T(8,128)S(1)}, f32[8,8,128]{2,1,0:T(8,128)}, u32[]{:S(2)}) copy-start(f32[8,8,128]{2,1,0:T(8,128)} %param.5) | copy-start | bytes 98308
  9.5 10.0 %slice-start = ((s8[4915200]{0:T(1024)(128)(4,1)}), s8[720896]{0:T(1024)(128)(4,1)S(1)}, s32[]{:S(2)}) async-start(s8[4915200]{0:T(1024)(128)(4,1)} %bitcast.8), calls=%async_computation.1 | async-start | bytes 1441792
  10.3 9.2 %slice-start.1 = ((s8[4915200]{0:T(1024)(128)(4,1)}), s8[4194304]{0:T(1024)(128)(4,1)S(1)}, s32[]{:S(2)}) async-start(s8[4915200]{0:T(1024)(128)(4,1)} %bitcast.8), calls=%async_computation.2 | async-start | bytes 8388608
  10.4 1.7 %collective-permute-start.4 = (f32[12,3,2,128]{3,2,1,0:T(2,128)S(1)}, f32[12,3,2,128]{3,2,1,0:T(2,128)S(1)}, u32[]{:S(2)}, u32[]{:S(2)}) collective-permute-start(f32[12,3,2,128]{3,2,1,0:T(2,128)S(1)} %get-tuple-element.41), channel_id=1, source_target_pairs={{1,0},{2,1},{3,2},{4,3},{5,4},{6,5},{7,6},{0,7},{9,8},{10,9},{11,1... | collective-permute-start | bytes 110600 | tf_op jit(solution)/shard_map/ppermute | solution.py:505
  10.4 3.4 %collective-permute-start.3 = (f32[12,3,2,128]{3,2,1,0:T(2,128)S(1)}, f32[12,3,2,128]{3,2,1,0:T(2,128)S(1)}, u32[]{:S(2)}, u32[]{:S(2)}) collective-permute-start(f32[12,3,2,128]{3,2,1,0:T(2,128)S(1)} %get-tuple-element.42), channel_id=1, source_target_pairs={{0,1},{1,2},{2,3},{3,4},{4,5},{5,6},{6,7},{7,0},{8,9},{9,10},{10,1... | collective-permute-start | bytes 110600 | tf_op jit(solution)/shard_map/ppermute | solution.py:504
  13.8 18.8 %collective-permute-start.5 = (bf16[10,3,3,64,128]{4,3,2,1,0:T(8,128)(2,1)S(1)}, bf16[10,3,3,64,128]{4,3,2,1,0:T(8,128)(2,1)S(1)}, u32[]{:S(2)}, u32[]{:S(2)}) collective-permute-start(bf16[10,3,3,64,128]{4,3,2,1,0:T(8,128)(2,1)S(1)} %get-tuple-element.32), channel_id=1, source_target_pairs={{0,1},{1,2},{2,3},{3,4},{4,5},{5,6},{6,7},{7,0},{8,9},{9,10},{10,1... | collective-permute-start | bytes 4423688 | tf_op jit(solution)/shard_map/ppermute | solution.py:543
  14.6 18.0 %collective-permute-start.6 = (bf16[10,3,3,64,128]{4,3,2,1,0:T(8,128)(2,1)S(1)}, bf16[10,3,3,64,128]{4,3,2,1,0:T(8,128)(2,1)S(1)}, u32[]{:S(2)}, u32[]{:S(2)}) collective-permute-start(bf16[10,3,3,64,128]{4,3,2,1,0:T(8,128)(2,1)S(1)} %get-tuple-element.33), channel_id=1, source_target_pairs={{1,0},{2,1},{3,2},{4,3},{5,4},{6,5},{7,6},{0,7},{9,8},{10,9},{11,1... | collective-permute-start | bytes 4423688 | tf_op jit(solution)/shard_map/ppermute | solution.py:544
  15.6 26.1 %collective-permute-start.2 = (bf16[3,10,3,64,128]{4,3,2,1,0:T(8,128)(2,1)S(1)}, bf16[3,10,3,64,128]{4,3,2,1,0:T(8,128)(2,1)S(1)}, u32[]{:S(2)}, u32[]{:S(2)}) collective-permute-start(bf16[3,10,3,64,128]{4,3,2,1,0:T(8,128)(2,1)S(1)} %get-tuple-element.27), channel_id=1, source_target_pairs={{8,0},{16,8},{24,16},{32,24},{40,32},{48,40},{56,48},{64,56},{72,6... | collective-permute-start | bytes 4423688 | tf_op jit(solution)/shard_map/ppermute | solution.py:538
  19.5 16.4 %collective-permute-start.7 = (bf16[3,3,3,64,128]{4,3,2,1,0:T(8,128)(2,1)S(1)}, bf16[3,3,3,64,128]{4,3,2,1,0:T(8,128)(2,1)S(1)}, u32[]{:S(2)}, u32[]{:S(2)}) collective-permute-start(bf16[3,3,3,64,128]{4,3,2,1,0:T(8,128)(2,1)S(1)} %get-tuple-element.38), channel_id=1, source_target_pairs={{0,8},{8,16},{16,24},{24,32},{32,40},{40,48},{48,56},{56,64},{64,7... | collective-permute-start | bytes 1327112 | tf_op jit(solution)/shard_map/ppermute | solution.py:539
  36.7 5.8 %collective-permute-start.8 = (f32[64,64]{1,0:T(8,128)S(1)}, f32[64,64]{1,0:T(8,128)S(1)}, u32[]{:S(2)}, u32[]{:S(2)}) collective-permute-start(f32[64,64]{1,0:T(8,128)S(1)} %get-tuple-element.39), channel_id=1, source_target_pairs={{0,1},{1,2},{2,3},{3,4},{4,5},{5,6},{6,7},{7,0},{8,9},{9,10},{10,1... | collective-permute-start | bytes 49160 | tf_op jit(solution)/shard_map/ppermute | solution.py:583

commit v7 on v6

--- a/solution.py
+++ b/solution.py
@@ -94,7 +94,11 @@
     here = jnp.where(is_odd(), ext - 3, 0)
     there = jnp.where(is_odd(), 0, ext - 3)
     copies = [
-        pltpu.make_async_copy(m_hbm.at[pl.ds(here, 3)], main_ref, sems.at[0]),
+        pltpu.make_async_copy(m_hbm.at[here + i], main_ref.at[pl.ds(i * ext, ext)], sems.at[4 + i])
+        for i in range(3)
+    ]
+    main_ref[3 * ext] = jnp.zeros(main_ref.shape[1:], BF16)
+    copies += [
         pltpu.make_async_copy(
             m_hbm.at[pl.ds(there, 3), pl.ds(ext - 3, 3)], corner_ref, sems.at[1]
         ),
@@ -168,7 +172,7 @@
     def image(f, chunk, edge=None, last=False):
         rows = pl.ds(pl.multiple_of(chunk * 16, 16), 16)
         low_rows = pl.ds(pl.multiple_of(64 + chunk * 16, 16), 16)
-        for g in range(frame):
+        for g in range(frame) if edge is None else range(1, ext + 1):
             values = None
             if 1 <= g <= ext and edge is None:
                 values = [m_ref[f - 1, (g - 1) * 3 + a, rows, :].astype(F32) for a in range(3)]
@@ -228,11 +232,17 @@
         image(ext, chunk, None, True)
 
     chunks(inner_last)
-    chunks(lambda chunk: dot(ext, chunk))
+    @pl.when(odd)
+    def _():
+        chunks(lambda chunk: dot(ext, chunk))
 
     @pl.when(jnp.logical_not(odd))
     def _():
-        chunks(lambda chunk: image(ext + 1, chunk, ext))
+        def inner_rim(chunk):
+            dot(ext, chunk)
+            image(ext + 1, chunk, ext)
+
+        chunks(inner_rim)
 
     out_ref[...] = fold(acc_ref[...])
 
@@ -250,15 +260,15 @@
             lines = side([img_ref[x + 1, s * (ext - 1) * 3 + i] for i in range(9)])
             acc_ref[s] += lax.dot_general(lines, right, NT, preferred_element_type=F32)
 
-    def corner(s, t, chunk):
+    def corner(s, t, chunk, use):
         raw_y = (2, 1, 0) if s == 0 else (0, 1, 2)
         raw_g = (2, 1, 0) if s == 0 else (9, 10, 11)
         img_g = (3, 2, 1) if s == 0 else (8, 9, 10)
         img_y = (2, 1, 0) if s == 0 else (0, 1, 2)
-        raw_x = (0, 1, 2) if t == 0 else (9, 8, 7)
-        raw_f = (1, 2, 3) if t == 0 else (10, 9, 8)
-        img_f = (0, 1, 2) if t == 0 else (11, 10, 9)
-        img_x = (0, 1, 2) if t == 0 else (2, 1, 0)
+        raw_x = [c + t * (ext - 1 - 2 * c) for c in range(3)]
+        raw_f = [1 + c + t * (ext - 1 - 2 * c) for c in range(3)]
+        img_f = [c + t * (ext + 1 - 2 * c) for c in range(3)]
+        img_x = [c + t * (2 - 2 * c) for c in range(3)]
         rows = pl.ds(pl.multiple_of(chunk * 16, 16), 16)
         low_rows = pl.ds(pl.multiple_of(64 + chunk * 16, 16), 16)
         for a in range(3):
@@ -274,7 +284,7 @@
                 across.append(spread3(w))
             for e in range(3):
                 for c, value in enumerate(spread3([across[i][e] for i in range(3)])):
-                    z_ref[s, c, e, a] = value
+                    z_ref[use, c, e, a] = value
         for c in range(3):
             for e in range(3):
                 values = None
@@ -284,7 +294,7 @@
                         for a in range(3)
                     ]
                 image = cell_image(
-                    [z_ref[s, c, e, a] for a in range(3)], values,
+                    [z_ref[use, c, e, a] for a in range(3)], values,
                     coef_rows(coef_ref, img_f[c], img_g[e], (DIA, VOL, OUT)),
                 )
                 for a in range(3):
@@ -293,15 +303,17 @@
                     cimg_ref[t, s, tile, rows, :] = high
                     cimg_ref[t, s, tile, low_rows, :] = (image[a] - high.astype(F32)).astype(BF16)
 
-    for t in range(2):
-
-        def step(chunk, _, t=t):
-            dots(t * 4 + chunk)
-            corner(0, t, chunk)
-            corner(1, t, chunk)
-            return 0
-
-        lax.fori_loop(0, 4, step, 0, unroll=2)
+    main_side = 1 - is_odd().astype(jnp.int32)
+
+    def step(chunk, _):
+        dots(2 * chunk)
+        dots(2 * chunk + 1)
+        corner(0, main_side, chunk, 0)
+        corner(1, 0, chunk, 1)
+        corner(1, 1, chunk, 2)
+        return 0
+
+    lax.fori_loop(0, 4, step, 0, unroll=2)
     for x in range(8, ext):
         dots(x)
     out_ref[...] = side([fold_rows(acc_ref[0]), fold_rows(acc_ref[1])])
@@ -331,16 +343,16 @@
 
 def main_kernel(main_ref, img_ref, cimg_ref, own_ref, rows_ref, below_ref, keep_ref, out_ref):
     t = 1 - is_odd().astype(jnp.int32)
-    ext = main_ref.shape[1]
+    ext = main_ref.shape[0] // 3
     start = jnp.where(is_odd(), 0, ext - 1)
     total = None
     for i in range(3):
-        right = side([main_ref[i, j, a] for j in range(ext) for a in range(3)])
+        right = side([main_ref[i * ext + j, a] for j in range(ext) for a in range(3)])
         lines = side([img_ref[start + i, 3 + j] for j in range(ext * 3)])
         part = lax.dot_general(lines, right, NT, preferred_element_type=F32)
         total = part if total is None else total + part
-    south = corner_dot(lambda i, j, a: main_ref[i, j, a], lambda i: cimg_ref[t, 0, i])
-    north = corner_dot(lambda i, j, a: main_ref[i, ext - 3 + j, a], lambda i: cimg_ref[t, 1, i])
+    south = corner_dot(lambda i, j, a: main_ref[i * ext + j, a], lambda i: cimg_ref[t, 0, i])
+    north = corner_dot(lambda i, j, a: main_ref[i * ext + ext - 3 + j, a], lambda i: cimg_ref[t, 1, i])
     low, high, beside = has_y(-1), has_y(1), has_x(True)
     around = rows_ref[...]
     blocks = [
@@ -517,14 +529,14 @@
     main, corner, south, north = call(
         pack_kernel,
         [
-            shape(3, ext, 3, 64, 128, dtype=BF16),
+            shape(3 * ext + 1, 3, 64, 128, dtype=BF16),
             shape(3, 3, 3, 64, 128, dtype=BF16),
             shape(ext, 3, 3, 64, 128, dtype=BF16),
             shape(ext, 3, 3, 64, 128, dtype=BF16),
         ],
         [vmem_spec()],
         [vmem_spec()] * 4,
-        [pltpu.SemaphoreType.DMA((4,))],
+        [pltpu.SemaphoreType.DMA((7,))],
         8,
         "pack",
     )(m)
@@ -565,7 +577,7 @@
         [vmem_spec()] * 4,
         [vmem_spec(), vmem_spec()],
         [
-            pltpu.VMEM((2, 3, 3, 3, 16, 128), F32),
+            pltpu.VMEM((3, 3, 3, 3, 16, 128), F32),
             pltpu.VMEM((2, 128, 64), F32),
         ],
         8,

time: 71.5 us -> 70.5 us (0.986)
  starting transfers between devices: 17.5 us -> 16.4 us
  waiting for transfers between devices: 4.32 us -> 5.34 us
  blocking collectives: 22.6 us -> 21.6 us
    ppermute x1, waiting for transfers between devices: 0.55 us -> 4.46 us  [local(): south = lax.ppermute(south, 'sy', up)]
    ppermute x1, waiting for transfers between devices: 1.77 us -> 0.01 us  [coef_edges(): lo = lax.ppermute(mid[:, :, -2:], 'sy', up)]
    ppermute x1, waiting for transfers between devices: 1.13 us -> 0.01 us  [coef_edges(): hi = lax.ppermute(mid[:, :, :2], 'sy', down)]
    all_to_all x1, blocking collectives: 22.6 us -> 21.6 us  [local(): code = lax.all_to_all(code, 'sx', 0, 0)]
  transfers between devices with their start and end apart: 9 -> 9, of which waited for: 4 -> 2; matrix products, arithmetic and copies ran while one was open for 0% -> 0% of each run, Pallas kernels for 24% -> 25%
where the time goes in v7:
time: 70.5 us; the launch traced here: 70.3 us
  Pallas kernels  23.5 us (33%)
  blocking collectives  21.6 us (31%)
  starting transfers between devices  16.4 us (23%)
  waiting for transfers between devices  5.34 us (8%)
  local copies, waits for them, and re-layouts  2.44 us (3%)
  other arithmetic  0.8 us (1%)
    all_to_all x1, blocking collectives, local(): code = lax.all_to_all(code, 'sx', 0, 0)  21.6 us
    pallas_call x1, Pallas kernels, local(): call(own_kernel, [shape(64, 64), shape(frame, 6, frame, 128), shape(frame...  12.6 us
    ppermute x1, starting transfers between devices, coef_columns(): high = lax.ppermute(own[:2], 'sx', down)  4.82 us
    ppermute x1, waiting for transfers between devices, local(): south = lax.ppermute(south, 'sy', up)  4.46 us
    ppermute x1, starting transfers between devices, local(): below = lax.ppermute(turned, 'sy', up)  4.45 us
    pallas_call x1, Pallas kernels, local(): call(final_kernel, shape(nx, 64, 576), [vmem_spec()], any_spec(), [pltpu....  4.33 us
    ppermute x1, starting transfers between devices, local(): main = lax.ppermute(main, ('sx', 'sy'), main_pairs)  3.35 us
    pallas_call x1, Pallas kernels, local(): call(rows_kernel, [shape(64, 128), shape(2, 2, 27, 128, 128, dtype=BF16)]...  2.79 us
  transfers between devices with their start and end apart: 9, of which 2 were waited for; matrix products, arithmetic and copies ran while one was open for 0% of the time, Pallas kernels for 25%

profile of v7, /device:TPU:24, one launch (start us, length us, event | category | flops | bytes accessed | tf_op | source)
XLA Modules:
  0.0 70.3 jit_solution(8996706480524073814)
XLA Ops:
  0.0 0.8 %pad_maximum_fusion.3 = (f32[2,3,8,128]{3,2,1,0:T(8,128)S(1)}, f32[2,3,8,128]{3,2,1,0:T(8,128)S(1)}) fusion(f32[8,1,8,128]{3,2,1,0:T(8,128)} %bitcast.11, f32[8,1,8,128]{3,2,1,0:T(8,128)} %bitcast.13, f32[8,1,8,128]{3,2,1,0:T(8,128)} %bitcast.15), kind=kLoop, calls=%fused_computation.3 | loop fusion | flops 24576 | bytes 147456 | tf_op jit(solution)/shard_map/slice | solution.py:509
  0.8 1.5 %collective-permute-start = (f32[2,3,8,128]{3,2,1,0:T(8,128)S(1)}, f32[2,3,8,128]{3,2,1,0:T(8,128)S(1)}, u32[]{:S(2)}, u32[]{:S(2)}) collective-permute-start(f32[2,3,8,128]{3,2,1,0:T(8,128)S(1)} %get-tuple-element.43), channel_id=1, source_target_pairs={{0,8},{8,16},{16,24},{24,32},{32,40},{40,48},{48,56},{56,64},{64,7... | collective-permute-start | bytes 73736 | tf_op jit(solution)/shard_map/ppermute | solution.py:509
  2.3 4.8 %collective-permute-start.1 = (f32[2,3,8,128]{3,2,1,0:T(8,128)S(1)}, f32[2,3,8,128]{3,2,1,0:T(8,128)S(1)}, u32[]{:S(2)}, u32[]{:S(2)}) collective-permute-start(f32[2,3,8,128]{3,2,1,0:T(8,128)S(1)} %get-tuple-element.44), channel_id=1, source_target_pairs={{8,0},{16,8},{24,16},{32,24},{40,32},{48,40},{56,48},{64,56},{72,6... | collective-permute-start | bytes 73736 | tf_op jit(solution)/shard_map/ppermute | solution.py:510
  7.1 0.0 copy-start
  7.1 2.4 %copy-done = bf16[10,10,64,3,128]{4,2,3,1,0:T(8,128)(2,1)S(1)} copy-done((bf16[10,10,64,3,128]{4,2,3,1,0:T(8,128)(2,1)S(1)}, bf16[10,10,64,3,128]{4,2,3,1,0:T(8,128)(2,1)}, u32[]{:S(2)}) %copy-start) | copy-done | bytes 4915224
  9.5 0.0 copy-start.1
  9.5 0.0 copy-start.2
  9.5 0.0 copy-start.3
  9.5 0.0 slice-start
  9.5 1.3 %pack.1 = (bf16[31,3,64,128]{3,2,1,0:T(8,128)(2,1)S(1)}, bf16[3,3,3,64,128]{4,3,2,1,0:T(8,128)(2,1)S(1)}, bf16[10,3,3,64,128]{4,3,2,1,0:T(8,128)(2,1)S(1)}, bf16[10,3,3,64,128]{4,3,2,1,0:T(8,128)(2,1)S(1)}) custom-call(bf16[10,10,3,64,128]{4,3,2,1,0:T(8,128)(2,1)S(1)} %bitcast.7), custom_call_target="tpu_custom_call" | custom-call | flops 1000 | bytes 1000 | tf_op jit(solution)/shard_map/pack/pallas_call | solution.py:529
  10.9 0.0 collective-permute-done
  10.9 0.0 collective-permute-done.1
  10.9 0.0 copy-done.1
  10.9 0.0 copy-done.2
  10.9 0.0 copy-done.3
  11.0 0.0 slice-start.1
  11.0 0.0 collective-permute-start.4
  11.0 0.5 collective-permute-start.3
  11.5 3.4 %collective-permute-start.2 = (bf16[31,3,64,128]{3,2,1,0:T(8,128)(2,1)S(1)}, bf16[31,3,64,128]{3,2,1,0:T(8,128)(2,1)S(1)}, u32[]{:S(2)}, u32[]{:S(2)}) collective-permute-start(bf16[31,3,64,128]{3,2,1,0:T(8,128)(2,1)S(1)} %get-tuple-element.27), channel_id=1, source_target_pairs={{8,0},{16,8},{24,16},{32,24},{40,32},{48,40},{56,48},{64,56},{72,6... | collective-permute-start | bytes 4571144 | tf_op jit(solution)/shard_map/ppermute | solution.py:550
  14.9 0.0 collective-permute-done.4.hi_ref.refs_3_
  14.9 0.0 collective-permute-done.3.lo_ref.refs_2_
  14.9 0.3 collective-permute-start.5
  15.2 1.5 %collective-permute-start.6 = (bf16[10,3,3,64,128]{4,3,2,1,0:T(8,128)(2,1)S(1)}, bf16[10,3,3,64,128]{4,3,2,1,0:T(8,128)(2,1)S(1)}, u32[]{:S(2)}, u32[]{:S(2)}) collective-permute-start(bf16[10,3,3,64,128]{4,3,2,1,0:T(8,128)(2,1)S(1)} %get-tuple-element.33), channel_id=1, source_target_pairs={{1,0},{2,1},{3,2},{4,3},{5,4},{6,5},{7,6},{0,7},{9,8},{10,9},{11,1... | collective-permute-start | bytes 4423688 | tf_op jit(solution)/shard_map/ppermute | solution.py:556
  16.6 0.0 collective-permute-start.7
  16.7 0.0 slice-done
  16.7 0.0 slice-done.1
  16.7 12.6 %own_gram.1 = (f32[64,64]{1,0:T(8,128)S(1)}, f32[12,6,12,128]{3,2,1,0:T(8,128)S(1)}, bf16[12,36,128,128]{3,2,1,0:T(8,128)(2,1)S(1)}) custom-call(bf16[10,30,64,128]{3,2,1,0:T(8,128)(2,1)S(1)} %bitcast.10, f32[12,3,8,128]{3,2,1,0:T(8,128)S(1)} %get-tuple-element.28.mid_ref, f32[12,3,2,128]{3,2,1,0:T(2,128)S(1)} %collective-permute-done.3.lo_ref.refs_2_, ...), custom_call_target="tpu_custom_call" | custom-call | flops 1000 | bytes 1000 | tf_op jit(solution)/shard_map/own_gram/pallas_call | solution.py:558
  29.2 4.5 %collective-permute-done.5.south_ref = bf16[10,3,3,64,128]{4,3,2,1,0:T(8,128)(2,1)S(1)} collective-permute-done((bf16[10,3,3,64,128]{4,3,2,1,0:T(8,128)(2,1)S(1)}, bf16[10,3,3,64,128]{4,3,2,1,0:T(8,128)(2,1)S(1)}, u32[]{:S(2)}, u32[]{:S(2)}) %collective-permute-start.5) | collective-permute-done | bytes 1474592 | tf_op jit(solution)/shard_map/ppermute | solution.py:555
  33.7 0.0 collective-permute-done.6.north_ref
  33.7 2.8 %row_gram.1 = (f32[64,128]{1,0:T(8,128)S(1)}, bf16[2,2,27,128,128]{4,3,2,1,0:T(8,128)(2,1)S(1)}) custom-call(bf16[10,3,3,64,128]{4,3,2,1,0:T(8,128)(2,1)S(1)} %collective-permute-done.5.south_ref, bf16[10,3,3,64,128]{4,3,2,1,0:T(8,128)(2,1)S(1)} %collective-permute-done.6.north_ref, bf16[12,36,128,128]{3,2,1,0:T(8,128)(2,1)S(1)} %get-tuple-element.29.img_ref, ...), custom_call_target="tpu_custom_call" | custom-call | flops 1000 | bytes 1000 | tf_op jit(solution)/shard_map/row_gram/pallas_call | solution.py:574
  36.5 0.0 collective-permute-done.7.corner_ref
  36.5 0.7 %corner_gram.1 = (f32[64,64]{1,0:T(8,128)S(1)}, f32[64,64]{1,0:T(8,128)S(1)}) custom-call(bf16[3,3,3,64,128]{4,3,2,1,0:T(8,128)(2,1)S(1)} %collective-permute-done.7.corner_ref, bf16[2,2,27,128,128]{4,3,2,1,0:T(8,128)(2,1)S(1)} %get-tuple-element.35.cimg_ref), custom_call_target="tpu_custom_call" | custom-call | flops 1000 | bytes 1000 | tf_op jit(solution)/shard_map/corner_gram/pallas_call | solution.py:586
  37.2 4.5 %collective-permute-start.8 = (f32[64,64]{1,0:T(8,128)S(1)}, f32[64,64]{1,0:T(8,128)S(1)}, u32[]{:S(2)}, u32[]{:S(2)}) collective-permute-start(f32[64,64]{1,0:T(8,128)S(1)} %get-tuple-element.39), channel_id=1, source_target_pairs={{0,1},{1,2},{2,3},{3,4},{4,5},{5,6},{6,7},{7,0},{8,9},{9,10},{10,1... | collective-permute-start | bytes 49160 | tf_op jit(solution)/shard_map/ppermute | solution.py:595
  41.7 0.0 collective-permute-done.2.main_ref
  41.7 0.9 %collective-permute-done.8.below_ref = f32[64,64]{1,0:T(8,128)S(1)} collective-permute-done((f32[64,64]{1,0:T(8,128)S(1)}, f32[64,64]{1,0:T(8,128)S(1)}, u32[]{:S(2)}, u32[]{:S(2)}) %collective-permute-start.8) | collective-permute-done | bytes 16416 | tf_op jit(solution)/shard_map/ppermute | solution.py:595
  42.5 1.8 %column_gram.1 = bf16[16,64,512]{2,1,0:T(8,128)(2,1)S(1)} custom-call(bf16[31,3,64,128]{3,2,1,0:T(8,128)(2,1)S(1)} %collective-permute-done.2.main_ref, bf16[12,36,128,128]{3,2,1,0:T(8,128)(2,1)S(1)} %get-tuple-element.29.img_ref, bf16[2,2,27,128,128]{4,3,2,1,0:T(8,128)(2,1)S(1)} %get-tuple-element.35.cimg_ref, f32[64,64]{1,0:T(8,128)S(1)} %get-tuple-element.36.own_ref, ...), custom_call_target="tpu_custom_call" | custom-call | flops 1000 | bytes 1000 | tf_op jit(solution)/shard_map/column_gram/pallas_call | solution.py:596
  44.3 21.6 %all_to_all.5.code_ref = bf16[16,64,512]{2,1,0:T(8,128)(2,1)S(1)} all-to-all(bf16[16,64,512]{2,1,0:T(8,128)(2,1)S(1)} %column_gram.1), channel_id=1, replica_groups=mesh['sx'=16,'sy'=8] {'sx'}, dimensions={0} | all-to-all | bytes 2097152 | tf_op jit(solution)/shard_map/all_to_all | solution.py:605
  65.9 4.3 %assemble.1 = f32[16,64,576]{2,1,0:T(8,128)} custom-call(bf16[16,64,512]{2,1,0:T(8,128)(2,1)S(1)} %all_to_all.5.code_ref), custom_call_target="tpu_custom_call" | custom-call | flops 1000 | bytes 1000 | tf_op jit(solution)/shard_map/assemble/pallas_call | solution.py:606
  (5 shorter events, 0.0 us)
Async XLA Ops:
  0.8 10.1 %collective-permute-start = (f32[2,3,8,128]{3,2,1,0:T(8,128)S(1)}, f32[2,3,8,128]{3,2,1,0:T(8,128)S(1)}, u32[]{:S(2)}, u32[]{:S(2)}) collective-permute-start(f32[2,3,8,128]{3,2,1,0:T(8,128)S(1)} %get-tuple-element.43), channel_id=1, source_target_pairs={{0,8},{8,16},{16,24},{24,32},{32,40},{40,48},{48,56},{56,64},{64,7... | collective-permute-start | bytes 73736 | tf_op jit(solution)/shard_map/ppermute | solution.py:509
  2.3 8.6 %collective-permute-start.1 = (f32[2,3,8,128]{3,2,1,0:T(8,128)S(1)}, f32[2,3,8,128]{3,2,1,0:T(8,128)S(1)}, u32[]{:S(2)}, u32[]{:S(2)}) collective-permute-start(f32[2,3,8,128]{3,2,1,0:T(8,128)S(1)} %get-tuple-element.44), channel_id=1, source_target_pairs={{8,0},{16,8},{24,16},{32,24},{40,32},{48,40},{56,48},{64,56},{72,6... | collective-permute-start | bytes 73736 | tf_op jit(solution)/shard_map/ppermute | solution.py:510
  7.1 2.4 %copy-start = (bf16[10,10,64,3,128]{4,2,3,1,0:T(8,128)(2,1)S(1)}, bf16[10,10,64,3,128]{4,2,3,1,0:T(8,128)(2,1)}, u32[]{:S(2)}) copy-start(bf16[10,10,64,3,128]{4,2,3,1,0:T(8,128)(2,1)} %param.4) | copy-start | bytes 14745604
  9.5 1.4 %copy-start.1 = (f32[8,8,128]{2,1,0:T(8,128)S(1)}, f32[8,8,128]{2,1,0:T(8,128)}, u32[]{:S(2)}) copy-start(f32[8,8,128]{2,1,0:T(8,128)} %param.7) | copy-start | bytes 98308
  9.5 1.4 %copy-start.2 = (f32[8,8,128]{2,1,0:T(8,128)S(1)}, f32[8,8,128]{2,1,0:T(8,128)}, u32[]{:S(2)}) copy-start(f32[8,8,128]{2,1,0:T(8,128)} %param.6) | copy-start | bytes 98308
  9.5 1.4 %copy-start.3 = (f32[8,8,128]{2,1,0:T(8,128)S(1)}, f32[8,8,128]{2,1,0:T(8,128)}, u32[]{:S(2)}) copy-start(f32[8,8,128]{2,1,0:T(8,128)} %param.5) | copy-start | bytes 98308
  9.5 7.1 %slice-start = ((s8[4915200]{0:T(1024)(128)(4,1)}), s8[720896]{0:T(1024)(128)(4,1)S(1)}, s32[]{:S(2)}) async-start(s8[4915200]{0:T(1024)(128)(4,1)} %bitcast.8), calls=%async_computation.1 | async-start | bytes 1441792
  11.0 5.7 %slice-start.1 = ((s8[4915200]{0:T(1024)(128)(4,1)}), s8[4194304]{0:T(1024)(128)(4,1)S(1)}, s32[]{:S(2)}) async-start(s8[4915200]{0:T(1024)(128)(4,1)} %bitcast.8), calls=%async_computation.2 | async-start | bytes 8388608
  11.0 3.9 %collective-permute-start.4 = (f32[12,3,2,128]{3,2,1,0:T(2,128)S(1)}, f32[12,3,2,128]{3,2,1,0:T(2,128)S(1)}, u32[]{:S(2)}, u32[]{:S(2)}) collective-permute-start(f32[12,3,2,128]{3,2,1,0:T(2,128)S(1)} %get-tuple-element.41), channel_id=1, source_target_pairs={{1,0},{2,1},{3,2},{4,3},{5,4},{6,5},{7,6},{0,7},{9,8},{10,9},{11,1... | collective-permute-start | bytes 110600 | tf_op jit(solution)/shard_map/ppermute | solution.py:517
  11.0 3.9 %collective-permute-start.3 = (f32[12,3,2,128]{3,2,1,0:T(2,128)S(1)}, f32[12,3,2,128]{3,2,1,0:T(2,128)S(1)}, u32[]{:S(2)}, u32[]{:S(2)}) collective-permute-start(f32[12,3,2,128]{3,2,1,0:T(2,128)S(1)} %get-tuple-element.42), channel_id=1, source_target_pairs={{0,1},{1,2},{2,3},{3,4},{4,5},{5,6},{6,7},{7,0},{8,9},{9,10},{10,1... | collective-permute-start | bytes 110600 | tf_op jit(solution)/shard_map/ppermute | solution.py:516
  11.5 30.1 %collective-permute-start.2 = (bf16[31,3,64,128]{3,2,1,0:T(8,128)(2,1)S(1)}, bf16[31,3,64,128]{3,2,1,0:T(8,128)(2,1)S(1)}, u32[]{:S(2)}, u32[]{:S(2)}) collective-permute-start(bf16[31,3,64,128]{3,2,1,0:T(8,128)(2,1)S(1)} %get-tuple-element.27), channel_id=1, source_target_pairs={{8,0},{16,8},{24,16},{32,24},{40,32},{48,40},{56,48},{64,56},{72,6... | collective-permute-start | bytes 4571144 | tf_op jit(solution)/shard_map/ppermute | solution.py:550
  14.9 18.8 %collective-permute-start.5 = (bf16[10,3,3,64,128]{4,3,2,1,0:T(8,128)(2,1)S(1)}, bf16[10,3,3,64,128]{4,3,2,1,0:T(8,128)(2,1)S(1)}, u32[]{:S(2)}, u32[]{:S(2)}) collective-permute-start(bf16[10,3,3,64,128]{4,3,2,1,0:T(8,128)(2,1)S(1)} %get-tuple-element.32), channel_id=1, source_target_pairs={{0,1},{1,2},{2,3},{3,4},{4,5},{5,6},{6,7},{7,0},{8,9},{9,10},{10,1... | collective-permute-start | bytes 4423688 | tf_op jit(solution)/shard_map/ppermute | solution.py:555
  15.2 18.5 %collective-permute-start.6 = (bf16[10,3,3,64,128]{4,3,2,1,0:T(8,128)(2,1)S(1)}, bf16[10,3,3,64,128]{4,3,2,1,0:T(8,128)(2,1)S(1)}, u32[]{:S(2)}, u32[]{:S(2)}) collective-permute-start(bf16[10,3,3,64,128]{4,3,2,1,0:T(8,128)(2,1)S(1)} %get-tuple-element.33), channel_id=1, source_target_pairs={{1,0},{2,1},{3,2},{4,3},{5,4},{6,5},{7,6},{0,7},{9,8},{10,9},{11,1... | collective-permute-start | bytes 4423688 | tf_op jit(solution)/shard_map/ppermute | solution.py:556
  16.6 19.8 %collective-permute-start.7 = (bf16[3,3,3,64,128]{4,3,2,1,0:T(8,128)(2,1)S(1)}, bf16[3,3,3,64,128]{4,3,2,1,0:T(8,128)(2,1)S(1)}, u32[]{:S(2)}, u32[]{:S(2)}) collective-permute-start(bf16[3,3,3,64,128]{4,3,2,1,0:T(8,128)(2,1)S(1)} %get-tuple-element.38), channel_id=1, source_target_pairs={{0,8},{8,16},{16,24},{24,32},{32,40},{40,48},{48,56},{56,64},{64,7... | collective-permute-start | bytes 1327112 | tf_op jit(solution)/shard_map/ppermute | solution.py:551
  37.2 5.3 %collective-permute-start.8 = (f32[64,64]{1,0:T(8,128)S(1)}, f32[64,64]{1,0:T(8,128)S(1)}, u32[]{:S(2)}, u32[]{:S(2)}) collective-permute-start(f32[64,64]{1,0:T(8,128)S(1)} %get-tuple-element.39), channel_id=1, source_target_pairs={{0,1},{1,2},{2,3},{3,4},{4,5},{5,6},{6,7},{7,0},{8,9},{9,10},{10,1... | collective-permute-start | bytes 49160 | tf_op jit(solution)/shard_map/ppermute | solution.py:595

commit v8 on v7

--- a/solution.py
+++ b/solution.py
@@ -89,13 +89,14 @@
     return total[:64] + total[64:]
 
 
-def pack_kernel(m_hbm, main_ref, corner_ref, south_ref, north_ref, sems):
+def pack_kernel(m_hbm, flat_hbm, main_ref, corner_ref, south_ref, north_ref, sems):
     ext = m_hbm.shape[0]
     here = jnp.where(is_odd(), ext - 3, 0)
     there = jnp.where(is_odd(), 0, ext - 3)
     copies = [
-        pltpu.make_async_copy(m_hbm.at[here + i], main_ref.at[pl.ds(i * ext, ext)], sems.at[4 + i])
-        for i in range(3)
+        pltpu.make_async_copy(
+            flat_hbm.at[pl.ds(here * ext, 3 * ext)], main_ref.at[pl.ds(0, 3 * ext)], sems.at[0]
+        )
     ]
     main_ref[3 * ext] = jnp.zeros(main_ref.shape[1:], BF16)
     copies += [
@@ -534,12 +535,12 @@
             shape(ext, 3, 3, 64, 128, dtype=BF16),
             shape(ext, 3, 3, 64, 128, dtype=BF16),
         ],
-        [vmem_spec()],
+        [vmem_spec()] * 2,
         [vmem_spec()] * 4,
-        [pltpu.SemaphoreType.DMA((7,))],
+        [pltpu.SemaphoreType.DMA((4,))],
         8,
         "pack",
-    )(m)
+    )(m, m.reshape(ext * ext, 3, 64, 128))
     main, corner, south, north, mid = gate((main, corner, south, north, mid), ())
     main_pairs, other_pairs = [], []
     for y in range(ny):

time: 70.5 us -> 70.6 us (level)
    unnamed x12 -> x10, local copies, waits for them, and re-layouts: 2.41 us -> 2.49 us
  transfers between devices with their start and end apart: 9 -> 9, of which waited for: 2 -> 2; matrix products, arithmetic and copies ran while one was open for 0% -> 0% of each run, Pallas kernels for 25% -> 24%
where the time goes in v8:
time: 70.6 us; the launch traced here: 70.3 us
  Pallas kernels  22.8 us (32%)
  blocking collectives  22.2 us (31%)
  starting transfers between devices  16.4 us (23%)
  waiting for transfers between devices  5.36 us (8%)
  local copies, waits for them, and re-layouts  2.51 us (4%)
  other arithmetic  0.8 us (1%)
    all_to_all x1, blocking collectives, local(): code = lax.all_to_all(code, 'sx', 0, 0)  22.2 us
    pallas_call x1, Pallas kernels, local(): call(own_kernel, [shape(64, 64), shape(frame, 6, frame, 128), shape(frame...  12.6 us
    ppermute x1, starting transfers between devices, coef_columns(): high = lax.ppermute(own[:2], 'sx', down)  4.82 us
    ppermute x1, waiting for transfers between devices, local(): south = lax.ppermute(south, 'sy', up)  4.48 us
    pallas_call x1, Pallas kernels, local(): call(final_kernel, shape(nx, 64, 576), [vmem_spec()], any_spec(), [pltpu....  4.33 us
    ppermute x1, starting transfers between devices, local(): main = lax.ppermute(main, ('sx', 'sy'), main_pairs)  3.98 us
    ppermute x1, starting transfers between devices, local(): below = lax.ppermute(turned, 'sy', up)  3.82 us
    pallas_call x1, Pallas kernels, local(): call(rows_kernel, [shape(64, 128), shape(2, 2, 27, 128, 128, dtype=BF16)]...  2.79 us
  transfers between devices with their start and end apart: 9, of which 2 were waited for; matrix products, arithmetic and copies ran while one was open for 0% of the time, Pallas kernels for 24%

profile of v8, /device:TPU:24, one launch (start us, length us, event | category | flops | bytes accessed | tf_op | source)
XLA Modules:
  0.0 70.3 jit_solution(4141368690397486678)
XLA Ops:
  0.0 0.8 %pad_maximum_fusion.3 = (f32[2,3,8,128]{3,2,1,0:T(8,128)S(1)}, f32[2,3,8,128]{3,2,1,0:T(8,128)S(1)}) fusion(f32[8,1,8,128]{3,2,1,0:T(8,128)} %bitcast.12, f32[8,1,8,128]{3,2,1,0:T(8,128)} %bitcast.14, f32[8,1,8,128]{3,2,1,0:T(8,128)} %bitcast.16), kind=kLoop, calls=%fused_computation.3 | loop fusion | flops 24576 | bytes 147456 | tf_op jit(solution)/shard_map/slice | solution.py:510
  0.8 1.5 %collective-permute-start = (f32[2,3,8,128]{3,2,1,0:T(8,128)S(1)}, f32[2,3,8,128]{3,2,1,0:T(8,128)S(1)}, u32[]{:S(2)}, u32[]{:S(2)}) collective-permute-start(f32[2,3,8,128]{3,2,1,0:T(8,128)S(1)} %get-tuple-element.43), channel_id=1, source_target_pairs={{0,8},{8,16},{16,24},{24,32},{32,40},{40,48},{48,56},{56,64},{64,7... | collective-permute-start | bytes 73736 | tf_op jit(solution)/shard_map/ppermute | solution.py:510
  2.3 4.8 %collective-permute-start.1 = (f32[2,3,8,128]{3,2,1,0:T(8,128)S(1)}, f32[2,3,8,128]{3,2,1,0:T(8,128)S(1)}, u32[]{:S(2)}, u32[]{:S(2)}) collective-permute-start(f32[2,3,8,128]{3,2,1,0:T(8,128)S(1)} %get-tuple-element.44), channel_id=1, source_target_pairs={{8,0},{16,8},{24,16},{32,24},{40,32},{48,40},{56,48},{64,56},{72,6... | collective-permute-start | bytes 73736 | tf_op jit(solution)/shard_map/ppermute | solution.py:511
  7.1 0.0 copy-start
  7.1 2.4 %copy-done = bf16[10,10,64,3,128]{4,2,3,1,0:T(8,128)(2,1)S(1)} copy-done((bf16[10,10,64,3,128]{4,2,3,1,0:T(8,128)(2,1)S(1)}, bf16[10,10,64,3,128]{4,2,3,1,0:T(8,128)(2,1)}, u32[]{:S(2)}) %copy-start) | copy-done | bytes 4915224
  9.5 0.0 copy-start.2
  9.5 0.0 copy-start.3
  9.5 0.0 copy-start.4
  9.5 0.7 pack.1
  10.2 0.0 collective-permute-done
  10.2 0.0 collective-permute-done.1
  10.2 0.1 copy-done.2
  10.3 0.0 copy-done.3
  10.3 0.0 copy-done.4
  10.3 0.0 copy-start.1
  10.4 0.0 collective-permute-start.4
  10.4 0.5 collective-permute-start.3
  10.9 4.0 %collective-permute-start.2 = (bf16[31,3,64,128]{3,2,1,0:T(8,128)(2,1)S(1)}, bf16[31,3,64,128]{3,2,1,0:T(8,128)(2,1)S(1)}, u32[]{:S(2)}, u32[]{:S(2)}) collective-permute-start(bf16[31,3,64,128]{3,2,1,0:T(8,128)(2,1)S(1)} %get-tuple-element.27), channel_id=1, source_target_pairs={{8,0},{16,8},{24,16},{32,24},{40,32},{48,40},{56,48},{64,56},{72,6... | collective-permute-start | bytes 4571144 | tf_op jit(solution)/shard_map/ppermute | solution.py:551
  14.9 0.0 collective-permute-done.4.hi_ref.refs_3_
  14.9 0.0 collective-permute-done.3.lo_ref.refs_2_
  14.9 0.0 collective-permute-start.5
  14.9 1.7 %collective-permute-start.6 = (bf16[10,3,3,64,128]{4,3,2,1,0:T(8,128)(2,1)S(1)}, bf16[10,3,3,64,128]{4,3,2,1,0:T(8,128)(2,1)S(1)}, u32[]{:S(2)}, u32[]{:S(2)}) collective-permute-start(bf16[10,3,3,64,128]{4,3,2,1,0:T(8,128)(2,1)S(1)} %get-tuple-element.33), channel_id=1, source_target_pairs={{1,0},{2,1},{3,2},{4,3},{5,4},{6,5},{7,6},{0,7},{9,8},{10,9},{11,1... | collective-permute-start | bytes 4423688 | tf_op jit(solution)/shard_map/ppermute | solution.py:557
  16.6 0.0 collective-permute-start.7
  16.7 0.0 copy-done.1
  16.7 12.6 %own_gram.1 = (f32[64,64]{1,0:T(8,128)S(1)}, f32[12,6,12,128]{3,2,1,0:T(8,128)S(1)}, bf16[12,36,128,128]{3,2,1,0:T(8,128)(2,1)S(1)}) custom-call(bf16[10,30,64,128]{3,2,1,0:T(8,128)(2,1)S(1)} %bitcast.11, f32[12,3,8,128]{3,2,1,0:T(8,128)S(1)} %get-tuple-element.28.mid_ref, f32[12,3,2,128]{3,2,1,0:T(2,128)S(1)} %collective-permute-done.3.lo_ref.refs_2_, ...), custom_call_target="tpu_custom_call" | custom-call | flops 1000 | bytes 1000 | tf_op jit(solution)/shard_map/own_gram/pallas_call | solution.py:559
  29.2 4.5 %collective-permute-done.5.south_ref = bf16[10,3,3,64,128]{4,3,2,1,0:T(8,128)(2,1)S(1)} collective-permute-done((bf16[10,3,3,64,128]{4,3,2,1,0:T(8,128)(2,1)S(1)}, bf16[10,3,3,64,128]{4,3,2,1,0:T(8,128)(2,1)S(1)}, u32[]{:S(2)}, u32[]{:S(2)}) %collective-permute-start.5) | collective-permute-done | bytes 1474592 | tf_op jit(solution)/shard_map/ppermute | solution.py:556
  33.7 0.0 collective-permute-done.6.north_ref
  33.7 2.8 %row_gram.1 = (f32[64,128]{1,0:T(8,128)S(1)}, bf16[2,2,27,128,128]{4,3,2,1,0:T(8,128)(2,1)S(1)}) custom-call(bf16[10,3,3,64,128]{4,3,2,1,0:T(8,128)(2,1)S(1)} %collective-permute-done.5.south_ref, bf16[10,3,3,64,128]{4,3,2,1,0:T(8,128)(2,1)S(1)} %collective-permute-done.6.north_ref, bf16[12,36,128,128]{3,2,1,0:T(8,128)(2,1)S(1)} %get-tuple-element.29.img_ref, ...), custom_call_target="tpu_custom_call" | custom-call | flops 1000 | bytes 1000 | tf_op jit(solution)/shard_map/row_gram/pallas_call | solution.py:575
  36.5 0.0 collective-permute-done.7.corner_ref
  36.5 0.7 %corner_gram.1 = (f32[64,64]{1,0:T(8,128)S(1)}, f32[64,64]{1,0:T(8,128)S(1)}) custom-call(bf16[3,3,3,64,128]{4,3,2,1,0:T(8,128)(2,1)S(1)} %collective-permute-done.7.corner_ref, bf16[2,2,27,128,128]{4,3,2,1,0:T(8,128)(2,1)S(1)} %get-tuple-element.35.cimg_ref), custom_call_target="tpu_custom_call" | custom-call | flops 1000 | bytes 1000 | tf_op jit(solution)/shard_map/corner_gram/pallas_call | solution.py:587
  37.2 3.8 %collective-permute-start.8 = (f32[64,64]{1,0:T(8,128)S(1)}, f32[64,64]{1,0:T(8,128)S(1)}, u32[]{:S(2)}, u32[]{:S(2)}) collective-permute-start(f32[64,64]{1,0:T(8,128)S(1)} %get-tuple-element.39), channel_id=1, source_target_pairs={{0,1},{1,2},{2,3},{3,4},{4,5},{5,6},{6,7},{7,0},{8,9},{9,10},{10,1... | collective-permute-start | bytes 49160 | tf_op jit(solution)/shard_map/ppermute | solution.py:596
  41.0 0.0 collective-permute-done.2.main_ref
  41.0 0.9 %collective-permute-done.8.below_ref = f32[64,64]{1,0:T(8,128)S(1)} collective-permute-done((f32[64,64]{1,0:T(8,128)S(1)}, f32[64,64]{1,0:T(8,128)S(1)}, u32[]{:S(2)}, u32[]{:S(2)}) %collective-permute-start.8) | collective-permute-done | bytes 16416 | tf_op jit(solution)/shard_map/ppermute | solution.py:596
  41.9 1.8 %column_gram.1 = bf16[16,64,512]{2,1,0:T(8,128)(2,1)S(1)} custom-call(bf16[31,3,64,128]{3,2,1,0:T(8,128)(2,1)S(1)} %collective-permute-done.2.main_ref, bf16[12,36,128,128]{3,2,1,0:T(8,128)(2,1)S(1)} %get-tuple-element.29.img_ref, bf16[2,2,27,128,128]{4,3,2,1,0:T(8,128)(2,1)S(1)} %get-tuple-element.35.cimg_ref, f32[64,64]{1,0:T(8,128)S(1)} %get-tuple-element.36.own_ref, ...), custom_call_target="tpu_custom_call" | custom-call | flops 1000 | bytes 1000 | tf_op jit(solution)/shard_map/column_gram/pallas_call | solution.py:597
  43.7 22.2 %all_to_all.5.code_ref = bf16[16,64,512]{2,1,0:T(8,128)(2,1)S(1)} all-to-all(bf16[16,64,512]{2,1,0:T(8,128)(2,1)S(1)} %column_gram.1), channel_id=1, replica_groups=mesh['sx'=16,'sy'=8] {'sx'}, dimensions={0} | all-to-all | bytes 2097152 | tf_op jit(solution)/shard_map/all_to_all | solution.py:606
  65.9 4.3 %assemble.1 = f32[16,64,576]{2,1,0:T(8,128)} custom-call(bf16[16,64,512]{2,1,0:T(8,128)(2,1)S(1)} %all_to_all.5.code_ref), custom_call_target="tpu_custom_call" | custom-call | flops 1000 | bytes 1000 | tf_op jit(solution)/shard_map/assemble/pallas_call | solution.py:607
  (4 shorter events, 0.0 us)
Async XLA Ops:
  0.8 9.4 %collective-permute-start = (f32[2,3,8,128]{3,2,1,0:T(8,128)S(1)}, f32[2,3,8,128]{3,2,1,0:T(8,128)S(1)}, u32[]{:S(2)}, u32[]{:S(2)}) collective-permute-start(f32[2,3,8,128]{3,2,1,0:T(8,128)S(1)} %get-tuple-element.43), channel_id=1, source_target_pairs={{0,8},{8,16},{16,24},{24,32},{32,40},{40,48},{48,56},{56,64},{64,7... | collective-permute-start | bytes 73736 | tf_op jit(solution)/shard_map/ppermute | solution.py:510
  2.3 7.9 %collective-permute-start.1 = (f32[2,3,8,128]{3,2,1,0:T(8,128)S(1)}, f32[2,3,8,128]{3,2,1,0:T(8,128)S(1)}, u32[]{:S(2)}, u32[]{:S(2)}) collective-permute-start(f32[2,3,8,128]{3,2,1,0:T(8,128)S(1)} %get-tuple-element.44), channel_id=1, source_target_pairs={{8,0},{16,8},{24,16},{32,24},{40,32},{48,40},{56,48},{64,56},{72,6... | collective-permute-start | bytes 73736 | tf_op jit(solution)/shard_map/ppermute | solution.py:511
  7.1 2.4 %copy-start = (bf16[10,10,64,3,128]{4,2,3,1,0:T(8,128)(2,1)S(1)}, bf16[10,10,64,3,128]{4,2,3,1,0:T(8,128)(2,1)}, u32[]{:S(2)}) copy-start(bf16[10,10,64,3,128]{4,2,3,1,0:T(8,128)(2,1)} %param.4) | copy-start | bytes 14745604
  9.5 0.8 %copy-start.2 = (f32[8,8,128]{2,1,0:T(8,128)S(1)}, f32[8,8,128]{2,1,0:T(8,128)}, u32[]{:S(2)}) copy-start(f32[8,8,128]{2,1,0:T(8,128)} %param.7) | copy-start | bytes 98308
  9.5 0.8 %copy-start.3 = (f32[8,8,128]{2,1,0:T(8,128)S(1)}, f32[8,8,128]{2,1,0:T(8,128)}, u32[]{:S(2)}) copy-start(f32[8,8,128]{2,1,0:T(8,128)} %param.6) | copy-start | bytes 98308
  9.5 0.8 %copy-start.4 = (f32[8,8,128]{2,1,0:T(8,128)S(1)}, f32[8,8,128]{2,1,0:T(8,128)}, u32[]{:S(2)}) copy-start(f32[8,8,128]{2,1,0:T(8,128)} %param.5) | copy-start | bytes 98308
  10.3 6.3 %copy-start.1 = (bf16[10,10,64,3,128]{4,2,3,1,0:T(8,128)(2,1)S(1)}, bf16[10,10,64,3,128]{4,2,3,1,0:T(8,128)(2,1)}, u32[]{:S(2)}) copy-start(bf16[10,10,64,3,128]{4,2,3,1,0:T(8,128)(2,1)} %param.4) | copy-start | bytes 14745604
  10.4 4.5 %collective-permute-start.4 = (f32[12,3,2,128]{3,2,1,0:T(2,128)S(1)}, f32[12,3,2,128]{3,2,1,0:T(2,128)S(1)}, u32[]{:S(2)}, u32[]{:S(2)}) collective-permute-start(f32[12,3,2,128]{3,2,1,0:T(2,128)S(1)} %get-tuple-element.41), channel_id=1, source_target_pairs={{1,0},{2,1},{3,2},{4,3},{5,4},{6,5},{7,6},{0,7},{9,8},{10,9},{11,1... | collective-permute-start | bytes 110600 | tf_op jit(solution)/shard_map/ppermute | solution.py:518
  10.4 4.5 %collective-permute-start.3 = (f32[12,3,2,128]{3,2,1,0:T(2,128)S(1)}, f32[12,3,2,128]{3,2,1,0:T(2,128)S(1)}, u32[]{:S(2)}, u32[]{:S(2)}) collective-permute-start(f32[12,3,2,128]{3,2,1,0:T(2,128)S(1)} %get-tuple-element.42), channel_id=1, source_target_pairs={{0,1},{1,2},{2,3},{3,4},{4,5},{5,6},{6,7},{7,0},{8,9},{9,10},{10,1... | collective-permute-start | bytes 110600 | tf_op jit(solution)/shard_map/ppermute | solution.py:517
  10.9 30.1 %collective-permute-start.2 = (bf16[31,3,64,128]{3,2,1,0:T(8,128)(2,1)S(1)}, bf16[31,3,64,128]{3,2,1,0:T(8,128)(2,1)S(1)}, u32[]{:S(2)}, u32[]{:S(2)}) collective-permute-start(bf16[31,3,64,128]{3,2,1,0:T(8,128)(2,1)S(1)} %get-tuple-element.27), channel_id=1, source_target_pairs={{8,0},{16,8},{24,16},{32,24},{40,32},{48,40},{56,48},{64,56},{72,6... | collective-permute-start | bytes 4571144 | tf_op jit(solution)/shard_map/ppermute | solution.py:551
  14.9 18.8 %collective-permute-start.5 = (bf16[10,3,3,64,128]{4,3,2,1,0:T(8,128)(2,1)S(1)}, bf16[10,3,3,64,128]{4,3,2,1,0:T(8,128)(2,1)S(1)}, u32[]{:S(2)}, u32[]{:S(2)}) collective-permute-start(bf16[10,3,3,64,128]{4,3,2,1,0:T(8,128)(2,1)S(1)} %get-tuple-element.32), channel_id=1, source_target_pairs={{0,1},{1,2},{2,3},{3,4},{4,5},{5,6},{6,7},{7,0},{8,9},{9,10},{10,1... | collective-permute-start | bytes 4423688 | tf_op jit(solution)/shard_map/ppermute | solution.py:556
  14.9 18.8 %collective-permute-start.6 = (bf16[10,3,3,64,128]{4,3,2,1,0:T(8,128)(2,1)S(1)}, bf16[10,3,3,64,128]{4,3,2,1,0:T(8,128)(2,1)S(1)}, u32[]{:S(2)}, u32[]{:S(2)}) collective-permute-start(bf16[10,3,3,64,128]{4,3,2,1,0:T(8,128)(2,1)S(1)} %get-tuple-element.33), channel_id=1, source_target_pairs={{1,0},{2,1},{3,2},{4,3},{5,4},{6,5},{7,6},{0,7},{9,8},{10,9},{11,1... | collective-permute-start | bytes 4423688 | tf_op jit(solution)/shard_map/ppermute | solution.py:557
  16.6 19.8 %collective-permute-start.7 = (bf16[3,3,3,64,128]{4,3,2,1,0:T(8,128)(2,1)S(1)}, bf16[3,3,3,64,128]{4,3,2,1,0:T(8,128)(2,1)S(1)}, u32[]{:S(2)}, u32[]{:S(2)}) collective-permute-start(bf16[3,3,3,64,128]{4,3,2,1,0:T(8,128)(2,1)S(1)} %get-tuple-element.38), channel_id=1, source_target_pairs={{0,8},{8,16},{16,24},{24,32},{32,40},{40,48},{48,56},{56,64},{64,7... | collective-permute-start | bytes 1327112 | tf_op jit(solution)/shard_map/ppermute | solution.py:552
  37.2 4.7 %collective-permute-start.8 = (f32[64,64]{1,0:T(8,128)S(1)}, f32[64,64]{1,0:T(8,128)S(1)}, u32[]{:S(2)}, u32[]{:S(2)}) collective-permute-start(f32[64,64]{1,0:T(8,128)S(1)} %get-tuple-element.39), channel_id=1, source_target_pairs={{0,1},{1,2},{2,3},{3,4},{4,5},{5,6},{6,7},{7,0},{8,9},{9,10},{10,1... | collective-permute-start | bytes 49160 | tf_op jit(solution)/shard_map/ppermute | solution.py:596
